TPU v7x, 32 devices: a whole 2x2x4 slice. The times are simulated.
32 devices in a mesh: dp: 4 (over x, core), fsdp: 8 (over z, y).
Axes of the slice: x: 2, y: 2, z: 4, core: 2. Of those that a mesh axis runs over, the one named last changes fastest.
Arguments:
- tokens: bfloat16 [32768, 768], P(('dp', 'fsdp')), may hold values from -6 to 6
- document_numbers: int32 [64, 512], P(('dp', 'fsdp')), may hold values from 0 to 3, never falling along the last dimension, each value on 1 to 256 neighbouring positions
- query_weight: bfloat16 [768, 768], P(('dp', 'fsdp')), may hold values from -0.21875 to 0.21875
- key_weight: bfloat16 [768, 768], P(('dp', 'fsdp')), may hold values from -0.21875 to 0.21875
- value_weight: bfloat16 [768, 768], P(('dp', 'fsdp')), may hold values from -0.21875 to 0.21875
- output_weight: bfloat16 [768, 768], P(('dp', 'fsdp')), may hold values from -2.5 to 2.5
- inner_weight: bfloat16 [768, 3072], P(('dp', 'fsdp')), may hold values from -0.21875 to 0.21875
- outer_weight: bfloat16 [3072, 768], P(('dp', 'fsdp')), may hold values from -0.109375 to 0.109375
- fixed_projection_bias: bfloat16 [4, 768], P(None, ('dp', 'fsdp')), may hold values from -3 to 3
- feedforward_inner_bias: bfloat16 [3072], P(('dp', 'fsdp')), may hold values from -3 to 3
- layer_norm_gain: bfloat16 [2, 768], P(None, ('dp', 'fsdp')), may hold values from 0.5 to 1.5
- layer_norm_shift: bfloat16 [2, 768], P(None, ('dp', 'fsdp')), may hold values from -2 to 2
- adapter_down_factors: float32 [2, 768, 8], replicated, may hold values from -0.21875 to 0.21875
- adapter_up_factors: float32 [2, 8, 768], replicated, may hold values from -0.6 to 0.6
- down_first_moment: float32 [2, 768, 8], replicated, may hold values from -3 to 3
- down_second_moment: float32 [2, 768, 8], replicated, may hold values from 0.05 to 2
- up_first_moment: float32 [2, 8, 768], replicated, may hold values from -3 to 3
- up_second_moment: float32 [2, 8, 768], replicated, may hold values from 0.005 to 0.2
- rate: float32 [1], replicated, may hold values from 0.001 to 0.01
- step: int32 [1], replicated, may hold values from 10 to 999
- cotangent: bfloat16 [32768, 768], P(('dp', 'fsdp')), may hold values from -6 to 6
Outputs:
- activations: bfloat16 [32768, 768], P(('dp', 'fsdp'))
- input_grad: float32 [32768, 768], P(('dp', 'fsdp'))
- down_gradient: float32 [2, 768, 8], replicated
- up_gradient: float32 [2, 8, 768], replicated
- gain_grad: float32 [2, 768], replicated
- shift_grad: float32 [2, 768], replicated
- updated_down_factors: float32 [2, 768, 8], replicated
- updated_up_factors: float32 [2, 8, 768], replicated
- updated_down_first_moment: float32 [2, 768, 8], replicated
- updated_down_second_moment: float32 [2, 768, 8], replicated
- updated_up_first_moment: float32 [2, 8, 768], replicated
- updated_up_second_moment: float32 [2, 8, 768], replicated
Inputs may be any that keep to these rules, and one draw needn't show every extreme that they name: `document_numbers`: within a row of 512 positions the numbers never fall.
All inputs are finite; a program needn't handle non-finite values.
Results may differ from a plain program's by a relative error of at most 0.015.
The roundings to bfloat16 on the way count: a program that leaves them out, or rounds other values in their place, can miss the bound.
Values may be sent and summed in bfloat16 or wider, within the bound.
No kernel may reach another device: no remote copies, remote signals or barrier semaphores. Data moves between devices by JAX's collectives and lax.ppermute only.
A program may use at most 128 MiB of HBM per device.

v0:
```python
import math

import jax
import jax.numpy as jnp
from jax import lax
from jax.sharding import PartitionSpec as P

HEAD = 64


beta_one = 0.9
beta_two = 0.999
adam_epsilon = 1e-08
down_decay_factor = 0.05
up_decay_factor = 0.01
norm_epsilon = 1e-05
masked_score = -1e30
root_half = 1.0 / math.sqrt(2.0)
root_circle = 1.0 / math.sqrt(2.0 * math.pi)


def layer_stats(value):
    centred = value - jnp.mean(value, axis=-1, keepdims=True)
    inverse = lax.rsqrt(jnp.mean(centred * centred, axis=-1, keepdims=True) + norm_epsilon)
    return (centred * inverse, inverse)


def norm_back(grad, normed, inverse, gain):
    scaled = grad * gain
    return inverse * (
        scaled
        - jnp.mean(scaled, axis=-1, keepdims=True)
        - normed * jnp.mean(scaled * normed, axis=-1, keepdims=True)
    )


def split_heads(value):
    return value.reshape(value.shape[0], -1, HEAD)


def pack_scores(query, key_rows, segment):
    scores = jnp.einsum(
        "qhd,khd->hqk",
        split_heads(query),
        split_heads(key_rows),
        preferred_element_type=jnp.float32,
    ) * HEAD ** (-0.5)
    same = segment[:, None] == segment[None, :]
    return jnp.where(same[None, :, :], scores, masked_score)


def attend_forward(query, key_rows, value_rows, segment):
    scores = pack_scores(query, key_rows, segment)
    peak = jnp.max(scores, axis=-1, keepdims=True)
    exponent = jnp.exp(scores - peak)
    total = jnp.sum(exponent, axis=-1, keepdims=True)
    weights = (exponent / total).astype(jnp.bfloat16)
    context = jnp.einsum(
        "hqk,khd->qhd", weights, split_heads(value_rows), preferred_element_type=jnp.float32
    )
    return (context.reshape(query.shape).astype(jnp.bfloat16), peak + jnp.log(total))


def attend_backward(query, key_rows, value_rows, segment, summit, grad_context):
    scores = pack_scores(query, key_rows, segment)
    weights = jnp.exp(scores - summit)
    grad_heads = split_heads(grad_context)
    grad_weights = jnp.einsum(
        "qhd,khd->hqk", grad_heads, split_heads(value_rows), preferred_element_type=jnp.float32
    )
    delta = jnp.sum(weights * grad_weights, axis=-1, keepdims=True)
    grad_scores = (weights * (grad_weights - delta)).astype(jnp.bfloat16)
    grad_query = jnp.einsum(
        "hqk,khd->qhd", grad_scores, split_heads(key_rows), preferred_element_type=jnp.float32
    ) * HEAD ** (-0.5)
    grad_keys = jnp.einsum(
        "hqk,qhd->khd", grad_scores, split_heads(query), preferred_element_type=jnp.float32
    ) * HEAD ** (-0.5)
    grad_values = jnp.einsum(
        "hqk,qhd->khd", weights.astype(jnp.bfloat16), grad_heads, preferred_element_type=jnp.float32
    )
    array_shape = query.shape
    return (
        grad_query.reshape(array_shape).astype(jnp.bfloat16),
        grad_keys.reshape(array_shape).astype(jnp.bfloat16),
        grad_values.reshape(array_shape).astype(jnp.bfloat16),
    )


def adamw_update(param, grad, first, second, learning_step_rate, decay, step_counter):
    first_new = beta_one * first + (1.0 - beta_one) * grad
    second_new = beta_two * second + (1.0 - beta_two) * grad * grad
    first_hat = first_new / (1.0 - beta_one**step_counter)
    second_hat = second_new / (1.0 - beta_two**step_counter)
    param_new = param - learning_step_rate * (
        first_hat / (jnp.sqrt(second_hat) + adam_epsilon) + decay * param
    )
    return (param_new, first_new, second_new)


def per_device(
    tokens,
    document_numbers,
    query_weight,
    key_weight,
    value_weight,
    output_weight,
    inner_weight,
    outer_weight,
    fixed_projection_bias,
    feedforward_inner_bias,
    layer_norm_gain,
    layer_norm_shift,
    adapter_down_factors,
    adapter_up_factors,
    down_first_moment,
    down_second_moment,
    up_first_moment,
    up_second_moment,
    rate,
    step,
    cotangent,
):
    rows = tokens.shape[0]
    width = tokens.shape[1]
    packs = document_numbers.shape[0]
    adapter_rank = adapter_down_factors.shape[2]
    query_full, key_full, value_full, output_full, bias_full = (
        lax.all_gather(query_weight, ("dp", "fsdp"), axis=0, tiled=True),
        lax.all_gather(key_weight, ("dp", "fsdp"), axis=0, tiled=True),
        lax.all_gather(value_weight, ("dp", "fsdp"), axis=0, tiled=True),
        lax.all_gather(output_weight, ("dp", "fsdp"), axis=0, tiled=True),
        lax.all_gather(fixed_projection_bias, ("dp", "fsdp"), axis=1, tiled=True),
    )
    inner_full, outer_full, inner_bias_full, gain_full, shift_full = (
        lax.all_gather(inner_weight, ("dp", "fsdp"), axis=0, tiled=True),
        lax.all_gather(outer_weight, ("dp", "fsdp"), axis=0, tiled=True),
        lax.all_gather(feedforward_inner_bias, ("dp", "fsdp"), axis=0, tiled=True),
        lax.all_gather(layer_norm_gain, ("dp", "fsdp"), axis=1, tiled=True),
        lax.all_gather(layer_norm_shift, ("dp", "fsdp"), axis=1, tiled=True),
    )
    bias_rows = bias_full.astype(jnp.float32)
    gain_rows = gain_full.astype(jnp.float32)
    shift_rows = shift_full.astype(jnp.float32)
    down_adapter_factor = adapter_down_factors.astype(jnp.bfloat16)
    up_adapter_factor = adapter_up_factors.astype(jnp.bfloat16)
    joined = jnp.concatenate([down_adapter_factor[0], down_adapter_factor[1]], axis=1)
    reduced = jnp.dot(tokens, joined, preferred_element_type=jnp.float32).astype(jnp.bfloat16)
    query = (
        jnp.dot(tokens, query_full, preferred_element_type=jnp.float32)
        + bias_rows[0]
        + 2.0
        * jnp.dot(
            reduced[:, :adapter_rank], up_adapter_factor[0], preferred_element_type=jnp.float32
        )
    ).astype(jnp.bfloat16)
    key_rows = jnp.dot(tokens, key_full, preferred_element_type=jnp.float32).astype(jnp.bfloat16)
    value_rows = (
        jnp.dot(tokens, value_full, preferred_element_type=jnp.float32)
        + bias_rows[1]
        + 2.0
        * jnp.dot(
            reduced[:, adapter_rank:], up_adapter_factor[1], preferred_element_type=jnp.float32
        )
    ).astype(jnp.bfloat16)

    def by_pack(value):
        return value.reshape(packs, rows // packs, width)

    context, summit = lax.map(
        lambda items: attend_forward(*items),
        (by_pack(query), by_pack(key_rows), by_pack(value_rows), document_numbers),
    )
    context = context.reshape(rows, width)
    attended = jnp.dot(context, output_full, preferred_element_type=jnp.float32) + bias_rows[2]
    normed_one, inverse_one = layer_stats(tokens.astype(jnp.float32) + attended)
    first = normed_one * gain_rows[0] + shift_rows[0]
    inner = jnp.dot(
        first.astype(jnp.bfloat16), inner_full, preferred_element_type=jnp.float32
    ) + inner_bias_full.astype(jnp.float32)
    activated = jax.nn.gelu(inner, approximate=False).astype(jnp.bfloat16)
    outer = jnp.dot(activated, outer_full, preferred_element_type=jnp.float32) + bias_rows[3]
    normed_two, inverse_two = layer_stats(first + outer)
    activations = (normed_two * gain_rows[1] + shift_rows[1]).astype(jnp.bfloat16)
    inner_full, outer_full, gain_full = (
        lax.all_gather(inner_weight, ("dp", "fsdp"), axis=0, tiled=True),
        lax.all_gather(outer_weight, ("dp", "fsdp"), axis=0, tiled=True),
        lax.all_gather(layer_norm_gain, ("dp", "fsdp"), axis=1, tiled=True),
    )
    gain_rows = gain_full.astype(jnp.float32)
    grad_out = cotangent.astype(jnp.float32)
    grad_gain_two = jnp.sum(grad_out * normed_two, axis=0)
    grad_shift_two = jnp.sum(grad_out, axis=0)
    grad_res = norm_back(grad_out, normed_two, inverse_two, gain_rows[1])
    grad_outer = grad_res.astype(jnp.bfloat16)
    grad_active = jnp.dot(grad_outer, outer_full.T, preferred_element_type=jnp.float32)
    cumulative = 0.5 * (1.0 + lax.erf(inner * root_half))
    density = jnp.exp(-0.5 * inner * inner) * root_circle
    grad_inner = (grad_active * (cumulative + inner * density)).astype(jnp.bfloat16)
    grad_first = grad_res + jnp.dot(grad_inner, inner_full.T, preferred_element_type=jnp.float32)
    grad_gain_one = jnp.sum(grad_first * normed_one, axis=0)
    grad_shift_one = jnp.sum(grad_first, axis=0)
    grad_mid = norm_back(grad_first, normed_one, inverse_one, gain_rows[0])
    grad_attended = grad_mid.astype(jnp.bfloat16)
    query_full, key_full, value_full, output_full = (
        lax.all_gather(query_weight, ("dp", "fsdp"), axis=0, tiled=True),
        lax.all_gather(key_weight, ("dp", "fsdp"), axis=0, tiled=True),
        lax.all_gather(value_weight, ("dp", "fsdp"), axis=0, tiled=True),
        lax.all_gather(output_weight, ("dp", "fsdp"), axis=0, tiled=True),
    )
    grad_context = jnp.dot(grad_attended, output_full.T, preferred_element_type=jnp.float32).astype(
        jnp.bfloat16
    )
    grad_query, grad_keys, grad_values = lax.map(
        lambda items: attend_backward(*items),
        (
            by_pack(query),
            by_pack(key_rows),
            by_pack(value_rows),
            document_numbers,
            summit,
            by_pack(grad_context),
        ),
    )
    grad_query = grad_query.reshape(rows, width)
    grad_keys = grad_keys.reshape(rows, width)
    grad_values = grad_values.reshape(rows, width)
    grad_reduced = jnp.concatenate(
        [
            2.0 * jnp.dot(grad_query, up_adapter_factor[0].T, preferred_element_type=jnp.float32),
            2.0 * jnp.dot(grad_values, up_adapter_factor[1].T, preferred_element_type=jnp.float32),
        ],
        axis=1,
    ).astype(jnp.bfloat16)
    input_grad = (
        grad_mid
        + jnp.dot(grad_query, query_full.T, preferred_element_type=jnp.float32)
        + jnp.dot(grad_keys, key_full.T, preferred_element_type=jnp.float32)
        + jnp.dot(grad_values, value_full.T, preferred_element_type=jnp.float32)
        + jnp.dot(grad_reduced, joined.T, preferred_element_type=jnp.float32)
    )
    local_joined = jnp.dot(tokens.T, grad_reduced, preferred_element_type=jnp.float32)
    local_down = jnp.stack([local_joined[:, :adapter_rank], local_joined[:, adapter_rank:]])
    local_up = jnp.stack(
        [
            2.0
            * jnp.dot(reduced[:, :adapter_rank].T, grad_query, preferred_element_type=jnp.float32),
            2.0
            * jnp.dot(reduced[:, adapter_rank:].T, grad_values, preferred_element_type=jnp.float32),
        ]
    )
    local_gain = jnp.stack([grad_gain_one, grad_gain_two])
    local_shift = jnp.stack([grad_shift_one, grad_shift_two])
    count = lax.axis_size(("dp", "fsdp"))
    step_counter = step[0].astype(jnp.float32)
    learning_step_rate = rate[0]
    total_down, total_up, total_gain, total_shift = lax.psum(
        (local_down, local_up, local_gain, local_shift), ("dp", "fsdp")
    )
    down_gradient = total_down / count
    up_gradient = total_up / count
    gain_grad = total_gain / count
    shift_grad = total_shift / count
    updated_down_factors, updated_down_first_moment, updated_down_second_moment = adamw_update(
        adapter_down_factors,
        down_gradient,
        down_first_moment,
        down_second_moment,
        learning_step_rate,
        down_decay_factor,
        step_counter,
    )
    updated_up_factors, updated_up_first_moment, updated_up_second_moment = adamw_update(
        adapter_up_factors,
        up_gradient,
        up_first_moment,
        up_second_moment,
        16.0 * learning_step_rate,
        up_decay_factor,
        step_counter,
    )
    return (
        activations,
        input_grad,
        down_gradient,
        up_gradient,
        gain_grad,
        shift_grad,
        updated_down_factors,
        updated_up_factors,
        updated_down_first_moment,
        updated_down_second_moment,
        updated_up_first_moment,
        updated_up_second_moment,
    )


def solution(mesh):
    in_specs = (
        P(("dp", "fsdp"), None),
        P(("dp", "fsdp"), None),
        P(("dp", "fsdp"), None),
        P(("dp", "fsdp"), None),
        P(("dp", "fsdp"), None),
        P(("dp", "fsdp"), None),
        P(("dp", "fsdp"), None),
        P(("dp", "fsdp"), None),
        P(None, ("dp", "fsdp")),
        P(("dp", "fsdp")),
        P(None, ("dp", "fsdp")),
        P(None, ("dp", "fsdp")),
        P(),
        P(),
        P(),
        P(),
        P(),
        P(),
        P(),
        P(),
        P(("dp", "fsdp"), None),
    )
    out_specs = (
        P(("dp", "fsdp"), None),
        P(("dp", "fsdp"), None),
        P(),
        P(),
        P(),
        P(),
        P(),
        P(),
        P(),
        P(),
        P(),
        P(),
    )
    return jax.shard_map(
        per_device, mesh=mesh, in_specs=in_specs, out_specs=out_specs, check_vma=False
    )
```

profile of v0, /device:TPU:0, one launch (start us, length us, event | category | flops | bytes accessed | tf_op | source)
XLA Modules:
  0.0 689.1 jit_solution(17591959528198819408)
XLA Ops:
  12.1 70.0 %all-gather = bf16[32,24,4]{1,2,0:T(4,128)(2,1)S(1)} all-gather(bf16[1,24,4]{1,2,0:T(4,128)(2,1)} %bitcast.209), channel_id=1, replica_groups=mesh['dp'=4,'fsdp'=8] {'dp','fsdp'}, dimensions={0}, use_global_device_ids=true | all-gather | bytes 6336 | tf_op jit(solution)/shard_map/all_gather | solution.py:133
  83.8 2.7 copy.111
  86.5 63.0 %all-gather.1 = bf16[32,24,2]{1,2,0:T(2,128)(2,1)S(1)} all-gather(bf16[1,24,2]{1,2,0:T(2,128)(2,1)S(1)} %bitcast.210), channel_id=1, replica_groups=mesh['dp'=4,'fsdp'=8] {'dp','fsdp'}, dimensions={0}, use_global_device_ids=true | all-gather | bytes 3168 | tf_op jit(solution)/shard_map/all_gather | solution.py:139
  150.4 65.2 %all-gather.2 = bf16[32,24,2]{1,2,0:T(2,128)(2,1)S(1)} all-gather(bf16[1,24,2]{1,2,0:T(2,128)(2,1)S(1)} %bitcast.211), channel_id=1, replica_groups=mesh['dp'=4,'fsdp'=8] {'dp','fsdp'}, dimensions={0}, use_global_device_ids=true | all-gather | bytes 3168 | tf_op jit(solution)/shard_map/all_gather | solution.py:140
  216.6 37.0 %all-reduce = bf16[3072]{0:T(1024)(128)(2,1)S(1)} all-reduce(bf16[3072]{0:T(1024)(128)(2,1)S(1)} %dynamic-update-slice), channel_id=1, replica_groups=mesh['dp'=4,'fsdp'=8] {'dp','fsdp'}, use_global_device_ids=true, to_apply=%add | all-reduce | flops 3072 | bytes 12288
  257.8 2.7 fusion.97
  262.8 2.7 fusion.98
  265.5 1.8 add_convert_fusion.1
  269.0 3.8 convolution_convert_fusion.1
  272.8 2.6 copy.116
  276.8 26.3 %while.26 = (s32[]{:T(128)}, bf16[2,512,768]{2,1,0:T(8,128)(2,1)}, f32[2,12,512,1]{2,1,3,0:T(8,128)S(1)}, bf16[2,512,768]{1,2,0:T(8,128)(2,1)}, s32[2,512]{1,0:T...) while((s32[]{:T(128)}, bf16[2,512,768]{2,1,0:T(8,128)(2,1)}, ...), condition=%wide.region_3.4_spmd, body=%wide.region_0.3_spmd.sunk | while | flops 843704320 | bytes 50035300 | solution.py:170
  279.3 2.1 fusion.169
  281.4 2.6 fusion.170
  285.2 3.6 fusion.171
  292.2 2.1 fusion.169
  294.3 2.6 fusion.170
  298.1 3.6 fusion.171
  303.7 5.5 fusion.94
  309.2 2.3 multiply_reduce_fusion.4
  311.6 11.1 %fusion.43 = f32[1024,3072]{1,0:T(8,128)} fusion(bf16[768,3072]{1,0:T(8,128)(2,1)} %all-gather.18.cloned.1.call-done, f32[1024,768]{0,1:T(8,128)} %get-tuple-element.301, f32[768]{0:T(1024)S(1)} %copy-done.21, f32[768]{0:T(1024)S(1)} %copy-done.15, f32[1024]{0:T(1024)S(1)} %add_rsqrt_fusion.1, f32[1024]{0:T(1024)S(1)} %broadcast_multiply_fusion.9), kind=kOutput, calls=%fused_computation.93 | convolution fusion | flops 4835770368 | bytes 20461568 | tf_op jit(solution)/shard_map/dot_general | solution.py:178
  322.7 43.7 %all-gather.20.cloned.1.call-done = bf16[3072,768]{1,0:T(8,128)(2,1)} async-done(((bf16[96,768]{1,0:T(8,128)(2,1)}), bf16[3072,768]{1,0:T(8,128)(2,1)}) %all-gather.20.cloned.1.call-update) | async-done | bytes 4718608 | tf_op jit(solution)/shard_map/all_gather | solution.py:137
  366.4 47.5 %fusion.95 = (f32[1024]{0:T(1024)S(1)}, f32[1024,768]{0,1:T(8,128)S(1)}) fusion(f32[768]{0:T(1024)S(1)} %copy-done.45, bf16[3072,768]{1,0:T(8,128)(2,1)} %all-gather.20.cloned.1.call-done, f32[1024,3072]{1,0:T(8,128)} %fusion.43, f32[3072]{0:T(1024)S(1)} %copy-done.44, f32[768]{0:T(1024)S(1)} %copy-done.21, f32[768]{0:T(1024)S(1)} %copy-done.15, ...), kind=kOutput, calls=%fused_computation.187 | convolution fusion | flops 5044960256 | bytes 23626752 | tf_op jit(solution)/shard_map/dot_general | solution.py:182
  414.4 2.1 copy-done.9
  416.5 3.4 fusion.39
  419.9 23.8 %multiply_reduce_fusion.1 = (f32[768]{0:T(1024)}, f32[1024]{0:T(1024)S(1)}, f32[1024]{0:T(1024)S(1)}, f32[768]{0:T(1024)}, f32[1024,768]{0,1:T(8,128)}) fusion(f32[1024,768]{0,1:T(8,128)} %get-tuple-element.301, f32[1024]{0:T(1024)S(1)} %add_rsqrt_fusion.1, f32[1024]{0:T(1024)S(1)} %broadcast_multiply_fusion.9, f32[768]{0:T(1024)S(1)} %copy-done.15, ...), kind=kOutput, calls=%fused_computation.74 | convolution fusion | flops 9719508992 | bytes 33087488 | tf_op jit(solution)/shard_map/dot_general | solution.py:200
  443.8 6.2 convolution_convert_fusion
  453.8 93.9 %while.27 = (s32[]{:T(128)}, bf16[2,512,768]{2,1,0:T(8,128)(2,1)}, bf16[2,512,768]{2,1,0:T(8,128)(2,1)}, bf16[2,512,768]{2,1,0:T(8,128)(2,1)}, bf16[2,512,768]{1...) while((s32[]{:T(128)}, bf16[2,512,768]{2,1,0:T(8,128)(2,1)}, ...), condition=%wide.region_14.15_spmd, body=%wide.region_12.14_spmd.sunk | while | flops 2062673920 | bytes 202554704 | solution.py:214
  454.2 1.8 constant_dynamic-slice_fusion.20
  456.1 6.4 fusion.182
  464.9 11.0 %multiply_reduce_fusion.7 = (f32[12,512]{1,0:T(8,128)S(1)}, f32[12,512,512]{1,2,0:T(8,128)}) fusion(f32[12,512,512]{1,2,0:T(8,128)} %fusion.182, f32[12,512]{1,0:T(8,128)S(1)} %dynamic-slice_bitcast_fusion.2, pred[512,512]{0,1:T(8,128)(4,1)S(1)} %broadcast_compare_fusion.5, bf16[512,12,64]{0,2,1:T(8,128)(2,1)S(1)} %bitcast.183, ...), kind=kOutput, calls=%fused_computation.17.clone.1 | convolution fusion | flops 418375680 | bytes 27049984 | tf_op jit(solution)/shard_map/while/body/eval_jaxpr/qhd,khd->hqk/dot_general | solution.py:68
  477.5 7.0 %multiply_convert_fusion.6 = bf16[12,512,512]{1,2,0:T(8,128)(2,1)S(1)} fusion(f32[12,512,512]{1,2,0:T(8,128)} %get-tuple-element.423, f32[12,512,512]{1,2,0:T(8,128)S(1)} %bitcast.177, f32[12,512]{1,0:T(8,128)S(1)} %get-tuple-element.424, f32[12,512]{1,0:T(8,128)S(1)} %dynamic-slice_bitcast_fusion.2, pred[512,512]{0,1:T(8,128)(4,1)S(1)} %broadcast_compare_fusion.5), kind=kLoop, calls=%fused_computation.16.clone.1 | loop fusion | flops 18874368 | bytes 31768576 | tf_op jit(solution)/shard_map/while/body/eval_jaxpr/convert_element_type | solution.py:72
  484.5 2.0 multiply_convert_fusion.8
  487.4 6.3 fusion.183
  495.3 3.9 multiply_convert_fusion.7
  500.9 1.7 constant_dynamic-slice_fusion.20
  502.7 6.4 fusion.182
  511.6 11.0 %multiply_reduce_fusion.7 = (f32[12,512]{1,0:T(8,128)S(1)}, f32[12,512,512]{1,2,0:T(8,128)}) fusion(f32[12,512,512]{1,2,0:T(8,128)} %fusion.182, f32[12,512]{1,0:T(8,128)S(1)} %dynamic-slice_bitcast_fusion.2, pred[512,512]{0,1:T(8,128)(4,1)S(1)} %broadcast_compare_fusion.5, bf16[512,12,64]{0,2,1:T(8,128)(2,1)S(1)} %bitcast.183, ...), kind=kOutput, calls=%fused_computation.17.clone.1 | convolution fusion | flops 418375680 | bytes 27049984 | tf_op jit(solution)/shard_map/while/body/eval_jaxpr/qhd,khd->hqk/dot_general | solution.py:68
  524.2 7.0 %multiply_convert_fusion.6 = bf16[12,512,512]{1,2,0:T(8,128)(2,1)S(1)} fusion(f32[12,512,512]{1,2,0:T(8,128)} %get-tuple-element.423, f32[12,512,512]{1,2,0:T(8,128)S(1)} %bitcast.177, f32[12,512]{1,0:T(8,128)S(1)} %get-tuple-element.424, f32[12,512]{1,0:T(8,128)S(1)} %dynamic-slice_bitcast_fusion.2, pred[512,512]{0,1:T(8,128)(4,1)S(1)} %broadcast_compare_fusion.5), kind=kLoop, calls=%fused_computation.16.clone.1 | loop fusion | flops 18874368 | bytes 31768576 | tf_op jit(solution)/shard_map/while/body/eval_jaxpr/convert_element_type | solution.py:72
  531.2 2.0 multiply_convert_fusion.8
  534.1 6.3 fusion.183
  541.9 3.9 multiply_convert_fusion.7
  547.8 1.9 fusion.55
  549.7 2.0 fusion.52
  555.5 2.8 fusion.99
  562.0 3.6 add_add_fusion
  565.5 2.4 copy.136
  567.9 2.6 copy.135
  570.6 105.9 %all-reduce.4.cloned.1.call-done = (f32[2,768,8]{1,2,0:T(8,128)}, f32[2,8,768]{2,1,0:T(8,128)}, f32[2,768]{1,0:T(2,128)}, f32[2,768]{1,0:T(2,128)}) async-done(((f32[2,768,8]{1,2,0:T(8,128)}, f32[2,8,768]{2,1,0:T(8,128)}, f32[2,768]{1,0:T(2,128)}, f32[2,768]{1,0:T(2,128)}), (f32[2,768,8]{1,2,0:T(8,128)}, f32[2,8,768]{2,1,0:T(8,128)}, f32[2,768]{1,0:T(2,128)}, ...) | async-done | bytes 110608 | tf_op jit(solution)/shard_map/psum | solution.py:257
  (238 shorter events, 60.0 us)
Async XLA Ops:
  7.2 79.3 %copy-start.48 = (bf16[2,24]{1,0:T(2,128)(2,1)S(1)}, bf16[2,24]{1,0:T(2,128)(2,1)}, u32[]{:S(2)}) copy-start(bf16[2,24]{1,0:T(2,128)(2,1)} %param.35) | copy-start | bytes 292
  7.2 143.2 %copy-start.49 = (bf16[2,24]{1,0:T(2,128)(2,1)S(1)}, bf16[2,24]{1,0:T(2,128)(2,1)}, u32[]{:S(2)}) copy-start(bf16[2,24]{1,0:T(2,128)(2,1)} %param.36) | copy-start | bytes 292
  7.2 209.2 %copy-start.52 = (bf16[96]{0:T(256)(128)(2,1)S(1)}, bf16[96]{0:T(256)(128)(2,1)}, u32[]{:S(2)}) copy-start(bf16[96]{0:T(256)(128)(2,1)} %param.34) | copy-start | bytes 580
  7.2 247.1 %copy-start.11 = (bf16[1024,768]{1,0:T(8,128)(2,1)S(1)}, bf16[1024,768]{1,0:T(8,128)(2,1)}, u32[]{:S(2)}) copy-start(bf16[1024,768]{1,0:T(8,128)(2,1)} %param.45) | copy-start | bytes 4718596
  7.2 250.6 %all-gather.10.cloned.1.call-start = ((), (), s32[]{:S(2)}) async-start(), calls=%async_computation | async-start | bytes 1216512 | tf_op jit(solution)/shard_map/all_gather | solution.py:131
  8.0 254.9 %all-gather.12.cloned.1.call-start = ((), (), s32[]{:S(2)}) async-start(), calls=%async_computation.1 | async-start | bytes 1216512 | tf_op jit(solution)/shard_map/all_gather | solution.py:129
  8.7 260.3 %all-gather.14.cloned.1.call-start = ((), (), s32[]{:S(2)}) async-start(), calls=%async_computation.2 | async-start | bytes 1216512 | tf_op jit(solution)/shard_map/all_gather | solution.py:130
  9.4 293.6 %all-gather.16.cloned.1.call-start = ((), (), s32[]{:S(2)}) async-start(), calls=%async_computation.3 | async-start | bytes 1216512 | tf_op jit(solution)/shard_map/all_gather | solution.py:132
  10.0 301.5 %all-gather.18.cloned.1.call-start = ((), (), s32[]{:S(2)}) async-start(), calls=%async_computation.4 | async-start | bytes 4866048 | tf_op jit(solution)/shard_map/all_gather | solution.py:136
  10.6 355.8 %all-gather.20.cloned.1.call-start = ((), (), s32[]{:S(2)}) async-start(), calls=%async_computation.5 | async-start | bytes 4866048 | tf_op jit(solution)/shard_map/all_gather | solution.py:137
  11.2 665.3 %all-reduce.4.cloned.1.call-start = ((), (), s32[]{:S(2)}) async-start(), calls=%async_computation.6 | async-start | bytes 221184 | tf_op jit(solution)/shard_map/psum | solution.py:257
  12.1 245.2 %copy-start.28 = (bf16[768,8]{0,1:T(8,128)(2,1)}, bf16[768,8]{0,1:T(8,128)(2,1)S(1)}, u32[]{:S(2)}) copy-start(bf16[768,8]{0,1:T(8,128)(2,1)S(1)} %get-tuple-element.298) | copy-start | bytes 36868
  12.1 245.2 %copy-start.30 = (bf16[768,8]{0,1:T(8,128)(2,1)}, bf16[768,8]{0,1:T(8,128)(2,1)S(1)}, u32[]{:S(2)}) copy-start(bf16[768,8]{0,1:T(8,128)(2,1)S(1)} %get-tuple-element.299) | copy-start | bytes 36868
  83.8 181.7 %copy-start.24 = (bf16[2,8,768]{2,1,0:T(8,128)(2,1)}, bf16[2,8,768]{2,1,0:T(8,128)(2,1)S(1)}, u32[]{:S(2)}) copy-start(bf16[2,8,768]{2,1,0:T(8,128)(2,1)S(1)} %convert_element_type.144) | copy-start | bytes 73732
  83.8 173.5 %copy-start.3 = (bf16[1024,768]{1,0:T(8,128)(2,1)S(1)}, bf16[1024,768]{1,0:T(8,128)(2,1)}, u32[]{:S(2)}) copy-start(bf16[1024,768]{1,0:T(8,128)(2,1)} %param.25) | copy-start | bytes 4718596
  257.8 7.7 %copy-start.22 = (bf16[1024,16]{0,1:T(8,128)(2,1)}, bf16[1024,16]{0,1:T(8,128)(2,1)S(1)}, u32[]{:S(2)}) copy-start(bf16[1024,16]{0,1:T(8,128)(2,1)S(1)} %fusion.51) | copy-start | bytes 98308
  309.1 134.6 %copy-start.13 = (f32[1024]{0:T(1024)}, f32[1024]{0:T(1024)S(1)}, u32[]{:S(2)}) copy-start(f32[1024]{0:T(1024)S(1)} %broadcast_multiply_fusion.9) | copy-start | bytes 12292
  311.5 132.3 %copy-start.17 = (f32[1024]{0:T(1024)}, f32[1024]{0:T(1024)S(1)}, u32[]{:S(2)}) copy-start(f32[1024]{0:T(1024)S(1)} %add_rsqrt_fusion.1) | copy-start | bytes 12292
  311.5 54.9 %copy-start.44 = (f32[3072]{0:T(1024)S(1)}, f32[3072]{0:T(1024)}, u32[]{:S(2)}) copy-start(f32[3072]{0:T(1024)} %convert_element_type.151) | copy-start | bytes 36868
  311.6 54.8 %copy-start.45 = (f32[768]{0:T(1024)S(1)}, f32[768]{0:T(1024)}, u32[]{:S(2)}) copy-start(f32[768]{0:T(1024)} %get-tuple-element.233) | copy-start | bytes 9220
  413.9 6.0 copy-start.7
  443.7 6.3 copy-start.40
  443.7 6.3 copy-start.42
  453.8 93.9 %copy-start.23 = (bf16[1024,16]{0,1:T(8,128)(2,1)S(1)}, bf16[1024,16]{0,1:T(8,128)(2,1)}, u32[]{:S(2)}) copy-start(bf16[1024,16]{0,1:T(8,128)(2,1)} %copy-done.22) | copy-start | bytes 98308
  454.2 8.2 %copy-start.1 = (bf16[2,512,768]{1,2,0:T(8,128)(2,1)}, bf16[2,512,768]{1,2,0:T(8,128)(2,1)S(1)}, u32[]{:S(2)}) copy-start(bf16[2,512,768]{1,2,0:T(8,128)(2,1)S(1)} %get-tuple-element.479) | copy-start | bytes 4718596 | tf_op jit(solution)/shard_map/while
  456.1 7.3 %copy-start.8 = (bf16[2,512,768]{2,1,0:T(8,128)(2,1)S(1)}, bf16[2,512,768]{2,1,0:T(8,128)(2,1)}, u32[]{:S(2)}) copy-start(bf16[2,512,768]{2,1,0:T(8,128)(2,1)} %get-tuple-element.481) | copy-start | bytes 4718596 | tf_op jit(solution)/shard_map/while
  464.9 11.0 %slice-start = ((s8[12582912]{0:T(1024)(128)(4,1)}), s8[4194304]{0:T(1024)(128)(4,1)S(1)}, s32[]{:S(2)}) async-start(s8[12582912]{0:T(1024)(128)(4,1)} %bitcast.176), calls=%async_computation.7 | async-start | bytes 8388608 | tf_op jit(solution)/shard_map/while
  464.9 11.0 %slice-start.1 = ((s8[12582912]{0:T(1024)(128)(4,1)}), s8[4194304]{0:T(1024)(128)(4,1)S(1)}, s32[]{:S(2)}) async-start(s8[12582912]{0:T(1024)(128)(4,1)} %bitcast.176), calls=%async_computation.8 | async-start | bytes 8388608 | tf_op jit(solution)/shard_map/while
  464.9 12.6 %slice-start.2 = ((s8[12582912]{0:T(1024)(128)(4,1)}), s8[4194304]{0:T(1024)(128)(4,1)S(1)}, s32[]{:S(2)}) async-start(s8[12582912]{0:T(1024)(128)(4,1)} %bitcast.176), calls=%async_computation.9 | async-start | bytes 8388608 | tf_op jit(solution)/shard_map/while
  500.9 8.2 %copy-start.1 = (bf16[2,512,768]{1,2,0:T(8,128)(2,1)}, bf16[2,512,768]{1,2,0:T(8,128)(2,1)S(1)}, u32[]{:S(2)}) copy-start(bf16[2,512,768]{1,2,0:T(8,128)(2,1)S(1)} %get-tuple-element.479) | copy-start | bytes 4718596 | tf_op jit(solution)/shard_map/while
  502.7 7.3 %copy-start.8 = (bf16[2,512,768]{2,1,0:T(8,128)(2,1)S(1)}, bf16[2,512,768]{2,1,0:T(8,128)(2,1)}, u32[]{:S(2)}) copy-start(bf16[2,512,768]{2,1,0:T(8,128)(2,1)} %get-tuple-element.481) | copy-start | bytes 4718596 | tf_op jit(solution)/shard_map/while
  511.6 11.0 %slice-start = ((s8[12582912]{0:T(1024)(128)(4,1)}), s8[4194304]{0:T(1024)(128)(4,1)S(1)}, s32[]{:S(2)}) async-start(s8[12582912]{0:T(1024)(128)(4,1)} %bitcast.176), calls=%async_computation.7 | async-start | bytes 8388608 | tf_op jit(solution)/shard_map/while
  511.6 11.0 %slice-start.1 = ((s8[12582912]{0:T(1024)(128)(4,1)}), s8[4194304]{0:T(1024)(128)(4,1)S(1)}, s32[]{:S(2)}) async-start(s8[12582912]{0:T(1024)(128)(4,1)} %bitcast.176), calls=%async_computation.8 | async-start | bytes 8388608 | tf_op jit(solution)/shard_map/while
  511.6 12.6 %slice-start.2 = ((s8[12582912]{0:T(1024)(128)(4,1)}), s8[4194304]{0:T(1024)(128)(4,1)S(1)}, s32[]{:S(2)}) async-start(s8[12582912]{0:T(1024)(128)(4,1)} %bitcast.176), calls=%async_computation.9 | async-start | bytes 8388608 | tf_op jit(solution)/shard_map/while
  547.7 4.0 copy-start.6
  547.7 4.3 copy-start.25
  547.7 4.8 copy-start.47
  547.7 4.8 copy-start.39
  547.7 4.8 copy-start.46
  547.8 4.9 copy-start.38
  547.8 4.9 copy-start.4
  549.7 5.8 copy-start.5
  567.9 111.2 %copy-start.26 = (f32[2,8,768]{2,1,0:T(8,128)S(1)}, f32[2,8,768]{2,1,0:T(8,128)}, u32[]{:S(2)}) copy-start(f32[2,8,768]{2,1,0:T(8,128)} %param.38) | copy-start | bytes 147460
  567.9 111.2 %copy-start.32 = (f32[2,8,768]{2,1,0:T(8,128)S(1)}, f32[2,8,768]{2,1,0:T(8,128)}, u32[]{:S(2)}) copy-start(f32[2,8,768]{2,1,0:T(8,128)} %param.42) | copy-start | bytes 147460
  567.9 111.2 %copy-start.33 = (f32[2,8,768]{2,1,0:T(8,128)S(1)}, f32[2,8,768]{2,1,0:T(8,128)}, u32[]{:S(2)}) copy-start(f32[2,8,768]{2,1,0:T(8,128)} %param.41) | copy-start | bytes 147460
  567.9 112.7 %copy-start.27 = (f32[2,768,8]{1,2,0:T(8,128)S(1)}, f32[2,768,8]{1,2,0:T(8,128)}, u32[]{:S(2)}) copy-start(f32[2,768,8]{1,2,0:T(8,128)} %param.37) | copy-start | bytes 147460
  567.9 112.7 %copy-start.34 = (f32[2,768,8]{1,2,0:T(8,128)S(1)}, f32[2,768,8]{1,2,0:T(8,128)}, u32[]{:S(2)}) copy-start(f32[2,768,8]{1,2,0:T(8,128)} %param.40) | copy-start | bytes 147460
  567.9 112.6 %copy-start.35 = (f32[2,768,8]{1,2,0:T(8,128)S(1)}, f32[2,768,8]{1,2,0:T(8,128)}, u32[]{:S(2)}) copy-start(f32[2,768,8]{1,2,0:T(8,128)} %param.39) | copy-start | bytes 147460
  (22 other events, 46.5 us)
Sparse Core Ops, SparseCore 0:
  11.0 56.7 all-gather.9
  70.7 53.0 all-gather.11
  126.7 53.1 all-gather.13
  182.7 53.0 all-gather.15
  238.5 62.5 all-gather.17
  303.8 62.5 all-gather.19
  555.6 120.8 all-reduce.3
where the time goes:
time: 697 us; the launch traced here: 689 us
  blocking collectives  235 us (34%)
  matrix products  191 us (27%)
  waiting for transfers between devices  153 us (22%)
  local copies, waits for them, and re-layouts  55.2 us (8%)
  other arithmetic  36.3 us (5%)
  between operations  16.3 us (2%)
    psum x1, waiting for transfers between devices, per_device(): lax.psum((local_down, local_up, local_gain, local_shift), ('dp', 'fsdp'))  106 us
    all_gather x1, blocking collectives, per_device(): lax.all_gather(fixed_projection_bias, ('dp', 'fsdp'), axis=1, tiled=True)  70 us
    all_gather x1, blocking collectives, per_device(): lax.all_gather(layer_norm_shift, ('dp', 'fsdp'), axis=1, tiled=True)  65.2 us
    all_gather x1, blocking collectives, per_device(): lax.all_gather(layer_norm_gain, ('dp', 'fsdp'), axis=1, tiled=True)  63 us
    dot_general x1, matrix products, per_device(): jnp.dot(activated, outer_full, preferred_element_type=jnp.float32)  47.5 us
    all_gather x1, waiting for transfers between devices, per_device(): lax.all_gather(outer_weight, ('dp', 'fsdp'), axis=0, tiled=True)  43.7 us
    unnamed x1, blocking collectives  37 us
    dot_general x1, matrix products, per_device(): jnp.dot(grad_inner, inner_full.T, preferred_element_type=jnp.float32)  23.8 us
  transfers between devices with their start and end apart: 7, of which 2 were waited for; matrix products, arithmetic and copies ran while one was open for 13% of the time, Pallas kernels for 0%

commit v1 on v0

v1 whole, which is shorter than its diff:
```python
import functools
import math

import jax
import jax.numpy as jnp
import numpy as np
from jax import lax
from jax.experimental import pallas as pl
from jax.experimental.pallas import tpu as pltpu
from jax.sharding import PartitionSpec as P

HEAD = 64
AXES = ("dp", "fsdp")

beta_one = 0.9
beta_two = 0.999
adam_epsilon = 1e-08
down_decay_factor = 0.05
up_decay_factor = 0.01
norm_epsilon = 1e-05
masked_score = -1e30
root_circle = 1.0 / math.sqrt(2.0 * math.pi)
LANES = 128
MIB = 1 << 20

f32 = jnp.float32
bf16 = jnp.bfloat16


def nn(a, b):
    return lax.dot_general(a, b, (((1,), (0,)), ((), ())), preferred_element_type=f32)


def nt(a, b):
    return lax.dot_general(a, b, (((1,), (1,)), ((), ())), preferred_element_type=f32)


class Layout:
    def __init__(self, mesh):
        n_dp, n_fsdp = mesh.shape["dp"], mesh.shape["fsdp"]
        self.n = n_dp * n_fsdp
        self.core = n_fsdp
        n_x = n_dp // 2
        n_y = n_x
        y_bits = [1 << t for t in range(int(math.log2(n_y)))]
        z_bits = [n_y << t for t in range(int(math.log2(n_fsdp // n_y)))]
        x_bits = [(2 * n_fsdp) << t for t in range(int(math.log2(n_x)))]
        self.orders = (z_bits + x_bits + y_bits, z_bits[::-1] + y_bits + x_bits)
        self.bits = y_bits + z_bits + x_bits + [self.core]

    def order_of(self, i):
        return self.orders[1 if i & self.core else 0]

    def stage_pairs(self, t):
        return [(i, i ^ self.order_of(i)[t]) for i in range(self.n)]

    def core_pairs(self):
        return [(i, i ^ self.core) for i in range(self.n)]

    def block_masks(self, order):
        masks = [0]
        for bit in order:
            masks = masks + [m ^ bit for m in masks]
        return masks


def gather_blocks(block, layout):
    held = block[None]
    stages = len(layout.orders[0])
    for t in range(stages):
        came = lax.ppermute(held, AXES, layout.stage_pairs(t))
        if t < stages - 1:
            held = jnp.concatenate([held, came], axis=0)
    return (
        held,
        came,
        lax.ppermute(held, AXES, layout.core_pairs()),
        lax.ppermute(came, AXES, layout.core_pairs()),
    )


def block_ids(layout):
    me = lax.axis_index(AXES).astype(jnp.int32)
    one, two = (np.array(layout.block_masks(o), np.int32) for o in layout.orders)
    second = (me & layout.core) != 0
    own = me ^ jnp.where(second, two, one)
    other = me ^ layout.core ^ jnp.where(second, one, two)
    return jnp.concatenate([own, other])


def as_blocks(full, count):
    return tuple(
        part for part in full.reshape((4, count // 4) + (full.shape[0] // count,) + full.shape[1:])
    )


def fetch_blocks(ids_ref, parts, stage, sems):
    each = parts[0].shape[0]
    for a, part in enumerate(parts):
        for j in range(each):
            k = a * each + j
            at = ids_ref[k]
            pltpu.make_async_copy(part.at[j], stage.at[at], sems.at[at]).start()


def wait_block(parts, stage, sems, i):
    pltpu.make_async_copy(parts[0].at[0], stage.at[i], sems.at[i]).wait()


def merge_pairs(parts, stage, sems, target, width, extra=None):
    shards, rows = stage.shape[0], stage.shape[1]
    for i in range(0, shards, 2):
        wait_block(parts, stage, sems, i)
        wait_block(parts, stage, sems, i + 1)
        for c in range(0, width, 768):
            low = stage[i, :, c : c + 768].astype(f32)
            high = stage[i + 1, :, c : c + 768].astype(f32)
            target[rows * i : rows * (i + 2), c : c + 768] = jnp.concatenate(
                [low, high], axis=0
            ).astype(bf16)


def spread(piece, width, step, count):
    lane = lax.broadcasted_iota(jnp.int32, (LANES, width), 1).astype(f32)
    slot = lax.broadcasted_iota(jnp.int32, (LANES, width), 0).astype(f32)
    within = lane - step * jnp.floor((lane + 0.5) * (1.0 / step))
    place = (within == slot).astype(bf16)
    wide = nn(piece.astype(bf16), place)
    at = lax.broadcasted_iota(jnp.int32, (8, width), 1)
    total = jnp.zeros((8, width), f32)
    for i in range(count):
        mine = (at >= step * i) & (at < step * (i + 1))
        total = total + jnp.where(mine, wide[8 * i : 8 * (i + 1)], 0.0)
    return total


def project_kernel(ids_ref, x_ref, down_ref, up_ref, p0, p1, p2, p3, qkv_ref, weight_ref, red_ref,
                   small_ref, inner_bias_ref, stage, sems):
    parts = (p0, p1, p2, p3)
    width = x_ref.shape[1]
    rank = down_ref.shape[1]

    @pl.when(pl.program_id(0) == 0)
    def _():
        fetch_blocks(ids_ref, parts, stage, sems)
        merge_pairs(parts, stage, sems, weight_ref, 3 * width)
        shards, rows = stage.shape[0], stage.shape[1]
        tail = stage[:, :, 3 * width :].astype(f32)
        small_ref[...] = spread(tail[:, 0:8].reshape(8 * shards, LANES), width, rows, shards)
        ff = inner_bias_ref.shape[1]
        inner_bias_ref[...] = spread(
            tail[:, 8:16].reshape(8 * shards, LANES), ff, ff // shards, shards
        )

    x = x_ref[...]
    down = down_ref[...].reshape(2 * rank, width).astype(bf16)
    up = (2.0 * up_ref[...].astype(bf16).astype(f32)).astype(bf16)
    zero = jnp.zeros((rank, width), bf16)
    reduced = nt(x, down).astype(bf16)
    red_ref[...] = nt(down, x).astype(bf16)
    up_query = jnp.concatenate([up[0], zero], axis=0)
    up_value = jnp.concatenate([zero, up[1]], axis=0)
    chunk = 256
    for c in range(0, 3 * width, chunk):
        y = nn(x, weight_ref[:, c : c + chunk])
        o = c % width
        if c < width:
            y = y + small_ref[0:1, o : o + chunk] + nn(reduced, up_query[:, o : o + chunk])
        elif c >= 2 * width:
            y = y + small_ref[1:2, o : o + chunk] + nn(reduced, up_value[:, o : o + chunk])
        qkv_ref[:, c : c + chunk] = y.astype(bf16)


def project(ids, tokens, down, up, parts):
    rows, width = tokens.shape
    shards = 4 * parts[0].shape[0]
    shard_rows = parts[0].shape[1]
    ff = 4 * width
    tile = 256
    whole = lambda *shape: pl.BlockSpec(shape, lambda i: (0,) * len(shape))
    return pl.pallas_call(
        project_kernel,
        grid=(rows // tile,),
        in_specs=[
            pl.BlockSpec(memory_space=pltpu.SMEM),
            pl.BlockSpec((tile, width), lambda i: (i, 0)),
            whole(*down.shape),
            whole(*up.shape),
        ]
        + [pl.BlockSpec(memory_space=pl.ANY)] * 4,
        out_specs=[
            pl.BlockSpec((tile, 3 * width), lambda i: (i, 0)),
            whole(width, 3 * width),
            pl.BlockSpec((2 * down.shape[1], tile), lambda i: (0, i)),
            whole(8, width),
            whole(8, ff),
        ],
        out_shape=[
            jax.ShapeDtypeStruct((rows, 3 * width), bf16),
            jax.ShapeDtypeStruct((width, 3 * width), bf16),
            jax.ShapeDtypeStruct((2 * down.shape[1], rows), bf16),
            jax.ShapeDtypeStruct((8, width), f32),
            jax.ShapeDtypeStruct((8, ff), f32),
        ],
        scratch_shapes=[
            pltpu.VMEM((shards, shard_rows, 3 * width + LANES), bf16),
            pltpu.SemaphoreType.DMA((shards,)),
        ],
        compiler_params=pltpu.CompilerParams(vmem_limit_bytes=40 * MIB),
        cost_estimate=pl.CostEstimate(
            flops=2 * rows * width * width * 3, bytes_accessed=14 * MIB, transcendentals=0
        ),
    )(ids, tokens, down, up, *parts)


def attend_kernel(seg_ref, q_ref, k_ref, v_ref, ctx_ref, w_ref, mask):
    pack, rows = seg_ref.shape[1], seg_ref.shape[1]

    @pl.when(pl.program_id(1) == 0)
    def _():
        row = jnp.broadcast_to(seg_ref[pl.ds(pl.program_id(0), 1), :].astype(f32), (8, rows))
        column = row.T[:, 0:1]
        mask[...] = jnp.where(column == row[0:1], 0.0, masked_score)

    lane = lax.broadcasted_iota(jnp.int32, (1, LANES), 1)
    for s in range(q_ref.shape[1] // LANES):
        cols = slice(s * LANES, (s + 1) * LANES)
        q = q_ref[:, cols] * jnp.asarray(HEAD**-0.5, bf16)
        k = k_ref[:, cols]
        v = v_ref[:, cols]
        ctx = None
        for h in range(2):
            mine = (lane < HEAD) if h == 0 else (lane >= HEAD)
            scores = nt(jnp.where(mine, q, jnp.zeros_like(q)), k) + mask[...]
            peak = jnp.max(scores, axis=-1, keepdims=True)
            exponent = jnp.exp(scores - peak)
            total = jnp.sum(exponent, axis=-1, keepdims=True)
            weights = (exponent * (1.0 / total)).astype(bf16)
            w_ref[2 * s + h] = weights
            part = nn(weights, jnp.where(mine, v, jnp.zeros_like(v)))
            ctx = part if ctx is None else ctx + part
        ctx_ref[:, cols] = ctx.astype(bf16)


HEADS_A_STEP = 4


def attend(segments, qkv):
    packs, length = segments.shape
    rows, wide = qkv.shape
    width = wide // 3
    step = HEADS_A_STEP * HEAD
    steps = width // step
    at = lambda which: pl.BlockSpec((length, step), lambda p, s: (p, which * steps + s))
    return pl.pallas_call(
        attend_kernel,
        grid=(packs, steps),
        in_specs=[pl.BlockSpec((packs, length), lambda p, s: (0, 0)), at(0), at(1), at(2)],
        out_specs=[
            pl.BlockSpec((length, step), lambda p, s: (p, s)),
            pl.BlockSpec((HEADS_A_STEP, length, length), lambda p, s: (p * steps + s, 0, 0)),
        ],
        out_shape=[
            jax.ShapeDtypeStruct((rows, width), bf16),
            jax.ShapeDtypeStruct((packs * width // HEAD, length, length), bf16),
        ],
        scratch_shapes=[pltpu.VMEM((length, length), f32)],
        compiler_params=pltpu.CompilerParams(vmem_limit_bytes=40 * MIB),
        cost_estimate=pl.CostEstimate(
            flops=16 * rows * length * width, bytes_accessed=20 * MIB, transcendentals=rows * length * 12
        ),
    )(segments, qkv, qkv, qkv)


def stats(value):
    centred = value - jnp.mean(value, axis=-1, keepdims=True)
    inverse = lax.rsqrt(jnp.mean(centred * centred, axis=-1, keepdims=True) + norm_epsilon)
    return centred * inverse, inverse


def norm_back(grad, normed, inverse, gain):
    scaled = grad * gain
    return inverse * (
        scaled
        - jnp.mean(scaled, axis=-1, keepdims=True)
        - normed * jnp.mean(scaled * normed, axis=-1, keepdims=True)
    )


def gelu_parts(z):
    size = jnp.abs(z)
    t = 1.0 / (1.0 + 0.2316419 * size)
    density = jnp.exp(z * z * -0.5) * root_circle
    poly = t * (
        0.319381530
        + t * (-0.356563782 + t * (1.781477937 + t * (-1.821255978 + t * 1.330274429)))
    )
    tail = density * poly
    cumulative = jnp.where(z >= 0.0, 1.0 - tail, tail)
    return z * cumulative, cumulative + z * density


def rows_kernel(ids_ref, x_ref, cot_ref, ctx_ref, small_ref, inner_bias_ref, b0, b1, b2, b3, d0, d1, d2, d3,
                act_ref, mid_ref, dctx_ref, sums_ref,
                stage, wo, wi, wf, active, slope, sem_b, sem_d):
    parts_b, parts_d = (b0, b1, b2, b3), (d0, d1, d2, d3)
    width = x_ref.shape[1]
    ff = wi.shape[1]
    shard = d0.shape[1]

    @pl.when(pl.program_id(0) == 0)
    def _():
        fetch_blocks(ids_ref, parts_b, stage, sem_b)
        each = d0.shape[0]
        for a, part in enumerate(parts_d):
            for j in range(each):
                at = ids_ref[a * each + j]
                pltpu.make_async_copy(
                    part.at[j], wf.at[pl.ds(pl.multiple_of(at * shard, shard), shard)], sem_d.at[at]
                ).start()
        shards, rows = stage.shape[0], stage.shape[1]
        for i in range(0, shards, 2):
            wait_block(parts_b, stage, sem_b, i)
            wait_block(parts_b, stage, sem_b, i + 1)
            for c in range(0, width + ff, width):
                both = jnp.concatenate(
                    [
                        stage[i, :, c : c + width].astype(f32),
                        stage[i + 1, :, c : c + width].astype(f32),
                    ],
                    axis=0,
                ).astype(bf16)
                where = slice(rows * i, rows * (i + 2))
                if c == 0:
                    wo[where] = both
                else:
                    wi[where, c - width : c] = both
        for i in range(shards):
            pltpu.make_async_copy(d0.at[0], wf.at[pl.ds(i * shard, shard)], sem_d.at[i]).wait()
        sums_ref[...] = jnp.zeros_like(sums_ref)

    bias_out, bias_ff = small_ref[2:3], small_ref[3:4]
    gain_one, gain_two = small_ref[4:5], small_ref[5:6]
    shift_one, shift_two = small_ref[6:7], small_ref[7:8]
    chunk = 512
    normed_one, inverse_one = stats(x_ref[...].astype(f32) + (nn(ctx_ref[...], wo[...]) + bias_out))
    first = normed_one * gain_one + shift_one
    first_b = first.astype(bf16)
    outer = None
    for c in range(0, ff, chunk):
        cols = slice(c, c + chunk)
        inner = nn(first_b, wi[:, cols]) + inner_bias_ref[0:1, cols]
        value, grad = gelu_parts(inner)
        active[:, cols] = value.astype(bf16)
        slope[:, cols] = grad.astype(bf16)
    outer = nn(active[...], wf[...]) + bias_ff
    normed_two, inverse_two = stats(first + outer)
    act_ref[...] = (normed_two * gain_two + shift_two).astype(bf16)
    grad_out = cot_ref[...].astype(f32)
    grad_gain_two = jnp.sum(grad_out * normed_two, axis=0, keepdims=True)
    grad_shift_two = jnp.sum(grad_out, axis=0, keepdims=True)
    grad_res = norm_back(grad_out, normed_two, inverse_two, gain_two)
    grad_outer = grad_res.astype(bf16)
    for c in range(0, ff, chunk):
        cols = slice(c, c + chunk)
        grad_active = nt(grad_outer, wf[cols])
        active[:, cols] = (grad_active * slope[:, cols].astype(f32)).astype(bf16)
    grad_first = grad_res + nt(active[...], wi[...])
    grad_gain_one = jnp.sum(grad_first * normed_one, axis=0, keepdims=True)
    grad_shift_one = jnp.sum(grad_first, axis=0, keepdims=True)
    sums_ref[0:4] += jnp.concatenate(
        [grad_gain_one, grad_gain_two, grad_shift_one, grad_shift_two], axis=0
    )
    grad_mid = norm_back(grad_first, normed_one, inverse_one, gain_one)
    mid_ref[...] = grad_mid
    dctx_ref[...] = nt(grad_mid.astype(bf16), wo[...]).astype(bf16)


def row_local(ids, tokens, cotangent, context, small, inner_bias, parts_b, parts_d):
    rows, width = tokens.shape
    ff = inner_bias.shape[1]
    shards = 4 * parts_b[0].shape[0]
    tile = 256
    whole = lambda *shape: pl.BlockSpec(shape, lambda i: (0,) * len(shape))
    tiled = pl.BlockSpec((tile, width), lambda i: (i, 0))
    return pl.pallas_call(
        rows_kernel,
        grid=(rows // tile,),
        in_specs=[pl.BlockSpec(memory_space=pltpu.SMEM), tiled, tiled, tiled, whole(8, width), whole(8, ff)]
        + [pl.BlockSpec(memory_space=pl.ANY)] * 8,
        out_specs=[tiled, tiled, tiled, whole(8, width)],
        out_shape=[
            jax.ShapeDtypeStruct((rows, width), bf16),
            jax.ShapeDtypeStruct((rows, width), f32),
            jax.ShapeDtypeStruct((rows, width), bf16),
            jax.ShapeDtypeStruct((8, width), f32),
        ],
        scratch_shapes=[
            pltpu.VMEM((shards,) + parts_b[0].shape[1:], bf16),
            pltpu.VMEM((width, width), bf16),
            pltpu.VMEM((width, ff), bf16),
            pltpu.VMEM((ff, width), bf16),
            pltpu.VMEM((tile, ff), bf16),
            pltpu.VMEM((tile, ff), bf16),
            pltpu.SemaphoreType.DMA((shards,)),
            pltpu.SemaphoreType.DMA((shards,)),
        ],
        compiler_params=pltpu.CompilerParams(vmem_limit_bytes=56 * MIB),
        cost_estimate=pl.CostEstimate(
            flops=2 * rows * width * (4 * ff + 2 * width), bytes_accessed=20 * MIB, transcendentals=0
        ),
    )(ids, tokens, cotangent, context, small, inner_bias, *parts_b, *parts_d)


def attend_back_kernel(q_ref, k_ref, v_ref, ctx_ref, dctx_ref, w_ref, dq_ref, dk_ref, dv_ref):
    scale = HEAD**-0.5
    lane = lax.broadcasted_iota(jnp.int32, (1, LANES), 1)
    for s in range(q_ref.shape[1] // LANES):
        cols = slice(s * LANES, (s + 1) * LANES)
        q, k, v = q_ref[:, cols], k_ref[:, cols], v_ref[:, cols]
        dctx = dctx_ref[:, cols]
        flat = dctx.astype(f32) * ctx_ref[:, cols].astype(f32)
        q_t = q.T
        dctx_t = dctx.T
        dq = None
        dk_t, dv_t = [], []
        for h in range(2):
            mine = (lane < HEAD) if h == 0 else (lane >= HEAD)
            zero = jnp.zeros_like(q)
            grad_weights = nt(jnp.where(mine, dctx, zero), v)
            delta = jnp.sum(jnp.where(mine, flat, 0.0), axis=-1, keepdims=True)
            weights = w_ref[2 * s + h]
            grad_scores = (weights.astype(f32) * (grad_weights - delta)).astype(bf16)
            part = nn(grad_scores, jnp.where(mine, k, zero))
            dq = part if dq is None else dq + part
            rows = slice(h * HEAD, (h + 1) * HEAD)
            dk_t.append(nn(q_t[rows], grad_scores))
            dv_t.append(nn(dctx_t[rows], weights))
        dq_ref[:, cols] = (dq * scale).astype(bf16)
        dk_ref[:, cols] = (jnp.concatenate(dk_t, axis=0) * scale).T.astype(bf16)
        dv_ref[:, cols] = jnp.concatenate(dv_t, axis=0).T.astype(bf16)


def attend_back(qkv, context, grad_context, weights):
    rows, width = context.shape
    length = weights.shape[1]
    packs = rows // length
    step = HEADS_A_STEP * HEAD
    steps = width // step
    at = lambda which: pl.BlockSpec((length, step), lambda p, s: (p, which * steps + s))
    flat = pl.BlockSpec((length, step), lambda p, s: (p, s))
    return pl.pallas_call(
        attend_back_kernel,
        grid=(packs, steps),
        in_specs=[
            at(0),
            at(1),
            at(2),
            flat,
            flat,
            pl.BlockSpec((HEADS_A_STEP, length, length), lambda p, s: (p * steps + s, 0, 0)),
        ],
        out_specs=[flat] * 3,
        out_shape=[jax.ShapeDtypeStruct((rows, width), bf16)] * 3,
        compiler_params=pltpu.CompilerParams(vmem_limit_bytes=40 * MIB),
        cost_estimate=pl.CostEstimate(
            flops=32 * rows * length * width, bytes_accessed=24 * MIB, transcendentals=0
        ),
    )(qkv, qkv, qkv, context, grad_context, weights)


def adapter_kernel(x_ref, dq_ref, dv_ref, up_ref, red_ref, sums_ref, dred_ref, grads_ref):
    rank = up_ref.shape[1]
    up = (2.0 * up_ref[...].astype(bf16).astype(f32)).astype(bf16)
    dq, dv = dq_ref[...], dv_ref[...]
    zero = jnp.zeros_like(up[0])
    up_query = jnp.concatenate([up[0], zero], axis=0)
    up_value = jnp.concatenate([zero, up[1]], axis=0)
    dred_ref[...] = (nt(dq, up_query) + nt(dv, up_value)).astype(bf16)
    dred_t = (nt(up_query, dq) + nt(up_value, dv)).astype(bf16)
    red = red_ref[...]
    grads_ref[0 : 2 * rank] = nn(dred_t, x_ref[...])
    grads_ref[2 * rank : 3 * rank] = 2.0 * nn(red, dq)[0:rank]
    grads_ref[3 * rank : 4 * rank] = 2.0 * nn(red, dv)[rank : 2 * rank]
    grads_ref[4 * rank : 5 * rank] = sums_ref[...]


def adapter_grads(tokens, dq, dv, up, red, sums):
    rows, width = tokens.shape
    rank = up.shape[1]
    return pl.pallas_call(
        adapter_kernel,
        out_shape=[
            jax.ShapeDtypeStruct((rows, 2 * rank), bf16),
            jax.ShapeDtypeStruct((5 * rank, width), f32),
        ],
        compiler_params=pltpu.CompilerParams(vmem_limit_bytes=24 * MIB),
        cost_estimate=pl.CostEstimate(flops=1 << 27, bytes_accessed=5 * MIB, transcendentals=0),
    )(tokens, dq, dv, up, red, sums)


def input_kernel(mid_ref, dq_ref, dk_ref, dv_ref, dred_ref, down_ref, w_ref, out_ref):
    width = mid_ref.shape[1]
    rank = down_ref.shape[1]
    down = down_ref[...].reshape(2 * rank, width).astype(bf16)
    out_ref[...] = (
        mid_ref[...]
        + nt(dq_ref[...], w_ref[:, 0:width])
        + nt(dk_ref[...], w_ref[:, width : 2 * width])
        + nt(dv_ref[...], w_ref[:, 2 * width : 3 * width])
        + nn(dred_ref[...], down)
    )


def input_gradient(mid, dq, dk, dv, dred, down, weight):
    rows, width = mid.shape
    tile = 256
    whole = lambda *shape: pl.BlockSpec(shape, lambda i: (0,) * len(shape))
    tiled = pl.BlockSpec((tile, width), lambda i: (i, 0))
    return pl.pallas_call(
        input_kernel,
        grid=(rows // tile,),
        in_specs=[
            tiled,
            tiled,
            tiled,
            tiled,
            pl.BlockSpec((tile, dred.shape[1]), lambda i: (i, 0)),
            whole(*down.shape),
            whole(*weight.shape),
        ],
        out_specs=tiled,
        out_shape=jax.ShapeDtypeStruct((rows, width), f32),
        compiler_params=pltpu.CompilerParams(vmem_limit_bytes=40 * MIB),
        cost_estimate=pl.CostEstimate(
            flops=6 * rows * width * width, bytes_accessed=15 * MIB, transcendentals=0
        ),
    )(mid, dq, dk, dv, dred, down, weight)


def adamw_kernel(count, scal_ref, total_ref, down_ref, up_ref, dm_ref, dv_ref, um_ref, uv_ref,
                 gd_ref, gu_ref, gain_ref, shift_ref, pd_ref, pu_ref, dm2_ref, dv2_ref, um2_ref, uv2_ref):
    rank = up_ref.shape[1]
    width = up_ref.shape[2]
    part = 1.0 / count
    first_scale, second_scale, rate = scal_ref[0], scal_ref[1], scal_ref[2]

    def update(param, grad, first, second, learn, decay):
        first_new = beta_one * first + (1.0 - beta_one) * grad
        second_new = beta_two * second + (1.0 - beta_two) * grad * grad
        first_hat = first_new / first_scale
        second_hat = second_new / second_scale
        new = param - learn * (first_hat / (jnp.sqrt(second_hat) + adam_epsilon) + decay * param)
        return new, first_new, second_new

    total = total_ref[...] * part
    grad_down = total[0 : 2 * rank].reshape(2, rank, width)
    grad_up = total[2 * rank : 4 * rank].reshape(2, rank, width)
    gd_ref[...] = grad_down
    gu_ref[...] = grad_up
    gain_ref[...] = total[4 * rank : 4 * rank + 2]
    shift_ref[...] = total[4 * rank + 2 : 4 * rank + 4]
    pd_ref[...], dm2_ref[...], dv2_ref[...] = update(
        down_ref[...], grad_down, dm_ref[...], dv_ref[...], rate, down_decay_factor
    )
    pu_ref[...], um2_ref[...], uv2_ref[...] = update(
        up_ref[...], grad_up, um_ref[...], uv_ref[...], 16.0 * rate, up_decay_factor
    )


def adamw(count, scalars, total, down, up, dm, dv, um, uv):
    width = total.shape[1]
    like = jax.ShapeDtypeStruct(up.shape, f32)
    pair = jax.ShapeDtypeStruct((2, width), f32)
    vmem = pl.BlockSpec(memory_space=pltpu.VMEM)
    return pl.pallas_call(
        functools.partial(adamw_kernel, count),
        in_specs=[pl.BlockSpec(memory_space=pltpu.SMEM)] + [vmem] * 7,
        out_shape=[like, like, pair, pair] + [like] * 6,
    )(scalars, total, down, up, dm, dv, um, uv)


def per_device(
    layout,
    tokens,
    document_numbers,
    query_weight,
    key_weight,
    value_weight,
    output_weight,
    inner_weight,
    outer_weight,
    fixed_projection_bias,
    feedforward_inner_bias,
    layer_norm_gain,
    layer_norm_shift,
    adapter_down_factors,
    adapter_up_factors,
    down_first_moment,
    down_second_moment,
    up_first_moment,
    up_second_moment,
    rate,
    step,
    cotangent,
):
    width = tokens.shape[1]
    shard = query_weight.shape[0]
    small = jnp.concatenate(
        [
            fixed_projection_bias,
            layer_norm_gain,
            layer_norm_shift,
        ],
        axis=0,
    )
    inner_bias = feedforward_inner_bias[None]
    if shard % 8 == 0 and shard * layout.n == width and layout.n == 32:
        tail = jnp.concatenate(
            [
                jnp.pad(small, ((0, 0), (0, LANES - shard))),
                jnp.pad(inner_bias, ((0, shard - 9), (0, LANES - inner_bias.shape[1]))),
            ],
            axis=0,
        )
        block_a = jnp.concatenate([query_weight, key_weight, value_weight, tail], axis=1)
        block_b = jnp.concatenate([output_weight, inner_weight], axis=1)
        parts_a = gather_blocks(block_a, layout)
        parts_b = gather_blocks(block_b, layout)
        parts_d = gather_blocks(outer_weight, layout)
        ids = block_ids(layout)
    else:
        count = 32
        rows = width // count
        whole = lambda w: lax.all_gather(w, AXES, axis=0, tiled=True)
        small_full = lax.all_gather(small, AXES, axis=1, tiled=True)
        bias_full = lax.all_gather(inner_bias, AXES, axis=1, tiled=True)
        tail = jnp.concatenate(
            [
                jnp.pad(small_full.reshape(8, count, rows), ((0, 0), (0, 0), (0, LANES - rows))),
                jnp.pad(
                    bias_full.reshape(1, count, -1),
                    ((0, rows - 9), (0, 0), (0, LANES - bias_full.shape[1] // count)),
                ),
            ],
            axis=0,
        )
        tail = jnp.swapaxes(tail, 0, 1).reshape(width, LANES)
        parts_a = as_blocks(
            jnp.concatenate([whole(query_weight), whole(key_weight), whole(value_weight), tail], axis=1), count
        )
        parts_b = as_blocks(jnp.concatenate([whole(output_weight), whole(inner_weight)], axis=1), count)
        parts_d = as_blocks(whole(outer_weight), count)
        ids = jnp.arange(count, dtype=jnp.int32)

    turn = lambda v: jnp.swapaxes(v, 1, 2)
    down = turn(adapter_down_factors)
    up = adapter_up_factors
    qkv, weight, red, small_rows, inner_rows = project(ids, tokens, down, up, parts_a)
    context, attention = attend(document_numbers, qkv)
    activations, grad_mid, grad_context, sums = row_local(
        ids, tokens, cotangent, context, small_rows, inner_rows, parts_b, parts_d
    )
    grad_query, grad_keys, grad_values = attend_back(qkv, context, grad_context, attention)
    grad_reduced, grads = adapter_grads(tokens, grad_query, grad_values, up, red, sums)
    input_grad = input_gradient(
        grad_mid, grad_query, grad_keys, grad_values, grad_reduced, down, weight
    )
    total = grads
    for bit in [layout.core] + layout.bits[:-1]:
        total = total + lax.ppermute(total, AXES, [(i, i ^ bit) for i in range(layout.n)])
    step_counter = step[0].astype(f32)
    scalars = jnp.stack([1.0 - beta_one**step_counter, 1.0 - beta_two**step_counter, rate[0]])
    gd, gu, gain_grad, shift_grad, pd, pu, dm, dv, um, uv = adamw(
        layout.n,
        scalars,
        total,
        down,
        up,
        turn(down_first_moment),
        turn(down_second_moment),
        up_first_moment,
        up_second_moment,
    )
    return (
        activations,
        input_grad,
        turn(gd),
        gu,
        gain_grad,
        shift_grad,
        turn(pd),
        pu,
        turn(dm),
        turn(dv),
        um,
        uv,
    )


def solution(mesh):
    rows = P(AXES, None)
    columns = P(None, AXES)
    in_specs = (
        (rows,) * 8
        + (columns, P(AXES), columns, columns)
        + (P(),) * 8
        + (rows,)
    )
    out_specs = (rows, rows) + (P(),) * 10
    return jax.shard_map(
        functools.partial(per_device, Layout(mesh)),
        mesh=mesh,
        in_specs=in_specs,
        out_specs=out_specs,
        check_vma=False,
    )
```

time: 697 us -> 220 us (0.32); the launches traced: 689 us -> 219 us
  blocking collectives: 235 us -> 0 us
  matrix products: 191 us -> 0 us
  Pallas kernels: 0 us -> 99.6 us
  waiting for transfers between devices: 153 us -> 75.5 us
  local copies, waits for them, and re-layouts: 55.2 us -> 6.34 us
  other arithmetic: 36.3 us -> 6.77 us
  starting transfers between devices: 0.27 us -> 28.7 us
  between operations: 16.3 us -> 2.52 us
    all_gather x3 -> x0, blocking collectives: 198 us -> none  [the longest x1 70 us: per_device(): lax.all_gather(fixed_projection_bias, ('dp', 'fsdp'), axis=1, tiled=True)]
    dot_general x34 -> x0, matrix products: 191 us -> none  [the longest x1 47.5 us: per_device(): jnp.dot(activated, outer_full, preferred_element_type=jnp.float32)]
    psum x1 -> x0, waiting for transfers between devices: 106 us -> none  [per_device(): lax.psum((local_down, local_up, local_gain, local_shift), ('dp', 'fsdp'))]
    pallas_call x0 -> x7, Pallas kernels: none -> 99.6 us  [the longest x1 44 us: row_local(): pl.pallas_call(rows_kernel, grid=(rows // tile,), in_specs=[pl.BlockSpec(...]
    ppermute x0 -> x23, waiting for transfers between devices: none -> 75.5 us  [the longest x12 61.3 us: gather_blocks(): came = lax.ppermute(held, AXES, layout.stage_pairs(t))]
    all_gather x6 -> x0, waiting for transfers between devices: 43.8 us -> none  [the longest x1 43.7 us: per_device(): lax.all_gather(outer_weight, ('dp', 'fsdp'), axis=0, tiled=True)]
    unnamed x1 -> x0, blocking collectives: 37 us -> none
    ppermute x0 -> x23, starting transfers between devices: none -> 28.7 us  [the longest x12 19.1 us: gather_blocks(): came = lax.ppermute(held, AXES, layout.stage_pairs(t))]
  transfers between devices with their start and end apart: 7 -> 23, of which waited for: 2 -> 12; matrix products, arithmetic and copies ran while one was open for 13% -> 2% of each run, Pallas kernels for 0% -> 16%
where the time goes in v1:
time: 220 us; the launch traced here: 219 us
  Pallas kernels  99.6 us (45%)
  waiting for transfers between devices  75.5 us (34%)
  starting transfers between devices  28.7 us (13%)
  other arithmetic  6.77 us (3%)
  local copies, waits for them, and re-layouts  6.34 us (3%)
  between operations  2.52 us (1%)
    ppermute x12, waiting for transfers between devices, gather_blocks(): came = lax.ppermute(held, AXES, layout.stage_pairs(t))  61.3 us
    pallas_call x1, Pallas kernels, row_local(): pl.pallas_call(rows_kernel, grid=(rows // tile,), in_specs=[pl.BlockSpec(...  44 us
    ppermute x12, starting transfers between devices, gather_blocks(): came = lax.ppermute(held, AXES, layout.stage_pairs(t))  19.1 us
    pallas_call x1, Pallas kernels, attend(): pl.pallas_call(attend_kernel, grid=(packs, steps), in_specs=[pl.BlockSpec...  17 us
    pallas_call x1, Pallas kernels, attend_back(): pl.pallas_call(attend_back_kernel, grid=(packs, steps), in_specs=[at(0),...  16.7 us
    ppermute x5, waiting for transfers between devices, per_device(): lax.ppermute(total, AXES, [(i, i ^ bit) for i in range(layout.n)])  14.2 us
    pallas_call x1, Pallas kernels, project(): pl.pallas_call(project_kernel, grid=(rows // tile,), in_specs=[pl.BlockSp...  11.9 us
    unnamed x40, local copies, waits for them, and re-layouts  6.34 us
  transfers between devices with their start and end apart: 23, of which 12 were waited for; matrix products, arithmetic and copies ran while one was open for 2% of the time, Pallas kernels for 16%

profile of v1, /device:TPU:0, one launch (start us, length us, event | category | flops | bytes accessed | tf_op | source)
XLA Modules:
  0.0 219.3 jit_solution(6594482457286976342)
XLA Ops:
  0.6 0.9 maximum_bitcast_fusion
  1.6 3.1 %collective-permute-start.6 = (bf16[1,24,3840]{2,1,0:T(8,128)(2,1)S(1)}, bf16[1,24,3840]{2,1,0:T(8,128)(2,1)S(1)}, u32[]{:S(2)}, u32[]{:S(2)}) collective-permute-start(bf16[1,24,3840]{2,1,0:T(8,128)(2,1)S(1)} %maximum_bitcast_fusion), channel_id=1, source_target_pairs={{0,2},{1,3},{2,0},{3,1},{4,6},{5,7},{6,4},{7,5},{8,12},{9,13},{10,... | collective-permute-start | bytes 552968 | tf_op jit(solution)/shard_map/ppermute | solution.py:71
  4.7 5.1 %collective-permute-done.6 = bf16[1,24,3840]{2,1,0:T(8,128)(2,1)S(1)} collective-permute-done((bf16[1,24,3840]{2,1,0:T(8,128)(2,1)S(1)}, bf16[1,24,3840]{2,1,0:T(8,128)(2,1)S(1)}, u32[]{:S(2)}, u32[]{:S(2)}) %collective-permute-start.6) | collective-permute-done | bytes 184352 | tf_op jit(solution)/shard_map/ppermute | solution.py:71
  9.8 2.4 %collective-permute-start.7 = (bf16[2,24,3840]{2,1,0:T(8,128)(2,1)S(1)}, bf16[2,24,3840]{2,1,0:T(8,128)(2,1)S(1)}, u32[]{:S(2)}, u32[]{:S(2)}) collective-permute-start(bf16[2,24,3840]{2,1,0:T(8,128)(2,1)S(1)} %pad_maximum_fusion.6), channel_id=1, source_target_pairs={{0,4},{1,5},{2,6},{3,7},{4,0},{5,1},{6,2},{7,3},{8,10},{9,11},{10,... | collective-permute-start | bytes 1105928 | tf_op jit(solution)/shard_map/ppermute | solution.py:71
  12.2 0.7 fusion.10
  12.9 0.8 fusion.5
  13.8 2.6 %collective-permute-start = (bf16[1,24,2432]{2,1,0:T(8,128)(2,1)S(1)}, bf16[1,24,2432]{2,1,0:T(8,128)(2,1)S(1)}, u32[]{:S(2)}, u32[]{:S(2)}) collective-permute-start(bf16[1,24,2432]{2,1,0:T(8,128)(2,1)S(1)} %fusion.5), channel_id=1, source_target_pairs={{0,2},{1,3},{2,0},{3,1},{4,6},{5,7},{6,4},{7,5},{8,12},{9,13},{10,... | collective-permute-start | bytes 350216 | tf_op jit(solution)/shard_map/ppermute | solution.py:71
  16.5 10.5 %collective-permute-done.7 = bf16[2,24,3840]{2,1,0:T(8,128)(2,1)S(1)} collective-permute-done((bf16[2,24,3840]{2,1,0:T(8,128)(2,1)S(1)}, bf16[2,24,3840]{2,1,0:T(8,128)(2,1)S(1)}, u32[]{:S(2)}, u32[]{:S(2)}) %collective-permute-start.7) | collective-permute-done | bytes 368672 | tf_op jit(solution)/shard_map/ppermute | solution.py:71
  27.1 2.5 %collective-permute-start.8 = (bf16[4,24,3840]{2,1,0:T(8,128)(2,1)S(1)}, bf16[4,24,3840]{2,1,0:T(8,128)(2,1)S(1)}, u32[]{:S(2)}, u32[]{:S(2)}) collective-permute-start(bf16[4,24,3840]{2,1,0:T(8,128)(2,1)S(1)} %pad_maximum_fusion.3), channel_id=1, source_target_pairs={{0,16},{1,17},{2,18},{3,19},{4,20},{5,21},{6,22},{7,23},{8,9},{9,8... | collective-permute-start | bytes 2211848 | tf_op jit(solution)/shard_map/ppermute | solution.py:71
  29.7 3.0 %collective-permute-start.13 = (bf16[2,96,768]{2,1,0:T(8,128)(2,1)S(1)}, bf16[2,96,768]{2,1,0:T(8,128)(2,1)S(1)}, u32[]{:S(2)}, u32[]{:S(2)}) collective-permute-start(bf16[2,96,768]{2,1,0:T(8,128)(2,1)S(1)} %pad_maximum_fusion.7), channel_id=1, source_target_pairs={{0,4},{1,5},{2,6},{3,7},{4,0},{5,1},{6,2},{7,3},{8,10},{9,11},{10,... | collective-permute-start | bytes 884744 | tf_op jit(solution)/shard_map/ppermute | solution.py:71
  32.7 9.6 %collective-permute-done.1 = bf16[2,24,2432]{2,1,0:T(8,128)(2,1)S(1)} collective-permute-done((bf16[2,24,2432]{2,1,0:T(8,128)(2,1)S(1)}, bf16[2,24,2432]{2,1,0:T(8,128)(2,1)S(1)}, u32[]{:S(2)}, u32[]{:S(2)}) %collective-permute-start.1) | collective-permute-done | bytes 233504 | tf_op jit(solution)/shard_map/ppermute | solution.py:71
  42.3 0.1 collective-permute-start.2
  42.5 3.0 %collective-permute-done.13 = bf16[2,96,768]{2,1,0:T(8,128)(2,1)S(1)} collective-permute-done((bf16[2,96,768]{2,1,0:T(8,128)(2,1)S(1)}, bf16[2,96,768]{2,1,0:T(8,128)(2,1)S(1)}, u32[]{:S(2)}, u32[]{:S(2)}) %collective-permute-start.13) | collective-permute-done | bytes 294944 | tf_op jit(solution)/shard_map/ppermute | solution.py:71
  45.6 1.3 pad_maximum_fusion.b0
  46.9 2.0 collective-permute-start.9
  49.0 7.1 %collective-permute-done.2 = bf16[4,24,2432]{2,1,0:T(8,128)(2,1)S(1)} collective-permute-done((bf16[4,24,2432]{2,1,0:T(8,128)(2,1)S(1)}, bf16[4,24,2432]{2,1,0:T(8,128)(2,1)S(1)}, u32[]{:S(2)}, u32[]{:S(2)}) %collective-permute-start.2) | collective-permute-done | bytes 466976 | tf_op jit(solution)/shard_map/ppermute | solution.py:71
  56.2 1.6 collective-permute-start.3
  57.8 10.9 %collective-permute-done.14 = bf16[4,96,768]{2,1,0:T(8,128)(2,1)S(1)} collective-permute-done((bf16[4,96,768]{2,1,0:T(8,128)(2,1)S(1)}, bf16[4,96,768]{2,1,0:T(8,128)(2,1)S(1)}, u32[]{:S(2)}, u32[]{:S(2)}) %collective-permute-start.14) | collective-permute-done | bytes 589856 | tf_op jit(solution)/shard_map/ppermute | solution.py:71
  68.7 1.1 pad_maximum_fusion.1.d0
  69.8 1.5 collective-permute-start.15
  71.3 5.2 %collective-permute-done.3.p1 = bf16[8,24,2432]{2,1,0:T(8,128)(2,1)S(1)} collective-permute-done((bf16[8,24,2432]{2,1,0:T(8,128)(2,1)S(1)}, bf16[8,24,2432]{2,1,0:T(8,128)(2,1)S(1)}, u32[]{:S(2)}, u32[]{:S(2)}) %collective-permute-start.3) | collective-permute-done | bytes 933920 | tf_op jit(solution)/shard_map/ppermute | solution.py:71
  76.5 2.2 %collective-permute-start.5 = (bf16[8,24,2432]{2,1,0:T(8,128)(2,1)S(1)}, bf16[8,24,2432]{2,1,0:T(8,128)(2,1)}, u32[]{:S(2)}, u32[]{:S(2)}) collective-permute-start(bf16[8,24,2432]{2,1,0:T(8,128)(2,1)S(1)} %collective-permute-done.3.p1), channel_id=1, source_target_pairs={{0,8},{1,9},{2,10},{3,11},{4,12},{5,13},{6,14},{7,15},{8,0},{9,1},... | collective-permute-start | bytes 2801672 | tf_op jit(solution)/shard_map/ppermute | solution.py:78
  78.7 0.5 collective-permute-start.11
  79.3 9.9 %collective-permute-done.15.d1 = bf16[8,96,768]{2,1,0:T(8,128)(2,1)} collective-permute-done((bf16[8,96,768]{2,1,0:T(8,128)(2,1)}, bf16[8,96,768]{2,1,0:T(8,128)(2,1)}, u32[]{:S(2)}, u32[]{:S(2)}) %collective-permute-start.15) | collective-permute-done | bytes 1179680 | tf_op jit(solution)/shard_map/ppermute | solution.py:71
  89.3 1.8 collective-permute-start.17
  91.2 11.9 %shard_map.310 = (bf16[1024,2304]{1,0:T(8,128)(2,1)S(1)}, bf16[768,2304]{1,0:T(8,128)(2,1)S(1)}, bf16[16,1024]{1,0:T(8,128)(2,1)S(1)}, f32[8,768]{1,0:T(8,128)S(1)}, f32[8,3072]{1,0:T(8,128)S(1)}) custom-call(s32[32]{0:T(128)S(1)} %pad_add_fusion.ids_ref, bf16[1024,768]{1,0:T(8,128)(2,1)S(1)} %copy-done.1, f32[2,8,768]{2,1,0:T(8,128)S(1)} %bitcast.14, ...), custom_call_target="tpu_custom_call" | custom-call | flops 3623878656 | bytes 14680064 | tf_op jit(solution)/shard_map/pallas_call | solution.py:181
  103.2 17.0 %shard_map.311 = (bf16[1024,768]{1,0:T(8,128)(2,1)S(1)}, bf16[24,512,512]{2,1,0:T(8,128)(2,1)}) custom-call(s32[2,512]{1,0:T(2,128)S(1)} %copy-done.6, bf16[1024,2304]{1,0:T(8,128)(2,1)S(1)} %get-tuple-element.38.q_ref.k_ref.v_ref, bf16[1024,2304]{1,0:T(8,128)(2,1)S(1)} %get-tuple-element.38.q_ref.k_ref.v_ref, ...), custom_call_target="tpu_custom_call" | custom-call | flops 6442450944 | bytes 20971520 | tf_op jit(solution)/shard_map/pallas_call | solution.py:255
  120.2 1.1 copy-done.10
  121.4 1.0 copy-done.18
  122.5 0.3 copy-done.19
  122.8 44.0 %shard_map.312 = (bf16[1024,768]{1,0:T(8,128)(2,1)}, f32[1024,768]{1,0:T(8,128)}, bf16[1024,768]{1,0:T(8,128)(2,1)}, f32[8,768]{1,0:T(8,128)}) custom-call(s32[32]{0:T(128)} %copy-done.7, bf16[1024,768]{1,0:T(8,128)(2,1)} %x_ref.5, bf16[1024,768]{1,0:T(8,128)(2,1)} %cot_ref.1, bf16[1024,768]{1,0:T(8,128)(2,1)} %copy-done.10, f32[8,768]{1,0:T(8,128)} %copy-done.14, ...), custom_call_target="tpu_custom_call" | custom-call | flops 21743271936 | bytes 20971520 | tf_op jit(solution)/shard_map/pallas_call | solution.py:386
  166.8 2.3 %copy-done.9 = bf16[1024,2304]{1,0:T(8,128)(2,1)S(1)} copy-done((bf16[1024,2304]{1,0:T(8,128)(2,1)S(1)}, bf16[1024,2304]{1,0:T(8,128)(2,1)}, u32[]{:S(2)}) %copy-start.9) | copy-done | bytes 4718616
  169.1 1.4 copy-done.12
  170.5 16.7 %shard_map.313 = (bf16[1024,768]{1,0:T(8,128)(2,1)S(1)}, bf16[1024,768]{1,0:T(8,128)(2,1)S(1)}, bf16[1024,768]{1,0:T(8,128)(2,1)S(1)}) custom-call(bf16[1024,2304]{1,0:T(8,128)(2,1)S(1)} %copy-done.9, bf16[1024,2304]{1,0:T(8,128)(2,1)S(1)} %copy-done.9, bf16[1024,2304]{1,0:T(8,128)(2,1)S(1)} %copy-done.9, bf16[1024,768]{1,0:T(8,128)(2,1)S(1)} %copy-done.11, ...), custom_call_target="tpu_custom_call" | custom-call | flops 12884901888 | bytes 25165824 | tf_op jit(solution)/shard_map/pallas_call | solution.py:452
  187.3 2.3 %shard_map.314 = (bf16[1024,16]{1,0:T(8,128)(2,1)S(1)}, f32[40,768]{1,0:T(8,128)S(1)}) custom-call(bf16[1024,768]{1,0:T(8,128)(2,1)S(1)} %copy-done.2, bf16[1024,768]{1,0:T(8,128)(2,1)S(1)} %get-tuple-element.46.dq_ref, bf16[1024,768]{1,0:T(8,128)(2,1)S(1)} %get-tuple-element.48.dv_ref, f32[2,8,768]{2,1,0:T(8,128)S(1)} %copy-done.3, ...), custom_call_target="tpu_custom_call" | custom-call | flops 134217728 | bytes 5242880 | tf_op jit(solution)/shard_map/pallas_call | solution.py:491
  189.6 0.3 collective-permute-start.18
  189.9 1.1 collective-permute-done.18
  191.1 1.1 collective-permute-start.19
  192.2 4.4 %collective-permute-done.19 = f32[40,768]{1,0:T(8,128)S(1)} collective-permute-done((f32[40,768]{1,0:T(8,128)S(1)}, f32[40,768]{1,0:T(8,128)S(1)}, u32[]{:S(2)}, u32[]{:S(2)}) %collective-permute-start.19) | collective-permute-done | bytes 122912 | tf_op jit(solution)/shard_map/ppermute | solution.py:671
  196.6 0.6 collective-permute-start.20
  197.3 4.3 %collective-permute-done.20 = f32[40,768]{1,0:T(8,128)S(1)} collective-permute-done((f32[40,768]{1,0:T(8,128)S(1)}, f32[40,768]{1,0:T(8,128)S(1)}, u32[]{:S(2)}, u32[]{:S(2)}) %collective-permute-start.20) | collective-permute-done | bytes 122912 | tf_op jit(solution)/shard_map/ppermute | solution.py:671
  201.6 0.8 collective-permute-start.21
  203.7 0.6 pad_maximum_fusion.9.scal_ref
  204.4 4.3 %collective-permute-done.21 = f32[40,768]{1,0:T(8,128)S(1)} collective-permute-done((f32[40,768]{1,0:T(8,128)S(1)}, f32[40,768]{1,0:T(8,128)S(1)}, u32[]{:S(2)}, u32[]{:S(2)}) %collective-permute-start.21) | collective-permute-done | bytes 122912 | tf_op jit(solution)/shard_map/ppermute | solution.py:671
  208.8 2.2 collective-permute-start.22
  210.9 5.8 %shard_map.315 = f32[1024,768]{1,0:T(8,128)} custom-call(f32[1024,768]{1,0:T(8,128)S(1)} %copy-done, bf16[1024,768]{1,0:T(8,128)(2,1)S(1)} %get-tuple-element.46.dq_ref, bf16[1024,768]{1,0:T(8,128)(2,1)S(1)} %get-tuple-element.47.dk_ref, bf16[1024,768]{1,0:T(8,128)(2,1)S(1)} %get-tuple-element.48.dv_ref, bf16[1024,16]{1,0:T(8,128)(2,1)S(1)} %get-tuple-element.51.dred_ref, ...), custom_call_target="tpu_custom_call" | custom-call | flops 3623878656 | bytes 15728640 | tf_op jit(solution)/shard_map/pallas_call | solution.py:520
  216.7 0.7 add.27.total_ref
  217.4 1.8 shard_map.316
  (65 shorter events, 1.0 us)
Async XLA Ops:
  1.6 28.1 %copy-start.15 = (bf16[96,768]{1,0:T(8,128)(2,1)S(1)}, bf16[96,768]{1,0:T(8,128)(2,1)}, u32[]{:S(2)}) copy-start(bf16[96,768]{1,0:T(8,128)(2,1)} %param.30) | copy-start | bytes 442372
  1.6 8.2 %collective-permute-start.6 = (bf16[1,24,3840]{2,1,0:T(8,128)(2,1)S(1)}, bf16[1,24,3840]{2,1,0:T(8,128)(2,1)S(1)}, u32[]{:S(2)}, u32[]{:S(2)}) collective-permute-start(bf16[1,24,3840]{2,1,0:T(8,128)(2,1)S(1)} %maximum_bitcast_fusion), channel_id=1, source_target_pairs={{0,2},{1,3},{2,0},{3,1},{4,6},{5,7},{6,4},{7,5},{8,12},{9,13},{10,... | collective-permute-start | bytes 552968 | tf_op jit(solution)/shard_map/ppermute | solution.py:71
  9.8 17.2 %collective-permute-start.7 = (bf16[2,24,3840]{2,1,0:T(8,128)(2,1)S(1)}, bf16[2,24,3840]{2,1,0:T(8,128)(2,1)S(1)}, u32[]{:S(2)}, u32[]{:S(2)}) collective-permute-start(bf16[2,24,3840]{2,1,0:T(8,128)(2,1)S(1)} %pad_maximum_fusion.6), channel_id=1, source_target_pairs={{0,4},{1,5},{2,6},{3,7},{4,0},{5,1},{6,2},{7,3},{8,10},{9,11},{10,... | collective-permute-start | bytes 1105928 | tf_op jit(solution)/shard_map/ppermute | solution.py:71
  13.8 15.8 %collective-permute-start = (bf16[1,24,2432]{2,1,0:T(8,128)(2,1)S(1)}, bf16[1,24,2432]{2,1,0:T(8,128)(2,1)S(1)}, u32[]{:S(2)}, u32[]{:S(2)}) collective-permute-start(bf16[1,24,2432]{2,1,0:T(8,128)(2,1)S(1)} %fusion.5), channel_id=1, source_target_pairs={{0,2},{1,3},{2,0},{3,1},{4,6},{5,7},{6,4},{7,5},{8,12},{9,13},{10,... | collective-permute-start | bytes 350216 | tf_op jit(solution)/shard_map/ppermute | solution.py:71
  16.4 13.3 %collective-permute-start.12 = (bf16[1,96,768]{2,1,0:T(8,128)(2,1)}, bf16[1,96,768]{2,1,0:T(8,128)(2,1)S(1)}, u32[]{:S(2)}, u32[]{:S(2)}) collective-permute-start(bf16[1,96,768]{2,1,0:T(8,128)(2,1)} %bitcast.16), channel_id=1, source_target_pairs={{0,2},{1,3},{2,0},{3,1},{4,6},{5,7},{6,4},{7,5},{8,12},{9,13},{10,... | collective-permute-start | bytes 442376 | tf_op jit(solution)/shard_map/ppermute | solution.py:71
  27.1 18.6 %collective-permute-start.8 = (bf16[4,24,3840]{2,1,0:T(8,128)(2,1)S(1)}, bf16[4,24,3840]{2,1,0:T(8,128)(2,1)S(1)}, u32[]{:S(2)}, u32[]{:S(2)}) collective-permute-start(bf16[4,24,3840]{2,1,0:T(8,128)(2,1)S(1)} %pad_maximum_fusion.3), channel_id=1, source_target_pairs={{0,16},{1,17},{2,18},{3,19},{4,20},{5,21},{6,22},{7,23},{8,9},{9,8... | collective-permute-start | bytes 2211848 | tf_op jit(solution)/shard_map/ppermute | solution.py:71
  29.6 12.7 %collective-permute-start.1 = (bf16[2,24,2432]{2,1,0:T(8,128)(2,1)S(1)}, bf16[2,24,2432]{2,1,0:T(8,128)(2,1)S(1)}, u32[]{:S(2)}, u32[]{:S(2)}) collective-permute-start(bf16[2,24,2432]{2,1,0:T(8,128)(2,1)S(1)} %pad_maximum_fusion.8), channel_id=1, source_target_pairs={{0,4},{1,5},{2,6},{3,7},{4,0},{5,1},{6,2},{7,3},{8,10},{9,11},{10,... | collective-permute-start | bytes 700424 | tf_op jit(solution)/shard_map/ppermute | solution.py:71
  29.7 15.7 %collective-permute-start.13 = (bf16[2,96,768]{2,1,0:T(8,128)(2,1)S(1)}, bf16[2,96,768]{2,1,0:T(8,128)(2,1)S(1)}, u32[]{:S(2)}, u32[]{:S(2)}) collective-permute-start(bf16[2,96,768]{2,1,0:T(8,128)(2,1)S(1)} %pad_maximum_fusion.7), channel_id=1, source_target_pairs={{0,4},{1,5},{2,6},{3,7},{4,0},{5,1},{6,2},{7,3},{8,10},{9,11},{10,... | collective-permute-start | bytes 884744 | tf_op jit(solution)/shard_map/ppermute | solution.py:71
  42.3 13.7 %collective-permute-start.2 = (bf16[4,24,2432]{2,1,0:T(8,128)(2,1)S(1)}, bf16[4,24,2432]{2,1,0:T(8,128)(2,1)S(1)}, u32[]{:S(2)}, u32[]{:S(2)}) collective-permute-start(bf16[4,24,2432]{2,1,0:T(8,128)(2,1)S(1)} %pad_maximum_fusion.5), channel_id=1, source_target_pairs={{0,16},{1,17},{2,18},{3,19},{4,20},{5,21},{6,22},{7,23},{8,9},{9,8... | collective-permute-start | bytes 1400840 | tf_op jit(solution)/shard_map/ppermute | solution.py:71
  45.5 23.2 %collective-permute-start.14 = (bf16[4,96,768]{2,1,0:T(8,128)(2,1)S(1)}, bf16[4,96,768]{2,1,0:T(8,128)(2,1)S(1)}, u32[]{:S(2)}, u32[]{:S(2)}) collective-permute-start(bf16[4,96,768]{2,1,0:T(8,128)(2,1)S(1)} %pad_maximum_fusion.4), channel_id=1, source_target_pairs={{0,16},{1,17},{2,18},{3,19},{4,20},{5,21},{6,22},{7,23},{8,9},{9,8... | collective-permute-start | bytes 1769480 | tf_op jit(solution)/shard_map/ppermute | solution.py:71
  46.9 31.8 %collective-permute-start.9 = (bf16[8,24,3840]{2,1,0:T(8,128)(2,1)}, bf16[8,24,3840]{2,1,0:T(8,128)(2,1)}, u32[]{:S(2)}, u32[]{:S(2)}) collective-permute-start(bf16[8,24,3840]{2,1,0:T(8,128)(2,1)} %pad_maximum_fusion.b0), channel_id=1, source_target_pairs={{0,1},{1,0},{2,3},{3,2},{4,5},{5,4},{6,7},{7,6},{8,24},{9,25},{10,... | collective-permute-start | bytes 4423688 | tf_op jit(solution)/shard_map/ppermute | solution.py:71
  56.2 34.9 %copy-start.16 = (s32[16]{0:T(128)S(1)}, s32[16]{0:T(128)}, u32[]{:S(2)}) copy-start(s32[16]{0:T(128)} %constant.28.clone) | copy-start | bytes 196
  56.2 34.9 %copy-start.17 = (s32[16]{0:T(128)S(1)}, s32[16]{0:T(128)}, u32[]{:S(2)}) copy-start(s32[16]{0:T(128)} %constant.29.clone) | copy-start | bytes 196
  56.2 35.0 %copy-start.1 = (bf16[1024,768]{1,0:T(8,128)(2,1)S(1)}, bf16[1024,768]{1,0:T(8,128)(2,1)}, u32[]{:S(2)}) copy-start(bf16[1024,768]{1,0:T(8,128)(2,1)} %x_ref.5) | copy-start | bytes 4718596
  56.2 35.0 %copy-start.3 = (f32[2,8,768]{2,1,0:T(8,128)S(1)}, f32[2,8,768]{2,1,0:T(8,128)}, u32[]{:S(2)}) copy-start(f32[2,8,768]{2,1,0:T(8,128)} %up_ref.5) | copy-start | bytes 147460
  56.2 35.0 %copy-start.4 = (f32[2,768,8]{1,2,0:T(8,128)S(1)}, f32[2,768,8]{1,2,0:T(8,128)}, u32[]{:S(2)}) copy-start(f32[2,768,8]{1,2,0:T(8,128)} %param.35) | copy-start | bytes 147460
  56.2 20.3 %collective-permute-start.3 = (bf16[8,24,2432]{2,1,0:T(8,128)(2,1)S(1)}, bf16[8,24,2432]{2,1,0:T(8,128)(2,1)S(1)}, u32[]{:S(2)}, u32[]{:S(2)}) collective-permute-start(bf16[8,24,2432]{2,1,0:T(8,128)(2,1)S(1)} %pad_maximum_fusion.2.p0), channel_id=1, source_target_pairs={{0,1},{1,0},{2,3},{3,2},{4,5},{5,4},{6,7},{7,6},{8,24},{9,25},{10,... | collective-permute-start | bytes 2801672 | tf_op jit(solution)/shard_map/ppermute | solution.py:71
  69.8 19.5 %collective-permute-start.15 = (bf16[8,96,768]{2,1,0:T(8,128)(2,1)}, bf16[8,96,768]{2,1,0:T(8,128)(2,1)}, u32[]{:S(2)}, u32[]{:S(2)}) collective-permute-start(bf16[8,96,768]{2,1,0:T(8,128)(2,1)} %pad_maximum_fusion.1.d0), channel_id=1, source_target_pairs={{0,1},{1,0},{2,3},{3,2},{4,5},{5,4},{6,7},{7,6},{8,24},{9,25},{10,... | collective-permute-start | bytes 3538952 | tf_op jit(solution)/shard_map/ppermute | solution.py:71
  71.3 7.9 %collective-permute-start.4 = (bf16[8,24,2432]{2,1,0:T(8,128)(2,1)S(1)}, bf16[8,24,2432]{2,1,0:T(8,128)(2,1)}, u32[]{:S(2)}, u32[]{:S(2)}) collective-permute-start(bf16[8,24,2432]{2,1,0:T(8,128)(2,1)S(1)} %pad_maximum_fusion.2.p0), channel_id=1, source_target_pairs={{0,8},{1,9},{2,10},{3,11},{4,12},{5,13},{6,14},{7,15},{8,0},{9,1},... | collective-permute-start | bytes 2801672 | tf_op jit(solution)/shard_map/ppermute | solution.py:77
  76.5 14.7 %collective-permute-start.5 = (bf16[8,24,2432]{2,1,0:T(8,128)(2,1)S(1)}, bf16[8,24,2432]{2,1,0:T(8,128)(2,1)}, u32[]{:S(2)}, u32[]{:S(2)}) collective-permute-start(bf16[8,24,2432]{2,1,0:T(8,128)(2,1)S(1)} %collective-permute-done.3.p1), channel_id=1, source_target_pairs={{0,8},{1,9},{2,10},{3,11},{4,12},{5,13},{6,14},{7,15},{8,0},{9,1},... | collective-permute-start | bytes 2801672 | tf_op jit(solution)/shard_map/ppermute | solution.py:78
  78.7 42.6 %collective-permute-start.10 = (bf16[8,24,3840]{2,1,0:T(8,128)(2,1)}, bf16[8,24,3840]{2,1,0:T(8,128)(2,1)}, u32[]{:S(2)}, u32[]{:S(2)}) collective-permute-start(bf16[8,24,3840]{2,1,0:T(8,128)(2,1)} %pad_maximum_fusion.b0), channel_id=1, source_target_pairs={{0,8},{1,9},{2,10},{3,11},{4,12},{5,13},{6,14},{7,15},{8,0},{9,1},... | collective-permute-start | bytes 4423688 | tf_op jit(solution)/shard_map/ppermute | solution.py:77
  78.7 42.7 %collective-permute-start.11 = (bf16[8,24,3840]{2,1,0:T(8,128)(2,1)}, bf16[8,24,3840]{2,1,0:T(8,128)(2,1)}, u32[]{:S(2)}, u32[]{:S(2)}) collective-permute-start(bf16[8,24,3840]{2,1,0:T(8,128)(2,1)} %collective-permute-done.9.b1), channel_id=1, source_target_pairs={{0,8},{1,9},{2,10},{3,11},{4,12},{5,13},{6,14},{7,15},{8,0},{9,1},... | collective-permute-start | bytes 4423688 | tf_op jit(solution)/shard_map/ppermute | solution.py:78
  79.3 42.1 %collective-permute-start.16 = (bf16[8,96,768]{2,1,0:T(8,128)(2,1)}, bf16[8,96,768]{2,1,0:T(8,128)(2,1)S(1)}, u32[]{:S(2)}, u32[]{:S(2)}) collective-permute-start(bf16[8,96,768]{2,1,0:T(8,128)(2,1)} %pad_maximum_fusion.1.d0), channel_id=1, source_target_pairs={{0,8},{1,9},{2,10},{3,11},{4,12},{5,13},{6,14},{7,15},{8,0},{9,1},... | collective-permute-start | bytes 3538952 | tf_op jit(solution)/shard_map/ppermute | solution.py:77
  89.3 32.1 %collective-permute-start.17 = (bf16[8,96,768]{2,1,0:T(8,128)(2,1)}, bf16[8,96,768]{2,1,0:T(8,128)(2,1)S(1)}, u32[]{:S(2)}, u32[]{:S(2)}) collective-permute-start(bf16[8,96,768]{2,1,0:T(8,128)(2,1)} %collective-permute-done.15.d1), channel_id=1, source_target_pairs={{0,8},{1,9},{2,10},{3,11},{4,12},{5,13},{6,14},{7,15},{8,0},{9,1},... | collective-permute-start | bytes 3538952 | tf_op jit(solution)/shard_map/ppermute | solution.py:78
  91.2 12.0 %copy-start.7 = (s32[32]{0:T(128)}, s32[32]{0:T(128)S(1)}, u32[]{:S(2)}) copy-start(s32[32]{0:T(128)S(1)} %pad_add_fusion.ids_ref) | copy-start | bytes 388
  91.2 12.0 %copy-start.6 = (s32[2,512]{1,0:T(2,128)S(1)}, s32[2,512]{1,0:T(2,128)}, u32[]{:S(2)}) copy-start(s32[2,512]{1,0:T(2,128)} %seg_ref.1) | copy-start | bytes 12292
  103.1 17.1 %copy-start.8 = (bf16[1024,2304]{1,0:T(8,128)(2,1)}, bf16[1024,2304]{1,0:T(8,128)(2,1)S(1)}, u32[]{:S(2)}) copy-start(bf16[1024,2304]{1,0:T(8,128)(2,1)S(1)} %get-tuple-element.38.q_ref.k_ref.v_ref) | copy-start | bytes 14155780
  103.1 17.1 %copy-start.13 = (f32[8,3072]{1,0:T(8,128)}, f32[8,3072]{1,0:T(8,128)S(1)}, u32[]{:S(2)}) copy-start(f32[8,3072]{1,0:T(8,128)S(1)} %get-tuple-element.41.inner_bias_ref) | copy-start | bytes 294916
  103.2 17.1 %copy-start.14 = (f32[8,768]{1,0:T(8,128)}, f32[8,768]{1,0:T(8,128)S(1)}, u32[]{:S(2)}) copy-start(f32[8,768]{1,0:T(8,128)S(1)} %get-tuple-element.40.small_ref) | copy-start | bytes 73732
  120.2 1.2 copy-start.10
  121.4 1.1 copy-start.18
  121.4 1.4 copy-start.19
  122.8 44.0 %copy-start.11 = (bf16[1024,768]{1,0:T(8,128)(2,1)S(1)}, bf16[1024,768]{1,0:T(8,128)(2,1)}, u32[]{:S(2)}) copy-start(bf16[1024,768]{1,0:T(8,128)(2,1)} %copy-done.10) | copy-start | bytes 4718596
  166.8 2.3 %copy-start.9 = (bf16[1024,2304]{1,0:T(8,128)(2,1)S(1)}, bf16[1024,2304]{1,0:T(8,128)(2,1)}, u32[]{:S(2)}) copy-start(bf16[1024,2304]{1,0:T(8,128)(2,1)} %copy-done.8) | copy-start | bytes 14155780
  169.1 1.4 copy-start.12
  170.5 16.8 %copy-start.2 = (bf16[1024,768]{1,0:T(8,128)(2,1)S(1)}, bf16[1024,768]{1,0:T(8,128)(2,1)}, u32[]{:S(2)}) copy-start(bf16[1024,768]{1,0:T(8,128)(2,1)} %x_ref.5) | copy-start | bytes 4718596
  170.5 16.8 %copy-start.5 = (f32[8,768]{1,0:T(8,128)S(1)}, f32[8,768]{1,0:T(8,128)}, u32[]{:S(2)}) copy-start(f32[8,768]{1,0:T(8,128)} %get-tuple-element.50.sums_ref) | copy-start | bytes 73732
  187.3 23.6 %copy-start = (f32[1024,768]{1,0:T(8,128)S(1)}, f32[1024,768]{1,0:T(8,128)}, u32[]{:S(2)}) copy-start(f32[1024,768]{1,0:T(8,128)} %get-tuple-element.43.mid_ref) | copy-start | bytes 9437188
  189.6 1.4 collective-permute-start.18
  191.1 5.5 %collective-permute-start.19 = (f32[40,768]{1,0:T(8,128)S(1)}, f32[40,768]{1,0:T(8,128)S(1)}, u32[]{:S(2)}, u32[]{:S(2)}) collective-permute-start(f32[40,768]{1,0:T(8,128)S(1)} %add.23), channel_id=1, source_target_pairs={{0,1},{1,0},{2,3},{3,2},{4,5},{5,4},{6,7},{7,6},{8,9},{9,8},{10,11... | collective-permute-start | bytes 368648 | tf_op jit(solution)/shard_map/ppermute | solution.py:671
  196.6 4.9 %collective-permute-start.20 = (f32[40,768]{1,0:T(8,128)S(1)}, f32[40,768]{1,0:T(8,128)S(1)}, u32[]{:S(2)}, u32[]{:S(2)}) collective-permute-start(f32[40,768]{1,0:T(8,128)S(1)} %add.24), channel_id=1, source_target_pairs={{0,2},{1,3},{2,0},{3,1},{4,6},{5,7},{6,4},{7,5},{8,10},{9,11},{10,... | collective-permute-start | bytes 368648 | tf_op jit(solution)/shard_map/ppermute | solution.py:671
  201.6 7.2 %collective-permute-start.21 = (f32[40,768]{1,0:T(8,128)S(1)}, f32[40,768]{1,0:T(8,128)S(1)}, u32[]{:S(2)}, u32[]{:S(2)}) collective-permute-start(f32[40,768]{1,0:T(8,128)S(1)} %add.25), channel_id=1, source_target_pairs={{0,4},{1,5},{2,6},{3,7},{4,0},{5,1},{6,2},{7,3},{8,12},{9,13},{10,... | collective-permute-start | bytes 368648 | tf_op jit(solution)/shard_map/ppermute | solution.py:671
  208.8 7.9 %collective-permute-start.22 = (f32[40,768]{1,0:T(8,128)S(1)}, f32[40,768]{1,0:T(8,128)S(1)}, u32[]{:S(2)}, u32[]{:S(2)}) collective-permute-start(f32[40,768]{1,0:T(8,128)S(1)} %add.26), channel_id=1, source_target_pairs={{0,16},{1,17},{2,18},{3,19},{4,20},{5,21},{6,22},{7,23},{8,24},{9,... | collective-permute-start | bytes 368648 | tf_op jit(solution)/shard_map/ppermute | solution.py:671

commit v2 on v1

--- a/solution.py
+++ b/solution.py
@@ -10,6 +10,7 @@
 from jax.sharding import PartitionSpec as P
 
 HEAD = 64
+OUTER_ROWS = 64
 AXES = ("dp", "fsdp")
 
 beta_one = 0.9
@@ -19,9 +20,12 @@
 up_decay_factor = 0.01
 norm_epsilon = 1e-05
 masked_score = -1e30
+root_half = math.sqrt(0.5)
 root_circle = 1.0 / math.sqrt(2.0 * math.pi)
+half_log = -0.5 * math.log2(math.e)
 LANES = 128
 MIB = 1 << 20
+VMEM_LIMIT = 60 * MIB
 
 f32 = jnp.float32
 bf16 = jnp.bfloat16
@@ -45,14 +49,15 @@
         y_bits = [1 << t for t in range(int(math.log2(n_y)))]
         z_bits = [n_y << t for t in range(int(math.log2(n_fsdp // n_y)))]
         x_bits = [(2 * n_fsdp) << t for t in range(int(math.log2(n_x)))]
-        self.orders = (z_bits + x_bits + y_bits, z_bits[::-1] + y_bits + x_bits)
-        self.bits = y_bits + z_bits + x_bits + [self.core]
-
-    def order_of(self, i):
-        return self.orders[1 if i & self.core else 0]
-
-    def stage_pairs(self, t):
-        return [(i, i ^ self.order_of(i)[t]) for i in range(self.n)]
+        self.z_first = (z_bits + x_bits + y_bits, z_bits[::-1] + y_bits + x_bits)
+        self.z_last = (x_bits + y_bits + z_bits, y_bits + x_bits + z_bits[::-1])
+        self.x_bits, self.y_bits, self.z_bits = x_bits, y_bits, z_bits
+
+    def stage_pairs(self, orders, t):
+        return [(i, i ^ orders[1 if i & self.core else 0][t]) for i in range(self.n)]
+
+    def pairs(self, bits):
+        return [(i, i ^ bits) for i in range(self.n)]
 
     def core_pairs(self):
         return [(i, i ^ self.core) for i in range(self.n)]
@@ -64,28 +69,45 @@
         return masks
 
 
-def gather_blocks(block, layout):
-    held = block[None]
-    stages = len(layout.orders[0])
-    for t in range(stages):
-        came = lax.ppermute(held, AXES, layout.stage_pairs(t))
-        if t < stages - 1:
-            held = jnp.concatenate([held, came], axis=0)
-    return (
-        held,
-        came,
-        lax.ppermute(held, AXES, layout.core_pairs()),
-        lax.ppermute(came, AXES, layout.core_pairs()),
-    )
-
-
-def block_ids(layout):
+def after(value, *others):
+    return lax.optimization_barrier((value,) + others)[0]
+
+
+def together(*values):
+    return lax.optimization_barrier(values)
+
+
+def stage(held, layout, orders, t):
+    return lax.ppermute(held, AXES, layout.stage_pairs(orders, t))
+
+
+def swap_cores(value, layout):
+    return lax.ppermute(value, AXES, layout.core_pairs())
+
+
+def join(held, came):
+    return jnp.concatenate([held, came], axis=0)
+
+
+def block_ids(layout, orders):
     me = lax.axis_index(AXES).astype(jnp.int32)
-    one, two = (np.array(layout.block_masks(o), np.int32) for o in layout.orders)
+    one, two = (np.array(layout.block_masks(o), np.int32) for o in orders)
     second = (me & layout.core) != 0
     own = me ^ jnp.where(second, two, one)
     other = me ^ layout.core ^ jnp.where(second, one, two)
     return jnp.concatenate([own, other])
+
+
+def exchange(total, layout, kinds, beside=None):
+    combos = [0]
+    for bit in kinds:
+        combos = combos + [c ^ bit for c in combos]
+    parts = [total] + [lax.ppermute(total, AXES, layout.pairs(c)) for c in combos[1:]]
+    if beside is not None:
+        *parts, beside = together(*parts, beside())
+    while len(parts) > 1:
+        parts = [one + two for one, two in zip(parts[::2], parts[1::2])]
+    return parts[0] if beside is None else (parts[0], beside)
 
 
 def as_blocks(full, count):
@@ -134,8 +156,8 @@
     return total
 
 
-def project_kernel(ids_ref, x_ref, down_ref, up_ref, p0, p1, p2, p3, qkv_ref, weight_ref, red_ref,
-                   small_ref, inner_bias_ref, stage, sems):
+def project_kernel(ids_ref, x_ref, down_ref, up_ref, p0, p1, p2, p3, qkv_ref, weight_hbm, red_ref,
+                   small_ref, inner_bias_ref, stage, weight_ref, sems, sem_w):
     parts = (p0, p1, p2, p3)
     width = x_ref.shape[1]
     rank = down_ref.shape[1]
@@ -144,6 +166,7 @@
     def _():
         fetch_blocks(ids_ref, parts, stage, sems)
         merge_pairs(parts, stage, sems, weight_ref, 3 * width)
+        pltpu.make_async_copy(weight_ref, weight_hbm, sem_w).start()
         shards, rows = stage.shape[0], stage.shape[1]
         tail = stage[:, :, 3 * width :].astype(f32)
         small_ref[...] = spread(tail[:, 0:8].reshape(8 * shards, LANES), width, rows, shards)
@@ -169,6 +192,10 @@
         elif c >= 2 * width:
             y = y + small_ref[1:2, o : o + chunk] + nn(reduced, up_value[:, o : o + chunk])
         qkv_ref[:, c : c + chunk] = y.astype(bf16)
+
+    @pl.when(pl.program_id(0) == pl.num_programs(0) - 1)
+    def _():
+        pltpu.make_async_copy(weight_ref, weight_hbm, sem_w).wait()
 
 
 def project(ids, tokens, down, up, parts):
@@ -190,7 +217,7 @@
         + [pl.BlockSpec(memory_space=pl.ANY)] * 4,
         out_specs=[
             pl.BlockSpec((tile, 3 * width), lambda i: (i, 0)),
-            whole(width, 3 * width),
+            pl.BlockSpec(memory_space=pl.ANY),
             pl.BlockSpec((2 * down.shape[1], tile), lambda i: (0, i)),
             whole(8, width),
             whole(8, ff),
@@ -204,21 +231,24 @@
         ],
         scratch_shapes=[
             pltpu.VMEM((shards, shard_rows, 3 * width + LANES), bf16),
+            pltpu.VMEM((width, 3 * width), bf16),
             pltpu.SemaphoreType.DMA((shards,)),
-        ],
-        compiler_params=pltpu.CompilerParams(vmem_limit_bytes=40 * MIB),
+            pltpu.SemaphoreType.DMA(()),
+        ],
+        compiler_params=pltpu.CompilerParams(vmem_limit_bytes=VMEM_LIMIT),
         cost_estimate=pl.CostEstimate(
             flops=2 * rows * width * width * 3, bytes_accessed=14 * MIB, transcendentals=0
         ),
     )(ids, tokens, down, up, *parts)
 
 
-def attend_kernel(seg_ref, q_ref, k_ref, v_ref, ctx_ref, w_ref, mask):
-    pack, rows = seg_ref.shape[1], seg_ref.shape[1]
-
-    @pl.when(pl.program_id(1) == 0)
+def attend_kernel(pack, seg_ref, q_ref, k_ref, v_ref, *rest):
+    ctx_ref, w_ref, mask = rest[-3:]
+    rows = seg_ref.shape[1]
+
+    @pl.when(pl.program_id(0) == 0)
     def _():
-        row = jnp.broadcast_to(seg_ref[pl.ds(pl.program_id(0), 1), :].astype(f32), (8, rows))
+        row = jnp.broadcast_to(seg_ref[pack : pack + 1, :].astype(f32), (8, rows))
         column = row.T[:, 0:1]
         mask[...] = jnp.where(column == row[0:1], 0.0, masked_score)
 
@@ -245,31 +275,32 @@
 HEADS_A_STEP = 4
 
 
-def attend(segments, qkv):
+def attend(pack, segments, qkv, before=()):
     packs, length = segments.shape
-    rows, wide = qkv.shape
-    width = wide // 3
+    width = qkv.shape[1] // 3
     step = HEADS_A_STEP * HEAD
     steps = width // step
-    at = lambda which: pl.BlockSpec((length, step), lambda p, s: (p, which * steps + s))
+    at = lambda which: pl.BlockSpec((length, step), lambda s: (pack, which * steps + s))
     return pl.pallas_call(
-        attend_kernel,
-        grid=(packs, steps),
-        in_specs=[pl.BlockSpec((packs, length), lambda p, s: (0, 0)), at(0), at(1), at(2)],
+        functools.partial(attend_kernel, pack),
+        grid=(steps,),
+        in_specs=[pl.BlockSpec((packs, length), lambda s: (0, 0)), at(0), at(1), at(2)]
+        + [pl.BlockSpec(memory_space=pl.ANY)] * len(before),
         out_specs=[
-            pl.BlockSpec((length, step), lambda p, s: (p, s)),
-            pl.BlockSpec((HEADS_A_STEP, length, length), lambda p, s: (p * steps + s, 0, 0)),
+            pl.BlockSpec((length, step), lambda s: (pack, s)),
+            pl.BlockSpec((HEADS_A_STEP, length, length), lambda s: (pack * steps + s, 0, 0)),
         ],
         out_shape=[
-            jax.ShapeDtypeStruct((rows, width), bf16),
+            jax.ShapeDtypeStruct((packs * length, width), bf16),
             jax.ShapeDtypeStruct((packs * width // HEAD, length, length), bf16),
         ],
+        input_output_aliases={4 + i: i for i in range(len(before))},
         scratch_shapes=[pltpu.VMEM((length, length), f32)],
-        compiler_params=pltpu.CompilerParams(vmem_limit_bytes=40 * MIB),
+        compiler_params=pltpu.CompilerParams(vmem_limit_bytes=VMEM_LIMIT),
         cost_estimate=pl.CostEstimate(
-            flops=16 * rows * length * width, bytes_accessed=20 * MIB, transcendentals=rows * length * 12
+            flops=16 * length * length * width, bytes_accessed=10 * MIB, transcendentals=0
         ),
-    )(segments, qkv, qkv, qkv)
+    )(segments, qkv, qkv, qkv, *before)
 
 
 def stats(value):
@@ -288,36 +319,29 @@
 
 
 def gelu_parts(z):
-    size = jnp.abs(z)
-    t = 1.0 / (1.0 + 0.2316419 * size)
-    density = jnp.exp(z * z * -0.5) * root_circle
-    poly = t * (
-        0.319381530
-        + t * (-0.356563782 + t * (1.781477937 + t * (-1.821255978 + t * 1.330274429)))
-    )
-    tail = density * poly
-    cumulative = jnp.where(z >= 0.0, 1.0 - tail, tail)
+    cumulative = 0.5 + 0.5 * lax.erf(z * root_half)
+    density = jnp.exp2(z * z * half_log) * root_circle
     return z * cumulative, cumulative + z * density
 
 
-def rows_kernel(ids_ref, x_ref, cot_ref, ctx_ref, small_ref, inner_bias_ref, b0, b1, b2, b3, d0, d1, d2, d3,
+def rows_kernel(ids_ref, ids_d_ref, x_ref, cot_ref, ctx_ref, small_ref, inner_bias_ref,
+                b0, b1, b2, b3, d0, d1, d2, d3,
                 act_ref, mid_ref, dctx_ref, sums_ref,
                 stage, wo, wi, wf, active, slope, sem_b, sem_d):
     parts_b, parts_d = (b0, b1, b2, b3), (d0, d1, d2, d3)
     width = x_ref.shape[1]
+    taken = d0.shape[1]
     ff = wi.shape[1]
-    shard = d0.shape[1]
+    shard = ff // stage.shape[0]
 
     @pl.when(pl.program_id(0) == 0)
     def _():
         fetch_blocks(ids_ref, parts_b, stage, sem_b)
-        each = d0.shape[0]
         for a, part in enumerate(parts_d):
-            for j in range(each):
-                at = ids_ref[a * each + j]
-                pltpu.make_async_copy(
-                    part.at[j], wf.at[pl.ds(pl.multiple_of(at * shard, shard), shard)], sem_d.at[at]
-                ).start()
+            for j in range(part.shape[0]):
+                at = ids_d_ref[a * part.shape[0] + j]
+                place = wf.at[pl.ds(pl.multiple_of(at * shard, shard), taken)]
+                pltpu.make_async_copy(part.at[j], place, sem_d.at[at]).start()
         shards, rows = stage.shape[0], stage.shape[1]
         for i in range(0, shards, 2):
             wait_block(parts_b, stage, sem_b, i)
@@ -335,8 +359,15 @@
                     wo[where] = both
                 else:
                     wi[where, c - width : c] = both
+            for k in (i, i + 1):
+                more = stage[k, :, width + ff :].astype(f32)
+                third = more[:, width:]
+                eight = [third[8 * n : 8 * (n + 1)] for n in range(3)]
+                wf[k * shard + taken : (k + 1) * shard] = jnp.concatenate(
+                    [more[:, :width], jnp.concatenate(eight, axis=1)], axis=0
+                ).astype(bf16)
         for i in range(shards):
-            pltpu.make_async_copy(d0.at[0], wf.at[pl.ds(i * shard, shard)], sem_d.at[i]).wait()
+            pltpu.make_async_copy(d0.at[0], wf.at[pl.ds(i * shard, taken)], sem_d.at[i]).wait()
         sums_ref[...] = jnp.zeros_like(sums_ref)
 
     bias_out, bias_ff = small_ref[2:3], small_ref[3:4]
@@ -376,7 +407,7 @@
     dctx_ref[...] = nt(grad_mid.astype(bf16), wo[...]).astype(bf16)
 
 
-def row_local(ids, tokens, cotangent, context, small, inner_bias, parts_b, parts_d):
+def row_local(ids, ids_d, tokens, cotangent, context, small, inner_bias, parts_b, parts_d):
     rows, width = tokens.shape
     ff = inner_bias.shape[1]
     shards = 4 * parts_b[0].shape[0]
@@ -386,7 +417,15 @@
     return pl.pallas_call(
         rows_kernel,
         grid=(rows // tile,),
-        in_specs=[pl.BlockSpec(memory_space=pltpu.SMEM), tiled, tiled, tiled, whole(8, width), whole(8, ff)]
+        in_specs=[
+            pl.BlockSpec(memory_space=pltpu.SMEM),
+            pl.BlockSpec(memory_space=pltpu.SMEM),
+            tiled,
+            tiled,
+            tiled,
+            whole(8, width),
+            whole(8, ff),
+        ]
         + [pl.BlockSpec(memory_space=pl.ANY)] * 8,
         out_specs=[tiled, tiled, tiled, whole(8, width)],
         out_shape=[
@@ -405,15 +444,29 @@
             pltpu.SemaphoreType.DMA((shards,)),
             pltpu.SemaphoreType.DMA((shards,)),
         ],
-        compiler_params=pltpu.CompilerParams(vmem_limit_bytes=56 * MIB),
+        compiler_params=pltpu.CompilerParams(vmem_limit_bytes=VMEM_LIMIT),
         cost_estimate=pl.CostEstimate(
             flops=2 * rows * width * (4 * ff + 2 * width), bytes_accessed=20 * MIB, transcendentals=0
         ),
-    )(ids, tokens, cotangent, context, small, inner_bias, *parts_b, *parts_d)
-
-
-def attend_back_kernel(q_ref, k_ref, v_ref, ctx_ref, dctx_ref, w_ref, dq_ref, dk_ref, dv_ref):
+    )(ids, ids_d, tokens, cotangent, context, small, inner_bias, *parts_b, *parts_d)
+
+
+def attend_back_kernel(core_ref, x_ref, q_ref, k_ref, v_ref, ctx_ref, dctx_ref, w_ref, up_ref, red_ref,
+                       sums_ref, dq_ref, dk_ref, dv_ref, dred_ref, keep_ref, send_ref, dred, grads):
     scale = HEAD**-0.5
+    pack, step = pl.program_id(0), pl.program_id(1)
+    rank = red_ref.shape[0] // 2
+
+    @pl.when((pack == 0) & (step == 0))
+    def _():
+        grads[...] = jnp.zeros_like(grads)
+        keep_ref[...] = jnp.zeros_like(keep_ref)
+        send_ref[...] = jnp.zeros_like(send_ref)
+
+    @pl.when(step == 0)
+    def _():
+        dred[...] = jnp.zeros_like(dred)
+
     lane = lax.broadcasted_iota(jnp.int32, (1, LANES), 1)
     for s in range(q_ref.shape[1] // LANES):
         cols = slice(s * LANES, (s + 1) * LANES)
@@ -439,76 +492,81 @@
         dq_ref[:, cols] = (dq * scale).astype(bf16)
         dk_ref[:, cols] = (jnp.concatenate(dk_t, axis=0) * scale).T.astype(bf16)
         dv_ref[:, cols] = jnp.concatenate(dv_t, axis=0).T.astype(bf16)
-
-
-def attend_back(qkv, context, grad_context, weights):
+    red = red_ref[...]
+    up = (2.0 * up_ref[...].astype(bf16).astype(f32)).astype(bf16)
+    none = jnp.zeros_like(up[0])
+    dq, dv = dq_ref[...], dv_ref[...]
+    dred[...] += nt(jnp.concatenate([up[0], none], axis=0), dq) + nt(jnp.concatenate([none, up[1]], axis=0), dv)
+    grads[step, 0:rank] += 2.0 * nn(red, dq)[0:rank]
+    grads[step, rank : 2 * rank] += 2.0 * nn(red, dv)[rank : 2 * rank]
+
+    @pl.when(step == pl.num_programs(1) - 1)
+    def _():
+        rounded = dred[...].astype(bf16)
+        dred_ref[...] = rounded
+        down = nn(rounded, x_ref[...])
+        raised = jnp.concatenate([grads[i] for i in range(grads.shape[0])], axis=1)
+        half = down.shape[1] // 2
+        low = (core_ref[0] == 0).astype(f32)
+        for out, left in ((keep_ref, low), (send_ref, 1.0 - low)):
+            pick = lambda a: jnp.where(left > 0.5, a[:, :half], a[:, half:])
+            out[0 : 2 * rank] += pick(down)
+            out[2 * rank : 4 * rank] = pick(raised)
+            out[4 * rank : 5 * rank] = pick(sums_ref[...])
+
+
+def attend_back(core, tokens, qkv, context, grad_context, weights, up, red, sums):
     rows, width = context.shape
     length = weights.shape[1]
-    packs = rows // length
+    rank = up.shape[1]
     step = HEADS_A_STEP * HEAD
     steps = width // step
     at = lambda which: pl.BlockSpec((length, step), lambda p, s: (p, which * steps + s))
-    flat = pl.BlockSpec((length, step), lambda p, s: (p, s))
+    own = pl.BlockSpec((length, step), lambda p, s: (p, s))
+    whole = lambda *shape: pl.BlockSpec(shape, lambda p, s: (0,) * len(shape))
+    along = pl.BlockSpec((2 * rank, length), lambda p, s: (0, p))
     return pl.pallas_call(
         attend_back_kernel,
-        grid=(packs, steps),
+        grid=(rows // length, steps),
         in_specs=[
+            pl.BlockSpec(memory_space=pltpu.SMEM),
+            pl.BlockSpec((length, width), lambda p, s: (p, 0)),
             at(0),
             at(1),
             at(2),
-            flat,
-            flat,
+            own,
+            own,
             pl.BlockSpec((HEADS_A_STEP, length, length), lambda p, s: (p * steps + s, 0, 0)),
-        ],
-        out_specs=[flat] * 3,
-        out_shape=[jax.ShapeDtypeStruct((rows, width), bf16)] * 3,
-        compiler_params=pltpu.CompilerParams(vmem_limit_bytes=40 * MIB),
+            pl.BlockSpec((2, rank, step), lambda p, s: (0, 0, s)),
+            along,
+            whole(*sums.shape),
+        ],
+        out_specs=[own, own, own, along, whole(5 * rank, width // 2), whole(5 * rank, width // 2)],
+        out_shape=[jax.ShapeDtypeStruct((rows, width), bf16)] * 3
+        + [
+            jax.ShapeDtypeStruct((2 * rank, rows), bf16),
+            jax.ShapeDtypeStruct((5 * rank, width // 2), f32),
+            jax.ShapeDtypeStruct((5 * rank, width // 2), f32),
+        ],
+        scratch_shapes=[pltpu.VMEM((2 * rank, length), f32), pltpu.VMEM((steps, 2 * rank, step), f32)],
+        compiler_params=pltpu.CompilerParams(vmem_limit_bytes=VMEM_LIMIT),
         cost_estimate=pl.CostEstimate(
-            flops=32 * rows * length * width, bytes_accessed=24 * MIB, transcendentals=0
+            flops=32 * rows * length * width, bytes_accessed=28 * MIB, transcendentals=0
         ),
-    )(qkv, qkv, qkv, context, grad_context, weights)
-
-
-def adapter_kernel(x_ref, dq_ref, dv_ref, up_ref, red_ref, sums_ref, dred_ref, grads_ref):
-    rank = up_ref.shape[1]
-    up = (2.0 * up_ref[...].astype(bf16).astype(f32)).astype(bf16)
-    dq, dv = dq_ref[...], dv_ref[...]
-    zero = jnp.zeros_like(up[0])
-    up_query = jnp.concatenate([up[0], zero], axis=0)
-    up_value = jnp.concatenate([zero, up[1]], axis=0)
-    dred_ref[...] = (nt(dq, up_query) + nt(dv, up_value)).astype(bf16)
-    dred_t = (nt(up_query, dq) + nt(up_value, dv)).astype(bf16)
-    red = red_ref[...]
-    grads_ref[0 : 2 * rank] = nn(dred_t, x_ref[...])
-    grads_ref[2 * rank : 3 * rank] = 2.0 * nn(red, dq)[0:rank]
-    grads_ref[3 * rank : 4 * rank] = 2.0 * nn(red, dv)[rank : 2 * rank]
-    grads_ref[4 * rank : 5 * rank] = sums_ref[...]
-
-
-def adapter_grads(tokens, dq, dv, up, red, sums):
-    rows, width = tokens.shape
-    rank = up.shape[1]
-    return pl.pallas_call(
-        adapter_kernel,
-        out_shape=[
-            jax.ShapeDtypeStruct((rows, 2 * rank), bf16),
-            jax.ShapeDtypeStruct((5 * rank, width), f32),
-        ],
-        compiler_params=pltpu.CompilerParams(vmem_limit_bytes=24 * MIB),
-        cost_estimate=pl.CostEstimate(flops=1 << 27, bytes_accessed=5 * MIB, transcendentals=0),
-    )(tokens, dq, dv, up, red, sums)
+    )(core, tokens, qkv, qkv, qkv, context, grad_context, weights, up, red, sums)
 
 
 def input_kernel(mid_ref, dq_ref, dk_ref, dv_ref, dred_ref, down_ref, w_ref, out_ref):
     width = mid_ref.shape[1]
     rank = down_ref.shape[1]
     down = down_ref[...].reshape(2 * rank, width).astype(bf16)
+    low = lax.dot_general(dred_ref[...], down, (((0,), (0,)), ((), ())), preferred_element_type=f32)
     out_ref[...] = (
         mid_ref[...]
+        + low
         + nt(dq_ref[...], w_ref[:, 0:width])
         + nt(dk_ref[...], w_ref[:, width : 2 * width])
         + nt(dv_ref[...], w_ref[:, 2 * width : 3 * width])
-        + nn(dred_ref[...], down)
     )
 
 
@@ -525,20 +583,20 @@
             tiled,
             tiled,
             tiled,
-            pl.BlockSpec((tile, dred.shape[1]), lambda i: (i, 0)),
+            pl.BlockSpec((dred.shape[0], tile), lambda i: (0, i)),
             whole(*down.shape),
             whole(*weight.shape),
         ],
         out_specs=tiled,
         out_shape=jax.ShapeDtypeStruct((rows, width), f32),
-        compiler_params=pltpu.CompilerParams(vmem_limit_bytes=40 * MIB),
+        compiler_params=pltpu.CompilerParams(vmem_limit_bytes=VMEM_LIMIT),
         cost_estimate=pl.CostEstimate(
             flops=6 * rows * width * width, bytes_accessed=15 * MIB, transcendentals=0
         ),
     )(mid, dq, dk, dv, dred, down, weight)
 
 
-def adamw_kernel(count, scal_ref, total_ref, down_ref, up_ref, dm_ref, dv_ref, um_ref, uv_ref,
+def adamw_kernel(count, scal_ref, core_ref, mine_ref, other_ref, down_ref, up_ref, dm_ref, dv_ref, um_ref, uv_ref,
                  gd_ref, gu_ref, gain_ref, shift_ref, pd_ref, pu_ref, dm2_ref, dv2_ref, um2_ref, uv2_ref):
     rank = up_ref.shape[1]
     width = up_ref.shape[2]
@@ -553,7 +611,9 @@
         new = param - learn * (first_hat / (jnp.sqrt(second_hat) + adam_epsilon) + decay * param)
         return new, first_new, second_new
 
-    total = total_ref[...] * part
+    mine, other = mine_ref[...] * part, other_ref[...] * part
+    low = core_ref[0] == 0
+    total = jnp.concatenate([jnp.where(low, mine, other), jnp.where(low, other, mine)], axis=1)
     grad_down = total[0 : 2 * rank].reshape(2, rank, width)
     grad_up = total[2 * rank : 4 * rank].reshape(2, rank, width)
     gd_ref[...] = grad_down
@@ -568,16 +628,17 @@
     )
 
 
-def adamw(count, scalars, total, down, up, dm, dv, um, uv):
-    width = total.shape[1]
+def adamw(count, scalars, core, mine, other, down, up, dm, dv, um, uv):
+    width = up.shape[2]
     like = jax.ShapeDtypeStruct(up.shape, f32)
     pair = jax.ShapeDtypeStruct((2, width), f32)
     vmem = pl.BlockSpec(memory_space=pltpu.VMEM)
+    smem = pl.BlockSpec(memory_space=pltpu.SMEM)
     return pl.pallas_call(
         functools.partial(adamw_kernel, count),
-        in_specs=[pl.BlockSpec(memory_space=pltpu.SMEM)] + [vmem] * 7,
+        in_specs=[smem, smem] + [vmem] * 8,
         out_shape=[like, like, pair, pair] + [like] * 6,
-    )(scalars, total, down, up, dm, dv, um, uv)
+    )(scalars, core, mine, other, down, up, dm, dv, um, uv)
 
 
 def per_device(
@@ -615,7 +676,8 @@
         axis=0,
     )
     inner_bias = feedforward_inner_bias[None]
-    if shard % 8 == 0 and shard * layout.n == width and layout.n == 32:
+    fast = shard % 8 == 0 and shard * layout.n == width and layout.n == 32
+    if fast:
         tail = jnp.concatenate(
             [
                 jnp.pad(small, ((0, 0), (0, LANES - shard))),
@@ -624,11 +686,35 @@
             axis=0,
         )
         block_a = jnp.concatenate([query_weight, key_weight, value_weight, tail], axis=1)
-        block_b = jnp.concatenate([output_weight, inner_weight], axis=1)
-        parts_a = gather_blocks(block_a, layout)
-        parts_b = gather_blocks(block_b, layout)
-        parts_d = gather_blocks(outer_weight, layout)
-        ids = block_ids(layout)
+        extra = outer_weight[OUTER_ROWS:]
+        third = extra[shard:].reshape(8, 3, width // 3)
+        third = jnp.swapaxes(third, 0, 1).reshape(shard, width // 3)
+        block_b = jnp.concatenate([output_weight, inner_weight, extra[:shard], third], axis=1)
+        zf, zl = layout.z_first, layout.z_last
+        ids = block_ids(layout, zf)
+        ids_d = block_ids(layout, zl)
+        a, b, d = block_a[None], block_b[None], outer_weight[None, :OUTER_ROWS]
+        a1 = stage(a, layout, zf, 0)
+        d1 = stage(d, layout, zl, 0)
+        a1, d1 = together(a1, d1)
+        a, d = join(a, a1), join(d, d1)
+        a2 = stage(a, layout, zf, 1)
+        d2 = stage(d, layout, zl, 1)
+        a2, d2, b = together(a2, d2, b)
+        a, d = join(a, a2), join(d, d2)
+        a3 = stage(a, layout, zf, 2)
+        b1 = stage(b, layout, zf, 0)
+        a3, b1 = together(a3, b1)
+        a, b = join(a, a3), join(b, b1)
+        a4 = stage(a, layout, zf, 3)
+        b2 = stage(b, layout, zf, 1)
+        a5 = swap_cores(a, layout)
+        a4, b2, a5, d = together(a4, b2, a5, d)
+        d3 = stage(d, layout, zl, 2)
+        a6 = swap_cores(a4, layout)
+        b = join(b, b2)
+        b3 = stage(b, layout, zf, 2)
+        parts_a = (a, a4, a5, a6)
     else:
         count = 32
         rows = width // count
@@ -649,32 +735,60 @@
         parts_a = as_blocks(
             jnp.concatenate([whole(query_weight), whole(key_weight), whole(value_weight), tail], axis=1), count
         )
-        parts_b = as_blocks(jnp.concatenate([whole(output_weight), whole(inner_weight)], axis=1), count)
-        parts_d = as_blocks(whole(outer_weight), count)
-        ids = jnp.arange(count, dtype=jnp.int32)
+        outer = whole(outer_weight).reshape(count, -1, width)
+        extra = outer[:, OUTER_ROWS:]
+        third = extra[:, rows:].reshape(count, 8, 3, width // 3)
+        third = jnp.swapaxes(third, 1, 2).reshape(width, width // 3)
+        parts_b = as_blocks(
+            jnp.concatenate(
+                [whole(output_weight), whole(inner_weight), extra[:, :rows].reshape(width, width), third], axis=1
+            ),
+            count,
+        )
+        parts_d = as_blocks(outer[:, :OUTER_ROWS].reshape(-1, width), count)
+        ids = ids_d = jnp.arange(count, dtype=jnp.int32)
 
     turn = lambda v: jnp.swapaxes(v, 1, 2)
     down = turn(adapter_down_factors)
     up = adapter_up_factors
     qkv, weight, red, small_rows, inner_rows = project(ids, tokens, down, up, parts_a)
-    context, attention = attend(document_numbers, qkv)
+    if fast:
+        b3, d3, qkv = together(b3, d3, qkv)
+        b = join(b, b3)
+        b4 = stage(b, layout, zf, 3)
+        d = join(d, d3)
+        d4 = stage(d, layout, zl, 3)
+    half = attend(0, document_numbers, qkv)
+    if fast:
+        b5 = swap_cores(after(b, *half), layout)
+        d5 = swap_cores(after(d, *half), layout)
+    context, attention = attend(1, document_numbers, qkv, half)
+    if fast:
+        b4, d4, context = together(b4, d4, context)
+        b6 = swap_cores(b4, layout)
+        d6 = swap_cores(d4, layout)
+        parts_b = (b, b4, b5, b6)
+        parts_d = (d, d4, d5, d6)
     activations, grad_mid, grad_context, sums = row_local(
-        ids, tokens, cotangent, context, small_rows, inner_rows, parts_b, parts_d
-    )
-    grad_query, grad_keys, grad_values = attend_back(qkv, context, grad_context, attention)
-    grad_reduced, grads = adapter_grads(tokens, grad_query, grad_values, up, red, sums)
-    input_grad = input_gradient(
-        grad_mid, grad_query, grad_keys, grad_values, grad_reduced, down, weight
-    )
-    total = grads
-    for bit in [layout.core] + layout.bits[:-1]:
-        total = total + lax.ppermute(total, AXES, [(i, i ^ bit) for i in range(layout.n)])
+        ids, ids_d, tokens, cotangent, context, small_rows, inner_rows, parts_b, parts_d
+    )
+    core = jnp.reshape((lax.axis_index(AXES) & layout.core) != 0, (1,)).astype(jnp.int32)
+    dq, dk, dv, dred, keep, send = attend_back(
+        core, tokens, qkv, context, grad_context, attention, up, red, sums
+    )
+    total = keep + swap_cores(send, layout)
+    gradient = lambda: input_gradient(grad_mid, after(dq, total), dk, dv, dred, down, weight)
+    total, input_grad = exchange(total, layout, layout.x_bits + layout.y_bits, gradient)
+    total = exchange(total, layout, layout.z_bits)
+    other = swap_cores(total, layout)
     step_counter = step[0].astype(f32)
     scalars = jnp.stack([1.0 - beta_one**step_counter, 1.0 - beta_two**step_counter, rate[0]])
     gd, gu, gain_grad, shift_grad, pd, pu, dm, dv, um, uv = adamw(
         layout.n,
         scalars,
+        core,
         total,
+        other,
         down,
         up,
         turn(down_first_moment),

time: 220 us -> 181 us (0.82)
  waiting for transfers between devices: 75.5 us -> 38.2 us
  starting transfers between devices: 28.7 us -> 26.3 us
    ppermute x23 -> x26, waiting for transfers between devices: 75.5 us -> 38.2 us  [the longest x12 27.8 us: stage(): return lax.ppermute(held, AXES, layout.stage_pairs(orders, t))]
    pallas_call x1, Pallas kernels: 44 us -> 38.9 us  [row_local(): pl.pallas_call(rows_kernel, grid=(rows // tile,), in_specs=[pl.BlockSpec(...]
    pallas_call x4, Pallas kernels: 37.9 us -> 41.6 us  [the longest x1 20.1 us: attend_back(): pl.pallas_call(attend_back_kernel, grid=(rows // length, steps), in_specs...]
    pallas_call x1, Pallas kernels: 5.77 us -> 9.3 us  [input_gradient(): pl.pallas_call(input_kernel, grid=(rows // tile,), in_specs=[tiled, tiled...]
    ppermute x23 -> x26, starting transfers between devices: 28.7 us -> 26.3 us  [the longest x12 17.3 us: stage(): return lax.ppermute(held, AXES, layout.stage_pairs(orders, t))]
    concatenate x9 -> x7, other arithmetic: 2.82 us -> 0.4 us  [join(): return jnp.concatenate([held, came], axis=0)]
    unnamed x40 -> x32, local copies, waits for them, and re-layouts: 6.34 us -> 3.92 us
  transfers between devices with their start and end apart: 23 -> 26, of which waited for: 12 -> 12; matrix products, arithmetic and copies ran while one was open for 2% -> 3% of each run, Pallas kernels for 16% -> 22%
where the time goes in v2:
time: 181 us
  Pallas kernels  101 us (56%)
  waiting for transfers between devices  38.2 us (21%)
  starting transfers between devices  26.3 us (15%)
  local copies, waits for them, and re-layouts  7.32 us (4%)
  other arithmetic  5.6 us (3%)
  between operations  2.48 us (1%)
    pallas_call x1, Pallas kernels, row_local(): pl.pallas_call(rows_kernel, grid=(rows // tile,), in_specs=[pl.BlockSpec(...  38.9 us
    ppermute x12, waiting for transfers between devices, stage(): return lax.ppermute(held, AXES, layout.stage_pairs(orders, t))  27.8 us
    pallas_call x1, Pallas kernels, attend_back(): pl.pallas_call(attend_back_kernel, grid=(rows // length, steps), in_specs...  20.1 us
    pallas_call x2, Pallas kernels, attend(): pl.pallas_call(functools.partial(attend_kernel, pack), grid=(steps,), in_...  19.8 us
    ppermute x12, starting transfers between devices, stage(): return lax.ppermute(held, AXES, layout.stage_pairs(orders, t))  17.3 us
    pallas_call x1, Pallas kernels, project(): pl.pallas_call(project_kernel, grid=(rows // tile,), in_specs=[pl.BlockSp...  11.1 us
    pallas_call x1, Pallas kernels, input_gradient(): pl.pallas_call(input_kernel, grid=(rows // tile,), in_specs=[tiled, tiled...  9.3 us
    ppermute x6, starting transfers between devices, exchange(): lax.ppermute(total, AXES, layout.pairs(c))  7.94 us
  transfers between devices with their start and end apart: 26, of which 12 were waited for; matrix products, arithmetic and copies ran while one was open for 3% of the time, Pallas kernels for 22%

profile of v2, /device:TPU:0, one launch (start us, length us, event | category | flops | bytes accessed | tf_op | source)
XLA Modules:
  0.0 180.8 jit_solution(5831717428461357847)
XLA Ops:
  0.7 0.7 fusion.10
  1.4 0.8 fusion.5
  2.3 3.1 %collective-permute-start = (bf16[1,24,2432]{2,1,0:T(8,128)(2,1)S(1)}, bf16[1,24,2432]{2,1,0:T(8,128)(2,1)S(1)}, u32[]{:S(2)}, u32[]{:S(2)}) collective-permute-start(bf16[1,24,2432]{2,1,0:T(8,128)(2,1)S(1)} %fusion.5), channel_id=1, source_target_pairs={{0,2},{1,3},{2,0},{3,1},{4,6},{5,7},{6,4},{7,5},{8,12},{9,13},{10,... | collective-permute-start | bytes 350216 | tf_op jit(solution)/shard_map/ppermute | solution.py:81
  5.4 0.9 slice_bitcast_fusion
  6.3 1.5 collective-permute-start.1
  7.7 0.8 slice.13
  8.5 0.7 slice.14
  9.2 1.6 collective-permute-done.1
  10.9 2.7 %collective-permute-start.2 = (bf16[2,24,2432]{2,1,0:T(8,128)(2,1)S(1)}, bf16[2,24,2432]{2,1,0:T(8,128)(2,1)S(1)}, u32[]{:S(2)}, u32[]{:S(2)}) collective-permute-start(bf16[2,24,2432]{2,1,0:T(8,128)(2,1)S(1)} %pad_maximum_fusion.5), channel_id=1, source_target_pairs={{0,4},{1,5},{2,6},{3,7},{4,0},{5,1},{6,2},{7,3},{8,10},{9,11},{10,... | collective-permute-start | bytes 700424 | tf_op jit(solution)/shard_map/ppermute | solution.py:81
  13.6 1.6 collective-permute-start.3
  15.2 0.9 maximum_bitcast_fusion
  16.1 3.2 %collective-permute-done.3 = bf16[2,64,768]{2,1,0:T(8,128)(2,1)S(1)} collective-permute-done((bf16[2,64,768]{2,1,0:T(8,128)(2,1)S(1)}, bf16[2,64,768]{2,1,0:T(8,128)(2,1)S(1)}, u32[]{:S(2)}, u32[]{:S(2)}) %collective-permute-start.3) | collective-permute-done | bytes 196640 | tf_op jit(solution)/shard_map/ppermute | solution.py:81
  19.3 1.1 collective-permute-done.2
  20.4 1.6 collective-permute-start.4
  22.1 0.6 pad_add_fusion.ids_ref
  22.8 6.3 %collective-permute-done.5 = bf16[1,24,4864]{2,1,0:T(8,128)(2,1)S(1)} collective-permute-done((bf16[1,24,4864]{2,1,0:T(8,128)(2,1)S(1)}, bf16[1,24,4864]{2,1,0:T(8,128)(2,1)S(1)}, u32[]{:S(2)}, u32[]{:S(2)}) %collective-permute-start.5) | collective-permute-done | bytes 233504 | tf_op jit(solution)/shard_map/ppermute | solution.py:81
  29.2 2.5 %collective-permute-start.6 = (bf16[8,24,2432]{2,1,0:T(8,128)(2,1)S(1)}, bf16[8,24,2432]{2,1,0:T(8,128)(2,1)S(1)}, u32[]{:S(2)}, u32[]{:S(2)}) collective-permute-start(bf16[8,24,2432]{2,1,0:T(8,128)(2,1)S(1)} %pad_maximum_fusion.p0), channel_id=1, source_target_pairs={{0,1},{1,0},{2,3},{3,2},{4,5},{5,4},{6,7},{7,6},{8,24},{9,25},{10,... | collective-permute-start | bytes 2801672 | tf_op jit(solution)/shard_map/ppermute | solution.py:81
  31.8 14.2 %collective-permute-done.7 = bf16[2,24,4864]{2,1,0:T(8,128)(2,1)S(1)} collective-permute-done((bf16[2,24,4864]{2,1,0:T(8,128)(2,1)S(1)}, bf16[2,24,4864]{2,1,0:T(8,128)(2,1)S(1)}, u32[]{:S(2)}, u32[]{:S(2)}) %collective-permute-start.7) | collective-permute-done | bytes 466976 | tf_op jit(solution)/shard_map/ppermute | solution.py:81
  46.0 1.0 copy-done.11
  47.1 1.5 collective-permute-start.9
  49.0 1.2 copy-done.4
  50.2 1.0 copy-done.12
  51.1 11.1 %shard_map.328 = (bf16[1024,2304]{1,0:T(8,128)(2,1)}, bf16[768,2304]{1,0:T(8,128)(2,1)}, bf16[16,1024]{1,0:T(8,128)(2,1)}, f32[8,768]{1,0:T(8,128)}, f32[8,3072]{1,0:T(8,128)}) custom-call(s32[32]{0:T(128)} %pad_add_fusion.ids_ref, bf16[1024,768]{1,0:T(8,128)(2,1)} %x_ref.5, f32[2,8,768]{2,1,0:T(8,128)} %bitcast.20, f32[2,8,768]{2,1,0:T(8,128)} %up_ref.5, ...), custom_call_target="tpu_custom_call" | custom-call | flops 3623878656 | bytes 14680064 | tf_op jit(solution)/shard_map/pallas_call | solution.py:208
  62.2 1.0 constant_dynamic-update-slice_fusion.b0
  63.4 2.5 %collective-permute-start.13 = (bf16[8,64,768]{2,1,0:T(8,128)(2,1)S(1)}, bf16[8,64,768]{2,1,0:T(8,128)(2,1)S(1)}, u32[]{:S(2)}, u32[]{:S(2)}) collective-permute-start(bf16[8,64,768]{2,1,0:T(8,128)(2,1)S(1)} %constant_dynamic-update-slice_fusion.4.d0), channel_id=1, source_target_pairs={{0,4},{1,5},{2,6},{3,7},{4,0},{5,1},{6,2},{7,3},{8,10},{9,11},{10,... | collective-permute-start | bytes 2359304 | tf_op jit(solution)/shard_map/ppermute | solution.py:81
  65.9 9.8 %shard_map.329 = (bf16[1024,768]{1,0:T(8,128)(2,1)}, bf16[24,512,512]{2,1,0:T(8,128)(2,1)}) custom-call(s32[2,512]{1,0:T(2,128)} %seg_ref.3, bf16[1024,2304]{1,0:T(8,128)(2,1)} %get-tuple-element.80.q_ref.k_ref.v_ref, bf16[1024,2304]{1,0:T(8,128)(2,1)} %get-tuple-element.80.q_ref.k_ref.v_ref, bf16[1024,2304]{1,0:T(8,128)(2,1)} %get-tuple-element.80.q_ref.k_ref.v_ref), custom_call_target="tpu_custom_call" | custom-call | flops 3221225472 | bytes 10485760 | tf_op jit(solution)/shard_map/pallas_call | solution.py:284
  75.8 9.9 %shard_map.330 = (bf16[1024,768]{1,0:T(8,128)(2,1)}, bf16[24,512,512]{2,1,0:T(8,128)(2,1)}) custom-call(s32[2,512]{1,0:T(2,128)} %seg_ref.3, bf16[1024,2304]{1,0:T(8,128)(2,1)} %get-tuple-element.80.q_ref.k_ref.v_ref, bf16[1024,2304]{1,0:T(8,128)(2,1)} %get-tuple-element.80.q_ref.k_ref.v_ref, ...), custom_call_target="tpu_custom_call", output_to_operand_aliasing={{0}: (4, {}), {1}: (5, {})} | custom-call | flops 3221225472 | bytes 10485760 | tf_op jit(solution)/shard_map/pallas_call | solution.py:284
  85.7 1.4 collective-permute-done.12.b1
  87.1 0.5 collective-permute-start.16
  87.6 0.6 pad_add_fusion.1.ids_d_ref
  88.2 3.6 %collective-permute-done.16.d2 = bf16[8,64,768]{2,1,0:T(8,128)(2,1)} collective-permute-done((bf16[8,64,768]{2,1,0:T(8,128)(2,1)S(1)}, bf16[8,64,768]{2,1,0:T(8,128)(2,1)}, u32[]{:S(2)}, u32[]{:S(2)}) %collective-permute-start.16) | collective-permute-done | bytes 786464 | tf_op jit(solution)/shard_map/ppermute | solution.py:85
  91.8 1.1 collective-permute-done.17.d3
  93.0 0.6 collective-permute-done.15.b3
  93.5 38.9 %shard_map.331 = (bf16[1024,768]{1,0:T(8,128)(2,1)}, f32[1024,768]{1,0:T(8,128)}, bf16[1024,768]{1,0:T(8,128)(2,1)}, f32[8,768]{1,0:T(8,128)}) custom-call(s32[32]{0:T(128)} %pad_add_fusion.ids_ref, s32[32]{0:T(128)} %pad_add_fusion.1.ids_d_ref, bf16[1024,768]{1,0:T(8,128)(2,1)} %x_ref.5, bf16[1024,768]{1,0:T(8,128)(2,1)} %cot_ref.1, ...), custom_call_target="tpu_custom_call" | custom-call | flops 21743271936 | bytes 20971520 | tf_op jit(solution)/shard_map/pallas_call | solution.py:417
  132.5 20.1 %shard_map.332 = (bf16[1024,768]{1,0:T(8,128)(2,1)}, bf16[1024,768]{1,0:T(8,128)(2,1)}, bf16[1024,768]{1,0:T(8,128)(2,1)}, bf16[16,1024]{1,0:T(8,128)(2,1)}, f32[40,384]{1,0:T(8,128)}, /*index=5*/f32[40,384]{1,0:T(8,128)}) custom-call(s32[1]{0:T(128)} %bitcast.8.core_ref, bf16[1024,768]{1,0:T(8,128)(2,1)} %x_ref.5, ...), custom_call_target="tpu_custom_call" | custom-call | flops 12884901888 | bytes 29360128 | tf_op jit(solution)/shard_map/pallas_call | solution.py:528
  152.9 1.2 collective-permute-done.18
  154.1 0.8 add.31
  154.9 1.1 collective-permute-start.19
  156.5 1.9 %collective-permute-start.21 = (f32[40,384]{1,0:T(8,128)S(1)}, f32[40,384]{1,0:T(8,128)S(1)}, u32[]{:S(2)}, u32[]{:S(2)}) collective-permute-start(f32[40,384]{1,0:T(8,128)S(1)} %add.31), channel_id=1, source_target_pairs={{0,17},{1,16},{2,19},{3,18},{4,21},{5,20},{6,23},{7,22},{8,25},{9,... | collective-permute-start | bytes 184328 | tf_op jit(solution)/shard_map/ppermute | solution.py:105
  158.4 9.3 %shard_map.333 = f32[1024,768]{1,0:T(8,128)} custom-call(f32[1024,768]{1,0:T(8,128)} %get-tuple-element.98.mid_ref, bf16[1024,768]{1,0:T(8,128)(2,1)} %get-tuple-element.100.dq_ref, bf16[1024,768]{1,0:T(8,128)(2,1)} %get-tuple-element.101.dk_ref, bf16[1024,768]{1,0:T(8,128)(2,1)} %get-tuple-element.102.dv_ref, bf16[16,1024]{1,0:T(8,128)(2,1)} %get-tuple-element.103.dred_ref, ...), custom_call_target="tpu_custom_call" | custom-call | flops 3623878656 | bytes 15728640 | tf_op jit(solution)/shard_map/pallas_call | solution.py:578
  167.7 1.9 %collective-permute-start.22 = (f32[40,384]{1,0:T(8,128)S(1)}, f32[40,384]{1,0:T(8,128)S(1)}, u32[]{:S(2)}, u32[]{:S(2)}) collective-permute-start(f32[40,384]{1,0:T(8,128)S(1)} %add_add_fusion.1), channel_id=1, source_target_pairs={{0,2},{1,3},{2,0},{3,1},{4,6},{5,7},{6,4},{7,5},{8,10},{9,11},{10,... | collective-permute-start | bytes 184328 | tf_op jit(solution)/shard_map/ppermute | solution.py:105
  169.7 0.6 collective-permute-start.23
  170.2 2.0 %collective-permute-start.24 = (f32[40,384]{1,0:T(8,128)S(1)}, f32[40,384]{1,0:T(8,128)S(1)}, u32[]{:S(2)}, u32[]{:S(2)}) collective-permute-start(f32[40,384]{1,0:T(8,128)S(1)} %add_add_fusion.1), channel_id=1, source_target_pairs={{0,6},{1,7},{2,4},{3,5},{4,2},{5,3},{6,0},{7,1},{8,14},{9,15},{10,... | collective-permute-start | bytes 184328 | tf_op jit(solution)/shard_map/ppermute | solution.py:105
  173.6 3.3 %collective-permute-done.23 = f32[40,384]{1,0:T(8,128)S(1)} collective-permute-done((f32[40,384]{1,0:T(8,128)S(1)}, f32[40,384]{1,0:T(8,128)S(1)}, u32[]{:S(2)}, u32[]{:S(2)}) %collective-permute-start.23) | collective-permute-done | bytes 61472 | tf_op jit(solution)/shard_map/ppermute | solution.py:105
  177.0 0.7 pad_maximum_fusion.7.scal_ref
  177.6 0.6 collective-permute-done.25.other_ref
  178.2 0.6 copy-done.3
  178.9 1.8 shard_map.334
  (65 shorter events, 2.2 us)
Async XLA Ops:
  0.6 21.4 %copy-start.6 = (s32[16]{0:T(128)S(1)}, s32[16]{0:T(128)}, u32[]{:S(2)}) copy-start(s32[16]{0:T(128)} %constant.32.clone) | copy-start | bytes 196
  0.7 21.4 %copy-start.7 = (s32[16]{0:T(128)S(1)}, s32[16]{0:T(128)}, u32[]{:S(2)}) copy-start(s32[16]{0:T(128)} %constant.33.clone) | copy-start | bytes 196
  0.7 21.4 %copy-start.8 = (s32[16]{0:T(128)S(1)}, s32[16]{0:T(128)}, u32[]{:S(2)}) copy-start(s32[16]{0:T(128)} %constant.34.clone) | copy-start | bytes 196
  0.7 21.3 %copy-start.9 = (s32[16]{0:T(128)S(1)}, s32[16]{0:T(128)}, u32[]{:S(2)}) copy-start(s32[16]{0:T(128)} %constant.35.clone) | copy-start | bytes 196
  2.3 8.6 %collective-permute-start = (bf16[1,24,2432]{2,1,0:T(8,128)(2,1)S(1)}, bf16[1,24,2432]{2,1,0:T(8,128)(2,1)S(1)}, u32[]{:S(2)}, u32[]{:S(2)}) collective-permute-start(bf16[1,24,2432]{2,1,0:T(8,128)(2,1)S(1)} %fusion.5), channel_id=1, source_target_pairs={{0,2},{1,3},{2,0},{3,1},{4,6},{5,7},{6,4},{7,5},{8,12},{9,13},{10,... | collective-permute-start | bytes 350216 | tf_op jit(solution)/shard_map/ppermute | solution.py:81
  6.3 4.6 %collective-permute-start.1 = (bf16[1,64,768]{2,1,0:T(8,128)(2,1)S(1)}, bf16[1,64,768]{2,1,0:T(8,128)(2,1)S(1)}, u32[]{:S(2)}, u32[]{:S(2)}) collective-permute-start(bf16[1,64,768]{2,1,0:T(8,128)(2,1)S(1)} %slice_bitcast_fusion), channel_id=1, source_target_pairs={{0,16},{1,17},{2,18},{3,19},{4,20},{5,21},{6,22},{7,23},{8,9},{9,8... | collective-permute-start | bytes 294920 | tf_op jit(solution)/shard_map/ppermute | solution.py:81
  10.9 9.5 %collective-permute-start.2 = (bf16[2,24,2432]{2,1,0:T(8,128)(2,1)S(1)}, bf16[2,24,2432]{2,1,0:T(8,128)(2,1)S(1)}, u32[]{:S(2)}, u32[]{:S(2)}) collective-permute-start(bf16[2,24,2432]{2,1,0:T(8,128)(2,1)S(1)} %pad_maximum_fusion.5), channel_id=1, source_target_pairs={{0,4},{1,5},{2,6},{3,7},{4,0},{5,1},{6,2},{7,3},{8,10},{9,11},{10,... | collective-permute-start | bytes 700424 | tf_op jit(solution)/shard_map/ppermute | solution.py:81
  13.6 5.7 %collective-permute-start.3 = (bf16[2,64,768]{2,1,0:T(8,128)(2,1)S(1)}, bf16[2,64,768]{2,1,0:T(8,128)(2,1)S(1)}, u32[]{:S(2)}, u32[]{:S(2)}) collective-permute-start(bf16[2,64,768]{2,1,0:T(8,128)(2,1)S(1)} %pad_maximum_fusion.6), channel_id=1, source_target_pairs={{0,1},{1,0},{2,3},{3,2},{4,5},{5,4},{6,7},{7,6},{8,24},{9,25},{10,... | collective-permute-start | bytes 589832 | tf_op jit(solution)/shard_map/ppermute | solution.py:81
  20.4 8.6 %collective-permute-start.4 = (bf16[4,24,2432]{2,1,0:T(8,128)(2,1)S(1)}, bf16[4,24,2432]{2,1,0:T(8,128)(2,1)S(1)}, u32[]{:S(2)}, u32[]{:S(2)}) collective-permute-start(bf16[4,24,2432]{2,1,0:T(8,128)(2,1)S(1)} %pad_maximum_fusion.2), channel_id=1, source_target_pairs={{0,16},{1,17},{2,18},{3,19},{4,20},{5,21},{6,22},{7,23},{8,9},{9,8... | collective-permute-start | bytes 1400840 | tf_op jit(solution)/shard_map/ppermute | solution.py:81
  22.0 7.0 %collective-permute-start.5 = (bf16[1,24,4864]{2,1,0:T(8,128)(2,1)S(1)}, bf16[1,24,4864]{2,1,0:T(8,128)(2,1)S(1)}, u32[]{:S(2)}, u32[]{:S(2)}) collective-permute-start(bf16[1,24,4864]{2,1,0:T(8,128)(2,1)S(1)} %maximum_bitcast_fusion), channel_id=1, source_target_pairs={{0,2},{1,3},{2,0},{3,1},{4,6},{5,7},{6,4},{7,5},{8,12},{9,13},{10,... | collective-permute-start | bytes 700424 | tf_op jit(solution)/shard_map/ppermute | solution.py:81
  29.2 19.4 %copy-start = (bf16[8,24,2432]{2,1,0:T(8,128)(2,1)}, bf16[8,24,2432]{2,1,0:T(8,128)(2,1)S(1)}, u32[]{:S(2)}) copy-start(bf16[8,24,2432]{2,1,0:T(8,128)(2,1)S(1)} %pad_maximum_fusion.p0) | copy-start | bytes 2801668
  29.2 16.8 %collective-permute-start.6 = (bf16[8,24,2432]{2,1,0:T(8,128)(2,1)S(1)}, bf16[8,24,2432]{2,1,0:T(8,128)(2,1)S(1)}, u32[]{:S(2)}, u32[]{:S(2)}) collective-permute-start(bf16[8,24,2432]{2,1,0:T(8,128)(2,1)S(1)} %pad_maximum_fusion.p0), channel_id=1, source_target_pairs={{0,1},{1,0},{2,3},{3,2},{4,5},{5,4},{6,7},{7,6},{8,24},{9,25},{10,... | collective-permute-start | bytes 2801672 | tf_op jit(solution)/shard_map/ppermute | solution.py:81
  31.7 14.3 %collective-permute-start.8 = (bf16[8,24,2432]{2,1,0:T(8,128)(2,1)S(1)}, bf16[8,24,2432]{2,1,0:T(8,128)(2,1)S(1)}, u32[]{:S(2)}, u32[]{:S(2)}) collective-permute-start(bf16[8,24,2432]{2,1,0:T(8,128)(2,1)S(1)} %pad_maximum_fusion.p0), channel_id=1, source_target_pairs={{0,8},{1,9},{2,10},{3,11},{4,12},{5,13},{6,14},{7,15},{8,0},{9,1},... | collective-permute-start | bytes 2801672 | tf_op jit(solution)/shard_map/ppermute | solution.py:85
  31.7 14.3 %collective-permute-start.7 = (bf16[2,24,4864]{2,1,0:T(8,128)(2,1)S(1)}, bf16[2,24,4864]{2,1,0:T(8,128)(2,1)S(1)}, u32[]{:S(2)}, u32[]{:S(2)}) collective-permute-start(bf16[2,24,4864]{2,1,0:T(8,128)(2,1)S(1)} %pad_maximum_fusion.3), channel_id=1, source_target_pairs={{0,4},{1,5},{2,6},{3,7},{4,0},{5,1},{6,2},{7,3},{8,10},{9,11},{10,... | collective-permute-start | bytes 1400840 | tf_op jit(solution)/shard_map/ppermute | solution.py:81
  46.0 4.2 %copy-start.10 = (bf16[8,24,2432]{2,1,0:T(8,128)(2,1)}, bf16[8,24,2432]{2,1,0:T(8,128)(2,1)S(1)}, u32[]{:S(2)}) copy-start(bf16[8,24,2432]{2,1,0:T(8,128)(2,1)S(1)} %collective-permute-done.6.p1) | copy-start | bytes 2801668
  46.0 1.0 copy-start.11
  47.0 3.2 %collective-permute-start.11 = (bf16[8,24,2432]{2,1,0:T(8,128)(2,1)S(1)}, bf16[8,24,2432]{2,1,0:T(8,128)(2,1)S(1)}, u32[]{:S(2)}, u32[]{:S(2)}) collective-permute-start(bf16[8,24,2432]{2,1,0:T(8,128)(2,1)S(1)} %collective-permute-done.6.p1), channel_id=1, source_target_pairs={{0,8},{1,9},{2,10},{3,11},{4,12},{5,13},{6,14},{7,15},{8,0},{9,1},... | collective-permute-start | bytes 2801672 | tf_op jit(solution)/shard_map/ppermute | solution.py:85
  47.1 15.1 %collective-permute-start.9 = (bf16[4,24,4864]{2,1,0:T(8,128)(2,1)S(1)}, bf16[4,24,4864]{2,1,0:T(8,128)(2,1)S(1)}, u32[]{:S(2)}, u32[]{:S(2)}) collective-permute-start(bf16[4,24,4864]{2,1,0:T(8,128)(2,1)S(1)} %pad_maximum_fusion.1), channel_id=1, source_target_pairs={{0,16},{1,17},{2,18},{3,19},{4,20},{5,21},{6,22},{7,23},{8,9},{9,8... | collective-permute-start | bytes 2801672 | tf_op jit(solution)/shard_map/ppermute | solution.py:81
  48.6 13.6 %collective-permute-start.10 = (bf16[4,64,768]{2,1,0:T(8,128)(2,1)S(1)}, bf16[4,64,768]{2,1,0:T(8,128)(2,1)S(1)}, u32[]{:S(2)}, u32[]{:S(2)}) collective-permute-start(bf16[4,64,768]{2,1,0:T(8,128)(2,1)S(1)} %pad_maximum_fusion.4), channel_id=1, source_target_pairs={{0,2},{1,3},{2,0},{3,1},{4,6},{5,7},{6,4},{7,5},{8,12},{9,13},{10,... | collective-permute-start | bytes 1179656 | tf_op jit(solution)/shard_map/ppermute | solution.py:81
  48.9 1.2 copy-start.4
  50.2 1.0 copy-start.12
  63.2 23.9 %collective-permute-start.12 = (bf16[8,24,4864]{2,1,0:T(8,128)(2,1)}, bf16[8,24,4864]{2,1,0:T(8,128)(2,1)}, u32[]{:S(2)}, u32[]{:S(2)}) collective-permute-start(bf16[8,24,4864]{2,1,0:T(8,128)(2,1)} %constant_dynamic-update-slice_fusion.b0), channel_id=1, source_target_pairs={{0,1},{1,0},{2,3},{3,2},{4,5},{5,4},{6,7},{7,6},{8,24},{9,25},{10,... | collective-permute-start | bytes 5603336 | tf_op jit(solution)/shard_map/ppermute | solution.py:81
  63.4 23.8 %copy-start.2 = (bf16[8,64,768]{2,1,0:T(8,128)(2,1)}, bf16[8,64,768]{2,1,0:T(8,128)(2,1)S(1)}, u32[]{:S(2)}) copy-start(bf16[8,64,768]{2,1,0:T(8,128)(2,1)S(1)} %constant_dynamic-update-slice_fusion.4.d0) | copy-start | bytes 2359300
  63.4 12.3 %copy-start.5 = (bf16[8,24,4864]{2,1,0:T(8,128)(2,1)S(1)}, bf16[8,24,4864]{2,1,0:T(8,128)(2,1)}, u32[]{:S(2)}) copy-start(bf16[8,24,4864]{2,1,0:T(8,128)(2,1)} %constant_dynamic-update-slice_fusion.b0) | copy-start | bytes 5603332
  63.4 22.3 %collective-permute-start.13 = (bf16[8,64,768]{2,1,0:T(8,128)(2,1)S(1)}, bf16[8,64,768]{2,1,0:T(8,128)(2,1)S(1)}, u32[]{:S(2)}, u32[]{:S(2)}) collective-permute-start(bf16[8,64,768]{2,1,0:T(8,128)(2,1)S(1)} %constant_dynamic-update-slice_fusion.4.d0), channel_id=1, source_target_pairs={{0,4},{1,5},{2,6},{3,7},{4,0},{5,1},{6,2},{7,3},{8,10},{9,11},{10,... | collective-permute-start | bytes 2359304 | tf_op jit(solution)/shard_map/ppermute | solution.py:81
  75.7 16.1 %collective-permute-start.14 = (bf16[8,24,4864]{2,1,0:T(8,128)(2,1)S(1)}, bf16[8,24,4864]{2,1,0:T(8,128)(2,1)}, u32[]{:S(2)}, u32[]{:S(2)}) collective-permute-start(bf16[8,24,4864]{2,1,0:T(8,128)(2,1)S(1)} %copy-done.5), channel_id=1, source_target_pairs={{0,8},{1,9},{2,10},{3,11},{4,12},{5,13},{6,14},{7,15},{8,0},{9,1},... | collective-permute-start | bytes 5603336 | tf_op jit(solution)/shard_map/ppermute | solution.py:85
  85.7 7.8 %copy-start.13 = (bf16[8,64,768]{2,1,0:T(8,128)(2,1)}, bf16[8,64,768]{2,1,0:T(8,128)(2,1)S(1)}, u32[]{:S(2)}) copy-start(bf16[8,64,768]{2,1,0:T(8,128)(2,1)S(1)} %collective-permute-done.13.d1) | copy-start | bytes 2359300
  87.1 6.4 %collective-permute-start.15 = (bf16[8,24,4864]{2,1,0:T(8,128)(2,1)}, bf16[8,24,4864]{2,1,0:T(8,128)(2,1)}, u32[]{:S(2)}, u32[]{:S(2)}) collective-permute-start(bf16[8,24,4864]{2,1,0:T(8,128)(2,1)} %collective-permute-done.12.b1), channel_id=1, source_target_pairs={{0,8},{1,9},{2,10},{3,11},{4,12},{5,13},{6,14},{7,15},{8,0},{9,1},... | collective-permute-start | bytes 5603336 | tf_op jit(solution)/shard_map/ppermute | solution.py:85
  87.1 4.7 %collective-permute-start.16 = (bf16[8,64,768]{2,1,0:T(8,128)(2,1)S(1)}, bf16[8,64,768]{2,1,0:T(8,128)(2,1)}, u32[]{:S(2)}, u32[]{:S(2)}) collective-permute-start(bf16[8,64,768]{2,1,0:T(8,128)(2,1)S(1)} %constant_dynamic-update-slice_fusion.4.d0), channel_id=1, source_target_pairs={{0,8},{1,9},{2,10},{3,11},{4,12},{5,13},{6,14},{7,15},{8,0},{9,1},... | collective-permute-start | bytes 2359304 | tf_op jit(solution)/shard_map/ppermute | solution.py:85
  87.6 5.3 %collective-permute-start.17 = (bf16[8,64,768]{2,1,0:T(8,128)(2,1)S(1)}, bf16[8,64,768]{2,1,0:T(8,128)(2,1)}, u32[]{:S(2)}, u32[]{:S(2)}) collective-permute-start(bf16[8,64,768]{2,1,0:T(8,128)(2,1)S(1)} %collective-permute-done.13.d1), channel_id=1, source_target_pairs={{0,8},{1,9},{2,10},{3,11},{4,12},{5,13},{6,14},{7,15},{8,0},{9,1},... | collective-permute-start | bytes 2359304 | tf_op jit(solution)/shard_map/ppermute | solution.py:85
  152.6 1.5 collective-permute-start.18
  154.9 12.8 %collective-permute-start.19 = (f32[40,384]{1,0:T(8,128)S(1)}, f32[40,384]{1,0:T(8,128)S(1)}, u32[]{:S(2)}, u32[]{:S(2)}) collective-permute-start(f32[40,384]{1,0:T(8,128)S(1)} %add.31), channel_id=1, source_target_pairs={{0,16},{1,17},{2,18},{3,19},{4,20},{5,21},{6,22},{7,23},{8,24},{9,... | collective-permute-start | bytes 184328 | tf_op jit(solution)/shard_map/ppermute | solution.py:105
  156.0 11.7 %collective-permute-start.20 = (f32[40,384]{1,0:T(8,128)S(1)}, f32[40,384]{1,0:T(8,128)S(1)}, u32[]{:S(2)}, u32[]{:S(2)}) collective-permute-start(f32[40,384]{1,0:T(8,128)S(1)} %add.31), channel_id=1, source_target_pairs={{0,1},{1,0},{2,3},{3,2},{4,5},{5,4},{6,7},{7,6},{8,9},{9,8},{10,11... | collective-permute-start | bytes 184328 | tf_op jit(solution)/shard_map/ppermute | solution.py:105
  156.5 11.2 %collective-permute-start.21 = (f32[40,384]{1,0:T(8,128)S(1)}, f32[40,384]{1,0:T(8,128)S(1)}, u32[]{:S(2)}, u32[]{:S(2)}) collective-permute-start(f32[40,384]{1,0:T(8,128)S(1)} %add.31), channel_id=1, source_target_pairs={{0,17},{1,16},{2,19},{3,18},{4,21},{5,20},{6,23},{7,22},{8,25},{9,... | collective-permute-start | bytes 184328 | tf_op jit(solution)/shard_map/ppermute | solution.py:105
  167.7 5.8 %collective-permute-start.22 = (f32[40,384]{1,0:T(8,128)S(1)}, f32[40,384]{1,0:T(8,128)S(1)}, u32[]{:S(2)}, u32[]{:S(2)}) collective-permute-start(f32[40,384]{1,0:T(8,128)S(1)} %add_add_fusion.1), channel_id=1, source_target_pairs={{0,2},{1,3},{2,0},{3,1},{4,6},{5,7},{6,4},{7,5},{8,10},{9,11},{10,... | collective-permute-start | bytes 184328 | tf_op jit(solution)/shard_map/ppermute | solution.py:105
  169.7 7.2 %collective-permute-start.23 = (f32[40,384]{1,0:T(8,128)S(1)}, f32[40,384]{1,0:T(8,128)S(1)}, u32[]{:S(2)}, u32[]{:S(2)}) collective-permute-start(f32[40,384]{1,0:T(8,128)S(1)} %add_add_fusion.1), channel_id=1, source_target_pairs={{0,4},{1,5},{2,6},{3,7},{4,0},{5,1},{6,2},{7,3},{8,12},{9,13},{10,... | collective-permute-start | bytes 184328 | tf_op jit(solution)/shard_map/ppermute | solution.py:105
  170.2 6.6 %collective-permute-start.24 = (f32[40,384]{1,0:T(8,128)S(1)}, f32[40,384]{1,0:T(8,128)S(1)}, u32[]{:S(2)}, u32[]{:S(2)}) collective-permute-start(f32[40,384]{1,0:T(8,128)S(1)} %add_add_fusion.1), channel_id=1, source_target_pairs={{0,6},{1,7},{2,4},{3,5},{4,2},{5,3},{6,0},{7,1},{8,14},{9,15},{10,... | collective-permute-start | bytes 184328 | tf_op jit(solution)/shard_map/ppermute | solution.py:105
  176.9 1.3 copy-start.1
  176.9 1.3 collective-permute-start.25
  178.2 0.6 copy-start.3

commit v3 on v2

--- a/solution.py
+++ b/solution.py
@@ -22,7 +22,7 @@
 masked_score = -1e30
 root_half = math.sqrt(0.5)
 root_circle = 1.0 / math.sqrt(2.0 * math.pi)
-half_log = -0.5 * math.log2(math.e)
+log_e = math.log2(math.e)
 LANES = 128
 MIB = 1 << 20
 VMEM_LIMIT = 60 * MIB
@@ -98,16 +98,14 @@
     return jnp.concatenate([own, other])
 
 
-def exchange(total, layout, kinds, beside=None):
+def exchange(total, layout, kinds):
     combos = [0]
     for bit in kinds:
         combos = combos + [c ^ bit for c in combos]
     parts = [total] + [lax.ppermute(total, AXES, layout.pairs(c)) for c in combos[1:]]
-    if beside is not None:
-        *parts, beside = together(*parts, beside())
     while len(parts) > 1:
         parts = [one + two for one, two in zip(parts[::2], parts[1::2])]
-    return parts[0] if beside is None else (parts[0], beside)
+    return parts[0]
 
 
 def as_blocks(full, count):
@@ -242,34 +240,53 @@
     )(ids, tokens, down, up, *parts)
 
 
+def interleave(programs, lag):
+    tick, alive = 0, list(enumerate(programs))
+    while alive:
+        for item in list(alive):
+            if tick >= item[0] * lag:
+                try:
+                    next(item[1])
+                except StopIteration:
+                    alive.remove(item)
+        tick += 1
+
+
 def attend_kernel(pack, seg_ref, q_ref, k_ref, v_ref, *rest):
-    ctx_ref, w_ref, mask = rest[-3:]
+    ctx_ref, w_ref, inverse_ref, hot, cold = rest[-5:]
     rows = seg_ref.shape[1]
+    lane = lax.broadcasted_iota(jnp.int32, (1, LANES), 1)
 
     @pl.when(pl.program_id(0) == 0)
     def _():
         row = jnp.broadcast_to(seg_ref[pack : pack + 1, :].astype(f32), (8, rows))
         column = row.T[:, 0:1]
-        mask[...] = jnp.where(column == row[0:1], 0.0, masked_score)
-
-    lane = lax.broadcasted_iota(jnp.int32, (1, LANES), 1)
-    for s in range(q_ref.shape[1] // LANES):
+        slot = jnp.where(lane < HEAD, lane, lane - HEAD).astype(f32)
+        hot[...] = jnp.where(column == slot, 1.0, 0.0).astype(bf16)
+        cold[...] = jnp.where(column == slot, 0.0, masked_score).astype(bf16)
+
+    sums = {}
+
+    def program(s, h):
         cols = slice(s * LANES, (s + 1) * LANES)
-        q = q_ref[:, cols] * jnp.asarray(HEAD**-0.5, bf16)
-        k = k_ref[:, cols]
+        mine = (lane < HEAD) if h == 0 else (lane >= HEAD)
+        q = jnp.where(mine, q_ref[:, cols] * jnp.asarray(HEAD**-0.5, bf16), hot[...])
+        scores = nt(q, jnp.where(mine, k_ref[:, cols], cold[...]))
+        yield
+        peak = jnp.max(scores, axis=-1, keepdims=True)
+        exponent = jnp.exp2((scores - peak) * log_e).astype(bf16)
+        w_ref[2 * s + h] = exponent
+        yield
         v = v_ref[:, cols]
-        ctx = None
-        for h in range(2):
-            mine = (lane < HEAD) if h == 0 else (lane >= HEAD)
-            scores = nt(jnp.where(mine, q, jnp.zeros_like(q)), k) + mask[...]
-            peak = jnp.max(scores, axis=-1, keepdims=True)
-            exponent = jnp.exp(scores - peak)
-            total = jnp.sum(exponent, axis=-1, keepdims=True)
-            weights = (exponent * (1.0 / total)).astype(bf16)
-            w_ref[2 * s + h] = weights
-            part = nn(weights, jnp.where(mine, v, jnp.zeros_like(v)))
-            ctx = part if ctx is None else ctx + part
-        ctx_ref[:, cols] = ctx.astype(bf16)
+        sums[h] = nn(exponent, jnp.where(mine, v, jnp.ones_like(v)))
+        if h == 1:
+            top = jnp.where(lane < HEAD, sums[0], sums[1])
+            total = pltpu.roll(jnp.where(lane < HEAD, sums[1], sums[0]), HEAD, axis=1)
+            inverse = 1.0 / total
+            inverse_ref[:, cols] = inverse
+            ctx_ref[:, cols] = (top * inverse).astype(bf16)
+
+    interleave([program(s, h) for s in range(q_ref.shape[1] // LANES) for h in range(2)], 1)
 
 
 HEADS_A_STEP = 4
@@ -289,13 +306,15 @@
         out_specs=[
             pl.BlockSpec((length, step), lambda s: (pack, s)),
             pl.BlockSpec((HEADS_A_STEP, length, length), lambda s: (pack * steps + s, 0, 0)),
+            pl.BlockSpec((length, step), lambda s: (pack, s)),
         ],
         out_shape=[
             jax.ShapeDtypeStruct((packs * length, width), bf16),
             jax.ShapeDtypeStruct((packs * width // HEAD, length, length), bf16),
+            jax.ShapeDtypeStruct((packs * length, width), f32),
         ],
         input_output_aliases={4 + i: i for i in range(len(before))},
-        scratch_shapes=[pltpu.VMEM((length, length), f32)],
+        scratch_shapes=[pltpu.VMEM((length, LANES), bf16), pltpu.VMEM((length, LANES), bf16)],
         compiler_params=pltpu.CompilerParams(vmem_limit_bytes=VMEM_LIMIT),
         cost_estimate=pl.CostEstimate(
             flops=16 * length * length * width, bytes_accessed=10 * MIB, transcendentals=0
@@ -320,14 +339,27 @@
 
 def gelu_parts(z):
     cumulative = 0.5 + 0.5 * lax.erf(z * root_half)
-    density = jnp.exp2(z * z * half_log) * root_circle
+    density = jnp.exp2(z * z * (-0.5 * log_e)) * root_circle
     return z * cumulative, cumulative + z * density
+
+
+ROW_TILE = 256
+ROW_TILES = 2
+ROW_LAG = 12
+PIECE = 64
+SIDE = 256
+FF_CHUNK = 512
+
+
+def fold(value):
+    rows, width = value.shape
+    return jnp.sum(value.reshape(rows // 8, 8, width), axis=0)
 
 
 def rows_kernel(ids_ref, ids_d_ref, x_ref, cot_ref, ctx_ref, small_ref, inner_bias_ref,
                 b0, b1, b2, b3, d0, d1, d2, d3,
                 act_ref, mid_ref, dctx_ref, sums_ref,
-                stage, wo, wi, wf, active, slope, sem_b, sem_d):
+                stage, wo, wi, wf, active, slope, normed, inverse, first, first_b, total, grad_res, grad_b, sem_b, sem_d):
     parts_b, parts_d = (b0, b1, b2, b3), (d0, d1, d2, d3)
     width = x_ref.shape[1]
     taken = d0.shape[1]
@@ -373,45 +405,76 @@
     bias_out, bias_ff = small_ref[2:3], small_ref[3:4]
     gain_one, gain_two = small_ref[4:5], small_ref[5:6]
     shift_one, shift_two = small_ref[6:7], small_ref[7:8]
-    chunk = 512
-    normed_one, inverse_one = stats(x_ref[...].astype(f32) + (nn(ctx_ref[...], wo[...]) + bias_out))
-    first = normed_one * gain_one + shift_one
-    first_b = first.astype(bf16)
-    outer = None
-    for c in range(0, ff, chunk):
-        cols = slice(c, c + chunk)
-        inner = nn(first_b, wi[:, cols]) + inner_bias_ref[0:1, cols]
-        value, grad = gelu_parts(inner)
-        active[:, cols] = value.astype(bf16)
-        slope[:, cols] = grad.astype(bf16)
-    outer = nn(active[...], wf[...]) + bias_ff
-    normed_two, inverse_two = stats(first + outer)
-    act_ref[...] = (normed_two * gain_two + shift_two).astype(bf16)
-    grad_out = cot_ref[...].astype(f32)
-    grad_gain_two = jnp.sum(grad_out * normed_two, axis=0, keepdims=True)
-    grad_shift_two = jnp.sum(grad_out, axis=0, keepdims=True)
-    grad_res = norm_back(grad_out, normed_two, inverse_two, gain_two)
-    grad_outer = grad_res.astype(bf16)
-    for c in range(0, ff, chunk):
-        cols = slice(c, c + chunk)
-        grad_active = nt(grad_outer, wf[cols])
-        active[:, cols] = (grad_active * slope[:, cols].astype(f32)).astype(bf16)
-    grad_first = grad_res + nt(active[...], wi[...])
-    grad_gain_one = jnp.sum(grad_first * normed_one, axis=0, keepdims=True)
-    grad_shift_one = jnp.sum(grad_first, axis=0, keepdims=True)
-    sums_ref[0:4] += jnp.concatenate(
-        [grad_gain_one, grad_gain_two, grad_shift_one, grad_shift_two], axis=0
-    )
-    grad_mid = norm_back(grad_first, normed_one, inverse_one, gain_one)
-    mid_ref[...] = grad_mid
-    dctx_ref[...] = nt(grad_mid.astype(bf16), wo[...]).astype(bf16)
+    sums = [jnp.zeros((8, width), f32) for _ in range(4)]
+
+    def program(t):
+        every = slice(t * ROW_TILE, (t + 1) * ROW_TILE)
+        pieces = [
+            (slice(t * ROW_TILE + p, t * ROW_TILE + p + PIECE), slice(p, p + PIECE))
+            for p in range(0, ROW_TILE, PIECE)
+        ]
+        sides = [slice(c, c + SIDE) for c in range(0, width, SIDE)]
+        chunks = [slice(c, c + FF_CHUNK) for c in range(0, ff, FF_CHUNK)]
+        for c in sides:
+            total[t, :, c] = x_ref[every, c].astype(f32) + (nn(ctx_ref[every], wo[:, c]) + bias_out[:, c])
+            yield
+        for far, near in pieces:
+            n, i = stats(total[t, near])
+            normed[t, near] = n
+            inverse[t, near] = i
+            f = n * gain_one + shift_one
+            first[t, near] = f
+            first_b[t, near] = f.astype(bf16)
+            yield
+        for c in chunks:
+            value, grad = gelu_parts(nn(first_b[t], wi[:, c]) + inner_bias_ref[0:1, c])
+            active[t, :, c] = value.astype(bf16)
+            slope[t, :, c] = grad.astype(bf16)
+            yield
+        for c in sides:
+            total[t, :, c] = first[t, :, c] + (nn(active[t], wf[:, c]) + bias_ff[:, c])
+            yield
+        for far, near in pieces:
+            n, i = stats(total[t, near])
+            act_ref[far] = (n * gain_two + shift_two).astype(bf16)
+            g = cot_ref[far].astype(f32)
+            sums[1] = sums[1] + fold(g * n)
+            sums[3] = sums[3] + fold(g)
+            res = norm_back(g, n, i, gain_two)
+            grad_res[t, near] = res
+            grad_b[t, near] = res.astype(bf16)
+            yield
+        for c in chunks:
+            grad_active = nt(grad_b[t], wf[c])
+            active[t, :, c] = (grad_active * slope[t, :, c].astype(f32)).astype(bf16)
+            yield
+        for c in sides:
+            total[t, :, c] = grad_res[t, :, c] + nt(active[t], wi[c])
+            yield
+        for far, near in pieces:
+            g = total[t, near]
+            n = normed[t, near]
+            sums[0] = sums[0] + fold(g * n)
+            sums[2] = sums[2] + fold(g)
+            mid = norm_back(g, n, inverse[t, near], gain_one)
+            mid_ref[far] = mid
+            grad_b[t, near] = mid.astype(bf16)
+            yield
+        for c in sides:
+            dctx_ref[every, c] = nt(grad_b[t], wo[c]).astype(bf16)
+            yield
+
+    interleave([program(t) for t in range(x_ref.shape[0] // ROW_TILE)], ROW_LAG)
+    for i, value in enumerate(sums):
+        sums_ref[i : i + 1] += jnp.sum(value, axis=0, keepdims=True)
 
 
 def row_local(ids, ids_d, tokens, cotangent, context, small, inner_bias, parts_b, parts_d):
     rows, width = tokens.shape
     ff = inner_bias.shape[1]
     shards = 4 * parts_b[0].shape[0]
-    tile = 256
+    tile = ROW_TILE * ROW_TILES
+    two = lambda w, kind: pltpu.VMEM((ROW_TILES, ROW_TILE, w), kind)
     whole = lambda *shape: pl.BlockSpec(shape, lambda i: (0,) * len(shape))
     tiled = pl.BlockSpec((tile, width), lambda i: (i, 0))
     return pl.pallas_call(
@@ -439,8 +502,15 @@
             pltpu.VMEM((width, width), bf16),
             pltpu.VMEM((width, ff), bf16),
             pltpu.VMEM((ff, width), bf16),
-            pltpu.VMEM((tile, ff), bf16),
-            pltpu.VMEM((tile, ff), bf16),
+            two(ff, bf16),
+            two(ff, bf16),
+            two(width, f32),
+            two(1, f32),
+            two(width, f32),
+            two(width, bf16),
+            two(width, f32),
+            two(width, f32),
+            two(width, bf16),
             pltpu.SemaphoreType.DMA((shards,)),
             pltpu.SemaphoreType.DMA((shards,)),
         ],
@@ -451,8 +521,12 @@
     )(ids, ids_d, tokens, cotangent, context, small, inner_bias, *parts_b, *parts_d)
 
 
-def attend_back_kernel(core_ref, x_ref, q_ref, k_ref, v_ref, ctx_ref, dctx_ref, w_ref, up_ref, red_ref,
-                       sums_ref, dq_ref, dk_ref, dv_ref, dred_ref, keep_ref, send_ref, dred, grads):
+BACK_LAG = 3
+
+
+def attend_back_kernel(core_ref, x_ref, q_ref, k_ref, v_ref, ctx_ref, dctx_ref, inverse_ref, w_ref, up_ref, red_ref,
+                       sums_ref, mid_ref, down_ref, wq_ref, wk_ref, wv_ref, out_ref, keep_ref, send_ref,
+                       dq_ref, dk_ref, dv_ref, dred, grads):
     scale = HEAD**-0.5
     pack, step = pl.program_id(0), pl.program_id(1)
     rank = red_ref.shape[0] // 2
@@ -468,30 +542,35 @@
         dred[...] = jnp.zeros_like(dred)
 
     lane = lax.broadcasted_iota(jnp.int32, (1, LANES), 1)
-    for s in range(q_ref.shape[1] // LANES):
+    held = {}
+
+    def program(s, h):
         cols = slice(s * LANES, (s + 1) * LANES)
-        q, k, v = q_ref[:, cols], k_ref[:, cols], v_ref[:, cols]
-        dctx = dctx_ref[:, cols]
-        flat = dctx.astype(f32) * ctx_ref[:, cols].astype(f32)
-        q_t = q.T
-        dctx_t = dctx.T
-        dq = None
-        dk_t, dv_t = [], []
-        for h in range(2):
-            mine = (lane < HEAD) if h == 0 else (lane >= HEAD)
-            zero = jnp.zeros_like(q)
-            grad_weights = nt(jnp.where(mine, dctx, zero), v)
-            delta = jnp.sum(jnp.where(mine, flat, 0.0), axis=-1, keepdims=True)
-            weights = w_ref[2 * s + h]
-            grad_scores = (weights.astype(f32) * (grad_weights - delta)).astype(bf16)
-            part = nn(grad_scores, jnp.where(mine, k, zero))
-            dq = part if dq is None else dq + part
-            rows = slice(h * HEAD, (h + 1) * HEAD)
-            dk_t.append(nn(q_t[rows], grad_scores))
-            dv_t.append(nn(dctx_t[rows], weights))
-        dq_ref[:, cols] = (dq * scale).astype(bf16)
-        dk_ref[:, cols] = (jnp.concatenate(dk_t, axis=0) * scale).T.astype(bf16)
-        dv_ref[:, cols] = jnp.concatenate(dv_t, axis=0).T.astype(bf16)
+        mine = (lane < HEAD) if h == 0 else (lane >= HEAD)
+        rows = slice(h * HEAD, (h + 1) * HEAD)
+        q = q_ref[:, cols]
+        zero = jnp.zeros_like(q)
+        if h == 0:
+            dctx = (dctx_ref[:, cols].astype(f32) * inverse_ref[:, cols]).astype(bf16)
+            flat = dctx.astype(f32) * ctx_ref[:, cols].astype(f32)
+            held[s] = (dctx, flat, q.T, dctx.T, [], [], [])
+        dctx, flat, q_t, dctx_t, dq, dk_t, dv_t = held[s]
+        grad_weights = nt(jnp.where(mine, dctx, zero), v_ref[:, cols])
+        yield
+        delta = jnp.sum(jnp.where(mine, flat, 0.0), axis=-1, keepdims=True)
+        weights = w_ref[2 * s + h]
+        grad_scores = (weights.astype(f32) * (grad_weights - delta)).astype(bf16)
+        yield
+        dv_t.append(nn(dctx_t[rows], weights))
+        dq.append(nn(grad_scores, jnp.where(mine, k_ref[:, cols], zero)))
+        dk_t.append(nn(q_t[rows], grad_scores))
+        if h == 1:
+            dq_ref[:, cols] = ((dq[0] + dq[1]) * scale).astype(bf16)
+            dk_ref[:, cols] = (jnp.concatenate(dk_t, axis=0) * scale).T.astype(bf16)
+            dv_ref[:, cols] = jnp.concatenate(dv_t, axis=0).T.astype(bf16)
+            del held[s]
+
+    interleave([program(s, h) for s in range(q_ref.shape[1] // LANES) for h in range(2)], BACK_LAG)
     red = red_ref[...]
     up = (2.0 * up_ref[...].astype(bf16).astype(f32)).astype(bf16)
     none = jnp.zeros_like(up[0])
@@ -500,10 +579,21 @@
     grads[step, 0:rank] += 2.0 * nn(red, dq)[0:rank]
     grads[step, rank : 2 * rank] += 2.0 * nn(red, dv)[rank : 2 * rank]
 
+    grad = nt(dq, wq_ref[...]) + nt(dk_ref[...], wk_ref[...]) + nt(dv, wv_ref[...])
+
+    @pl.when(step == 0)
+    def _():
+        out_ref[...] = mid_ref[...] + grad
+
+    @pl.when(step > 0)
+    def _():
+        out_ref[...] += grad
+
     @pl.when(step == pl.num_programs(1) - 1)
     def _():
         rounded = dred[...].astype(bf16)
-        dred_ref[...] = rounded
+        joined = down_ref[...].reshape(2 * rank, down_ref.shape[2]).astype(bf16)
+        out_ref[...] += lax.dot_general(rounded, joined, (((0,), (0,)), ((), ())), preferred_element_type=f32)
         down = nn(rounded, x_ref[...])
         raised = jnp.concatenate([grads[i] for i in range(grads.shape[0])], axis=1)
         half = down.shape[1] // 2
@@ -515,85 +605,54 @@
             out[4 * rank : 5 * rank] = pick(sums_ref[...])
 
 
-def attend_back(core, tokens, qkv, context, grad_context, weights, up, red, sums):
+def attend_back(core, tokens, qkv, context, grad_context, inverse, weights, up, red, sums, mid, down, weight):
     rows, width = context.shape
     length = weights.shape[1]
     rank = up.shape[1]
     step = HEADS_A_STEP * HEAD
     steps = width // step
     at = lambda which: pl.BlockSpec((length, step), lambda p, s: (p, which * steps + s))
+    from_weight = lambda which: pl.BlockSpec((width, step), lambda p, s: (0, which * steps + s))
     own = pl.BlockSpec((length, step), lambda p, s: (p, s))
+    pack = pl.BlockSpec((length, width), lambda p, s: (p, 0))
     whole = lambda *shape: pl.BlockSpec(shape, lambda p, s: (0,) * len(shape))
-    along = pl.BlockSpec((2 * rank, length), lambda p, s: (0, p))
+    half = whole(5 * rank, width // 2)
     return pl.pallas_call(
         attend_back_kernel,
         grid=(rows // length, steps),
         in_specs=[
             pl.BlockSpec(memory_space=pltpu.SMEM),
-            pl.BlockSpec((length, width), lambda p, s: (p, 0)),
+            pack,
             at(0),
             at(1),
             at(2),
             own,
             own,
+            own,
             pl.BlockSpec((HEADS_A_STEP, length, length), lambda p, s: (p * steps + s, 0, 0)),
             pl.BlockSpec((2, rank, step), lambda p, s: (0, 0, s)),
-            along,
+            pl.BlockSpec((2 * rank, length), lambda p, s: (0, p)),
             whole(*sums.shape),
-        ],
-        out_specs=[own, own, own, along, whole(5 * rank, width // 2), whole(5 * rank, width // 2)],
-        out_shape=[jax.ShapeDtypeStruct((rows, width), bf16)] * 3
-        + [
-            jax.ShapeDtypeStruct((2 * rank, rows), bf16),
+            pack,
+            whole(*down.shape),
+            from_weight(0),
+            from_weight(1),
+            from_weight(2),
+        ],
+        out_specs=[pack, half, half],
+        out_shape=[
+            jax.ShapeDtypeStruct((rows, width), f32),
             jax.ShapeDtypeStruct((5 * rank, width // 2), f32),
             jax.ShapeDtypeStruct((5 * rank, width // 2), f32),
         ],
-        scratch_shapes=[pltpu.VMEM((2 * rank, length), f32), pltpu.VMEM((steps, 2 * rank, step), f32)],
+        scratch_shapes=[pltpu.VMEM((length, step), bf16)] * 3
+        + [pltpu.VMEM((2 * rank, length), f32), pltpu.VMEM((steps, 2 * rank, step), f32)],
         compiler_params=pltpu.CompilerParams(vmem_limit_bytes=VMEM_LIMIT),
         cost_estimate=pl.CostEstimate(
             flops=32 * rows * length * width, bytes_accessed=28 * MIB, transcendentals=0
         ),
-    )(core, tokens, qkv, qkv, qkv, context, grad_context, weights, up, red, sums)
-
-
-def input_kernel(mid_ref, dq_ref, dk_ref, dv_ref, dred_ref, down_ref, w_ref, out_ref):
-    width = mid_ref.shape[1]
-    rank = down_ref.shape[1]
-    down = down_ref[...].reshape(2 * rank, width).astype(bf16)
-    low = lax.dot_general(dred_ref[...], down, (((0,), (0,)), ((), ())), preferred_element_type=f32)
-    out_ref[...] = (
-        mid_ref[...]
-        + low
-        + nt(dq_ref[...], w_ref[:, 0:width])
-        + nt(dk_ref[...], w_ref[:, width : 2 * width])
-        + nt(dv_ref[...], w_ref[:, 2 * width : 3 * width])
-    )
-
-
-def input_gradient(mid, dq, dk, dv, dred, down, weight):
-    rows, width = mid.shape
-    tile = 256
-    whole = lambda *shape: pl.BlockSpec(shape, lambda i: (0,) * len(shape))
-    tiled = pl.BlockSpec((tile, width), lambda i: (i, 0))
-    return pl.pallas_call(
-        input_kernel,
-        grid=(rows // tile,),
-        in_specs=[
-            tiled,
-            tiled,
-            tiled,
-            tiled,
-            pl.BlockSpec((dred.shape[0], tile), lambda i: (0, i)),
-            whole(*down.shape),
-            whole(*weight.shape),
-        ],
-        out_specs=tiled,
-        out_shape=jax.ShapeDtypeStruct((rows, width), f32),
-        compiler_params=pltpu.CompilerParams(vmem_limit_bytes=VMEM_LIMIT),
-        cost_estimate=pl.CostEstimate(
-            flops=6 * rows * width * width, bytes_accessed=15 * MIB, transcendentals=0
-        ),
-    )(mid, dq, dk, dv, dred, down, weight)
+    )(core, tokens, qkv, qkv, qkv, context, grad_context, inverse, weights, up, red, sums, mid, down, weight,
+      weight, weight)
 
 
 def adamw_kernel(count, scal_ref, core_ref, mine_ref, other_ref, down_ref, up_ref, dm_ref, dv_ref, um_ref, uv_ref,
@@ -762,7 +821,7 @@
     if fast:
         b5 = swap_cores(after(b, *half), layout)
         d5 = swap_cores(after(d, *half), layout)
-    context, attention = attend(1, document_numbers, qkv, half)
+    context, attention, inverse = attend(1, document_numbers, qkv, half)
     if fast:
         b4, d4, context = together(b4, d4, context)
         b6 = swap_cores(b4, layout)
@@ -773,12 +832,11 @@
         ids, ids_d, tokens, cotangent, context, small_rows, inner_rows, parts_b, parts_d
     )
     core = jnp.reshape((lax.axis_index(AXES) & layout.core) != 0, (1,)).astype(jnp.int32)
-    dq, dk, dv, dred, keep, send = attend_back(
-        core, tokens, qkv, context, grad_context, attention, up, red, sums
+    input_grad, keep, send = attend_back(
+        core, tokens, qkv, context, grad_context, inverse, attention, up, red, sums, grad_mid, down, weight
     )
     total = keep + swap_cores(send, layout)
-    gradient = lambda: input_gradient(grad_mid, after(dq, total), dk, dv, dred, down, weight)
-    total, input_grad = exchange(total, layout, layout.x_bits + layout.y_bits, gradient)
+    total = exchange(total, layout, layout.x_bits + layout.y_bits)
     total = exchange(total, layout, layout.z_bits)
     other = swap_cores(total, layout)
     step_counter = step[0].astype(f32)

time: 181 us -> 177 us (0.978)
  Pallas kernels: 101 us -> 90 us
  waiting for transfers between devices: 38.2 us -> 44.9 us
    pallas_call x1 -> x0, Pallas kernels: 9.3 us -> none  [input_gradient(): pl.pallas_call(input_kernel, grid=(rows // tile,), in_specs=[tiled, tiled...]
    pallas_call x1, Pallas kernels: 20.1 us -> 25.1 us  [attend_back(): pl.pallas_call(attend_back_kernel, grid=(rows // length, steps), in_specs...]
    ppermute x12, waiting for transfers between devices: 27.8 us -> 31.7 us  [stage(): return lax.ppermute(held, AXES, layout.stage_pairs(orders, t))]
    pallas_call x2, Pallas kernels: 19.8 us -> 15.9 us  [attend(): pl.pallas_call(functools.partial(attend_kernel, pack), grid=(steps,), in_...]
    ppermute x6, waiting for transfers between devices: 3.29 us -> 6.07 us  [exchange(): lax.ppermute(total, AXES, layout.pairs(c))]
    pallas_call x1, Pallas kernels: 38.9 us -> 36.2 us  [row_local(): pl.pallas_call(rows_kernel, grid=(rows // tile,), in_specs=[pl.BlockSpec(...]
  transfers between devices with their start and end apart: 26 -> 26, of which waited for: 12 -> 16; matrix products, arithmetic and copies ran while one was open for 3% -> 3% of each run, Pallas kernels for 22% -> 15%
where the time goes in v3:
time: 177 us
  Pallas kernels  90 us (51%)
  waiting for transfers between devices  44.9 us (25%)
  starting transfers between devices  26.3 us (15%)
  local copies, waits for them, and re-layouts  7.31 us (4%)
  other arithmetic  5.6 us (3%)
  between operations  2.48 us (1%)
    pallas_call x1, Pallas kernels, row_local(): pl.pallas_call(rows_kernel, grid=(rows // tile,), in_specs=[pl.BlockSpec(...  36.2 us
    ppermute x12, waiting for transfers between devices, stage(): return lax.ppermute(held, AXES, layout.stage_pairs(orders, t))  31.7 us
    pallas_call x1, Pallas kernels, attend_back(): pl.pallas_call(attend_back_kernel, grid=(rows // length, steps), in_specs...  25.1 us
    ppermute x12, starting transfers between devices, stage(): return lax.ppermute(held, AXES, layout.stage_pairs(orders, t))  17.3 us
    pallas_call x2, Pallas kernels, attend(): pl.pallas_call(functools.partial(attend_kernel, pack), grid=(steps,), in_...  15.9 us
    pallas_call x1, Pallas kernels, project(): pl.pallas_call(project_kernel, grid=(rows // tile,), in_specs=[pl.BlockSp...  11.1 us
    ppermute x6, starting transfers between devices, exchange(): lax.ppermute(total, AXES, layout.pairs(c))  7.94 us
    ppermute x8, waiting for transfers between devices, swap_cores(): return lax.ppermute(value, AXES, layout.core_pairs())  7.1 us
  transfers between devices with their start and end apart: 26, of which 16 were waited for; matrix products, arithmetic and copies ran while one was open for 3% of the time, Pallas kernels for 15%

profile of v3, /device:TPU:0, one launch (start us, length us, event | category | flops | bytes accessed | tf_op | source)
XLA Modules:
  0.0 176.5 jit_solution(2480617313817131087)
XLA Ops:
  0.7 0.7 fusion.10
  1.4 0.8 fusion.5
  2.3 3.1 %collective-permute-start = (bf16[1,24,2432]{2,1,0:T(8,128)(2,1)S(1)}, bf16[1,24,2432]{2,1,0:T(8,128)(2,1)S(1)}, u32[]{:S(2)}, u32[]{:S(2)}) collective-permute-start(bf16[1,24,2432]{2,1,0:T(8,128)(2,1)S(1)} %fusion.5), channel_id=1, source_target_pairs={{0,2},{1,3},{2,0},{3,1},{4,6},{5,7},{6,4},{7,5},{8,12},{9,13},{10,... | collective-permute-start | bytes 350216 | tf_op jit(solution)/shard_map/ppermute | solution.py:81
  5.4 0.9 slice_bitcast_fusion
  6.3 1.5 collective-permute-start.1
  7.7 0.8 slice.13
  8.5 0.7 slice.14
  9.2 1.6 collective-permute-done.1
  10.9 2.7 %collective-permute-start.2 = (bf16[2,24,2432]{2,1,0:T(8,128)(2,1)S(1)}, bf16[2,24,2432]{2,1,0:T(8,128)(2,1)S(1)}, u32[]{:S(2)}, u32[]{:S(2)}) collective-permute-start(bf16[2,24,2432]{2,1,0:T(8,128)(2,1)S(1)} %pad_maximum_fusion.5), channel_id=1, source_target_pairs={{0,4},{1,5},{2,6},{3,7},{4,0},{5,1},{6,2},{7,3},{8,10},{9,11},{10,... | collective-permute-start | bytes 700424 | tf_op jit(solution)/shard_map/ppermute | solution.py:81
  13.6 1.6 collective-permute-start.3
  15.2 0.9 maximum_bitcast_fusion
  16.1 3.2 %collective-permute-done.3 = bf16[2,64,768]{2,1,0:T(8,128)(2,1)S(1)} collective-permute-done((bf16[2,64,768]{2,1,0:T(8,128)(2,1)S(1)}, bf16[2,64,768]{2,1,0:T(8,128)(2,1)S(1)}, u32[]{:S(2)}, u32[]{:S(2)}) %collective-permute-start.3) | collective-permute-done | bytes 196640 | tf_op jit(solution)/shard_map/ppermute | solution.py:81
  19.3 1.1 collective-permute-done.2
  20.4 1.6 collective-permute-start.4
  22.1 0.6 pad_add_fusion.ids_ref
  22.8 6.3 %collective-permute-done.5 = bf16[1,24,4864]{2,1,0:T(8,128)(2,1)S(1)} collective-permute-done((bf16[1,24,4864]{2,1,0:T(8,128)(2,1)S(1)}, bf16[1,24,4864]{2,1,0:T(8,128)(2,1)S(1)}, u32[]{:S(2)}, u32[]{:S(2)}) %collective-permute-start.5) | collective-permute-done | bytes 233504 | tf_op jit(solution)/shard_map/ppermute | solution.py:81
  29.2 2.5 %collective-permute-start.6 = (bf16[8,24,2432]{2,1,0:T(8,128)(2,1)S(1)}, bf16[8,24,2432]{2,1,0:T(8,128)(2,1)S(1)}, u32[]{:S(2)}, u32[]{:S(2)}) collective-permute-start(bf16[8,24,2432]{2,1,0:T(8,128)(2,1)S(1)} %pad_maximum_fusion.p0), channel_id=1, source_target_pairs={{0,1},{1,0},{2,3},{3,2},{4,5},{5,4},{6,7},{7,6},{8,24},{9,25},{10,... | collective-permute-start | bytes 2801672 | tf_op jit(solution)/shard_map/ppermute | solution.py:81
  31.8 14.2 %collective-permute-done.7 = bf16[2,24,4864]{2,1,0:T(8,128)(2,1)S(1)} collective-permute-done((bf16[2,24,4864]{2,1,0:T(8,128)(2,1)S(1)}, bf16[2,24,4864]{2,1,0:T(8,128)(2,1)S(1)}, u32[]{:S(2)}, u32[]{:S(2)}) %collective-permute-start.7) | collective-permute-done | bytes 466976 | tf_op jit(solution)/shard_map/ppermute | solution.py:81
  46.0 1.0 copy-done.11
  47.1 1.5 collective-permute-start.9
  49.0 1.2 copy-done.4
  50.2 1.0 copy-done.12
  51.1 11.1 %shard_map.328 = (bf16[1024,2304]{1,0:T(8,128)(2,1)}, bf16[768,2304]{1,0:T(8,128)(2,1)}, bf16[16,1024]{1,0:T(8,128)(2,1)}, f32[8,768]{1,0:T(8,128)}, f32[8,3072]{1,0:T(8,128)}) custom-call(s32[32]{0:T(128)} %pad_add_fusion.ids_ref, bf16[1024,768]{1,0:T(8,128)(2,1)} %x_ref.5, f32[2,8,768]{2,1,0:T(8,128)} %bitcast.20, f32[2,8,768]{2,1,0:T(8,128)} %up_ref.5, ...), custom_call_target="tpu_custom_call" | custom-call | flops 3623878656 | bytes 14680064 | tf_op jit(solution)/shard_map/pallas_call | solution.py:206
  62.2 1.0 constant_dynamic-update-slice_fusion.b0
  63.4 2.5 %collective-permute-start.13 = (bf16[8,64,768]{2,1,0:T(8,128)(2,1)S(1)}, bf16[8,64,768]{2,1,0:T(8,128)(2,1)S(1)}, u32[]{:S(2)}, u32[]{:S(2)}) collective-permute-start(bf16[8,64,768]{2,1,0:T(8,128)(2,1)S(1)} %constant_dynamic-update-slice_fusion.4.d0), channel_id=1, source_target_pairs={{0,4},{1,5},{2,6},{3,7},{4,0},{5,1},{6,2},{7,3},{8,10},{9,11},{10,... | collective-permute-start | bytes 2359304 | tf_op jit(solution)/shard_map/ppermute | solution.py:81
  65.9 7.9 %shard_map.329 = (bf16[1024,768]{1,0:T(8,128)(2,1)}, bf16[24,512,512]{2,1,0:T(8,128)(2,1)}, f32[1024,768]{1,0:T(8,128)}) custom-call(s32[2,512]{1,0:T(2,128)} %seg_ref.3, bf16[1024,2304]{1,0:T(8,128)(2,1)} %get-tuple-element.73.q_ref.k_ref.v_ref, bf16[1024,2304]{1,0:T(8,128)(2,1)} %get-tuple-element.73.q_ref.k_ref.v_ref, ...), custom_call_target="tpu_custom_call" | custom-call | flops 3221225472 | bytes 10485760 | tf_op jit(solution)/shard_map/pallas_call | solution.py:301
  73.9 8.0 %shard_map.330 = (bf16[1024,768]{1,0:T(8,128)(2,1)}, bf16[24,512,512]{2,1,0:T(8,128)(2,1)}, f32[1024,768]{1,0:T(8,128)}) custom-call(s32[2,512]{1,0:T(2,128)} %seg_ref.3, bf16[1024,2304]{1,0:T(8,128)(2,1)} %get-tuple-element.73.q_ref.k_ref.v_ref, ...), custom_call_target="tpu_custom_call", output_to_operand_aliasing={{0}: (4, {}), {1}: (5, {}), {2}: (6, {})} | custom-call | flops 3221225472 | bytes 10485760 | tf_op jit(solution)/shard_map/pallas_call | solution.py:301
  81.8 1.8 %collective-permute-done.13.d1 = bf16[8,64,768]{2,1,0:T(8,128)(2,1)S(1)} collective-permute-done((bf16[8,64,768]{2,1,0:T(8,128)(2,1)S(1)}, bf16[8,64,768]{2,1,0:T(8,128)(2,1)S(1)}, u32[]{:S(2)}, u32[]{:S(2)}) %collective-permute-start.13) | collective-permute-done | bytes 786464 | tf_op jit(solution)/shard_map/ppermute | solution.py:81
  83.6 3.5 %collective-permute-done.12.b1 = bf16[8,24,4864]{2,1,0:T(8,128)(2,1)} collective-permute-done((bf16[8,24,4864]{2,1,0:T(8,128)(2,1)}, bf16[8,24,4864]{2,1,0:T(8,128)(2,1)}, u32[]{:S(2)}, u32[]{:S(2)}) %collective-permute-start.12) | collective-permute-done | bytes 1867808 | tf_op jit(solution)/shard_map/ppermute | solution.py:81
  87.6 0.6 pad_add_fusion.1.ids_d_ref
  88.2 3.6 %collective-permute-done.16.d2 = bf16[8,64,768]{2,1,0:T(8,128)(2,1)} collective-permute-done((bf16[8,64,768]{2,1,0:T(8,128)(2,1)S(1)}, bf16[8,64,768]{2,1,0:T(8,128)(2,1)}, u32[]{:S(2)}, u32[]{:S(2)}) %collective-permute-start.16) | collective-permute-done | bytes 786464 | tf_op jit(solution)/shard_map/ppermute | solution.py:85
  91.8 1.1 collective-permute-done.17.d3
  93.5 36.2 %shard_map.331 = (bf16[1024,768]{1,0:T(8,128)(2,1)}, f32[1024,768]{1,0:T(8,128)}, bf16[1024,768]{1,0:T(8,128)(2,1)}, f32[8,768]{1,0:T(8,128)}) custom-call(s32[32]{0:T(128)} %pad_add_fusion.ids_ref, s32[32]{0:T(128)} %pad_add_fusion.1.ids_d_ref, bf16[1024,768]{1,0:T(8,128)(2,1)} %x_ref.5, bf16[1024,768]{1,0:T(8,128)(2,1)} %cot_ref.1, ...), custom_call_target="tpu_custom_call" | custom-call | flops 21743271936 | bytes 20971520 | tf_op jit(solution)/shard_map/pallas_call | solution.py:480
  129.7 25.1 %shard_map.332 = (f32[1024,768]{1,0:T(8,128)}, f32[40,384]{1,0:T(8,128)}, f32[40,384]{1,0:T(8,128)}) custom-call(s32[1]{0:T(128)} %bitcast.8.core_ref, bf16[1024,768]{1,0:T(8,128)(2,1)} %x_ref.5, bf16[1024,2304]{1,0:T(8,128)(2,1)} %get-tuple-element.73.q_ref.k_ref.v_ref, bf16[1024,2304]{1,0:T(8,128)(2,1)} %get-tuple-element.73.q_ref.k_ref.v_ref, ...), custom_call_target="tpu_custom_call" | custom-call | flops 12884901888 | bytes 29360128 | tf_op jit(solution)/shard_map/pallas_call | solution.py:620
  155.2 1.2 collective-permute-done.18
  156.4 0.8 add.31
  157.2 1.1 collective-permute-start.19
  158.3 2.4 %collective-permute-start.21 = (f32[40,384]{1,0:T(8,128)S(1)}, f32[40,384]{1,0:T(8,128)S(1)}, u32[]{:S(2)}, u32[]{:S(2)}) collective-permute-start(f32[40,384]{1,0:T(8,128)S(1)} %add.31), channel_id=1, source_target_pairs={{0,17},{1,16},{2,19},{3,18},{4,21},{5,20},{6,23},{7,22},{8,25},{9,... | collective-permute-start | bytes 184328 | tf_op jit(solution)/shard_map/ppermute | solution.py:105
  160.7 0.7 collective-permute-done.19
  161.4 2.3 %collective-permute-done.20 = f32[40,384]{1,0:T(8,128)S(1)} collective-permute-done((f32[40,384]{1,0:T(8,128)S(1)}, f32[40,384]{1,0:T(8,128)S(1)}, u32[]{:S(2)}, u32[]{:S(2)}) %collective-permute-start.20) | collective-permute-done | bytes 61472 | tf_op jit(solution)/shard_map/ppermute | solution.py:105
  163.8 2.0 %collective-permute-start.22 = (f32[40,384]{1,0:T(8,128)S(1)}, f32[40,384]{1,0:T(8,128)S(1)}, u32[]{:S(2)}, u32[]{:S(2)}) collective-permute-start(f32[40,384]{1,0:T(8,128)S(1)} %add_add_fusion.1), channel_id=1, source_target_pairs={{0,2},{1,3},{2,0},{3,1},{4,6},{5,7},{6,4},{7,5},{8,10},{9,11},{10,... | collective-permute-start | bytes 184328 | tf_op jit(solution)/shard_map/ppermute | solution.py:105
  165.8 0.7 collective-permute-start.23
  166.5 1.7 collective-permute-start.24
  169.6 2.0 %collective-permute-done.23 = f32[40,384]{1,0:T(8,128)S(1)} collective-permute-done((f32[40,384]{1,0:T(8,128)S(1)}, f32[40,384]{1,0:T(8,128)S(1)}, u32[]{:S(2)}, u32[]{:S(2)}) %collective-permute-start.23) | collective-permute-done | bytes 61472 | tf_op jit(solution)/shard_map/ppermute | solution.py:105
  171.7 1.0 collective-permute-done.24
  172.7 0.7 pad_maximum_fusion.7.scal_ref
  174.0 0.6 copy-done.3
  174.6 1.8 shard_map.333
  (64 shorter events, 3.3 us)
Async XLA Ops:
  0.6 21.4 %copy-start.6 = (s32[16]{0:T(128)S(1)}, s32[16]{0:T(128)}, u32[]{:S(2)}) copy-start(s32[16]{0:T(128)} %constant.32.clone) | copy-start | bytes 196
  0.7 21.4 %copy-start.7 = (s32[16]{0:T(128)S(1)}, s32[16]{0:T(128)}, u32[]{:S(2)}) copy-start(s32[16]{0:T(128)} %constant.33.clone) | copy-start | bytes 196
  0.7 21.4 %copy-start.8 = (s32[16]{0:T(128)S(1)}, s32[16]{0:T(128)}, u32[]{:S(2)}) copy-start(s32[16]{0:T(128)} %constant.34.clone) | copy-start | bytes 196
  0.7 21.3 %copy-start.9 = (s32[16]{0:T(128)S(1)}, s32[16]{0:T(128)}, u32[]{:S(2)}) copy-start(s32[16]{0:T(128)} %constant.35.clone) | copy-start | bytes 196
  2.3 8.6 %collective-permute-start = (bf16[1,24,2432]{2,1,0:T(8,128)(2,1)S(1)}, bf16[1,24,2432]{2,1,0:T(8,128)(2,1)S(1)}, u32[]{:S(2)}, u32[]{:S(2)}) collective-permute-start(bf16[1,24,2432]{2,1,0:T(8,128)(2,1)S(1)} %fusion.5), channel_id=1, source_target_pairs={{0,2},{1,3},{2,0},{3,1},{4,6},{5,7},{6,4},{7,5},{8,12},{9,13},{10,... | collective-permute-start | bytes 350216 | tf_op jit(solution)/shard_map/ppermute | solution.py:81
  6.3 4.6 %collective-permute-start.1 = (bf16[1,64,768]{2,1,0:T(8,128)(2,1)S(1)}, bf16[1,64,768]{2,1,0:T(8,128)(2,1)S(1)}, u32[]{:S(2)}, u32[]{:S(2)}) collective-permute-start(bf16[1,64,768]{2,1,0:T(8,128)(2,1)S(1)} %slice_bitcast_fusion), channel_id=1, source_target_pairs={{0,16},{1,17},{2,18},{3,19},{4,20},{5,21},{6,22},{7,23},{8,9},{9,8... | collective-permute-start | bytes 294920 | tf_op jit(solution)/shard_map/ppermute | solution.py:81
  10.9 9.5 %collective-permute-start.2 = (bf16[2,24,2432]{2,1,0:T(8,128)(2,1)S(1)}, bf16[2,24,2432]{2,1,0:T(8,128)(2,1)S(1)}, u32[]{:S(2)}, u32[]{:S(2)}) collective-permute-start(bf16[2,24,2432]{2,1,0:T(8,128)(2,1)S(1)} %pad_maximum_fusion.5), channel_id=1, source_target_pairs={{0,4},{1,5},{2,6},{3,7},{4,0},{5,1},{6,2},{7,3},{8,10},{9,11},{10,... | collective-permute-start | bytes 700424 | tf_op jit(solution)/shard_map/ppermute | solution.py:81
  13.6 5.7 %collective-permute-start.3 = (bf16[2,64,768]{2,1,0:T(8,128)(2,1)S(1)}, bf16[2,64,768]{2,1,0:T(8,128)(2,1)S(1)}, u32[]{:S(2)}, u32[]{:S(2)}) collective-permute-start(bf16[2,64,768]{2,1,0:T(8,128)(2,1)S(1)} %pad_maximum_fusion.6), channel_id=1, source_target_pairs={{0,1},{1,0},{2,3},{3,2},{4,5},{5,4},{6,7},{7,6},{8,24},{9,25},{10,... | collective-permute-start | bytes 589832 | tf_op jit(solution)/shard_map/ppermute | solution.py:81
  20.4 8.6 %collective-permute-start.4 = (bf16[4,24,2432]{2,1,0:T(8,128)(2,1)S(1)}, bf16[4,24,2432]{2,1,0:T(8,128)(2,1)S(1)}, u32[]{:S(2)}, u32[]{:S(2)}) collective-permute-start(bf16[4,24,2432]{2,1,0:T(8,128)(2,1)S(1)} %pad_maximum_fusion.2), channel_id=1, source_target_pairs={{0,16},{1,17},{2,18},{3,19},{4,20},{5,21},{6,22},{7,23},{8,9},{9,8... | collective-permute-start | bytes 1400840 | tf_op jit(solution)/shard_map/ppermute | solution.py:81
  22.0 7.0 %collective-permute-start.5 = (bf16[1,24,4864]{2,1,0:T(8,128)(2,1)S(1)}, bf16[1,24,4864]{2,1,0:T(8,128)(2,1)S(1)}, u32[]{:S(2)}, u32[]{:S(2)}) collective-permute-start(bf16[1,24,4864]{2,1,0:T(8,128)(2,1)S(1)} %maximum_bitcast_fusion), channel_id=1, source_target_pairs={{0,2},{1,3},{2,0},{3,1},{4,6},{5,7},{6,4},{7,5},{8,12},{9,13},{10,... | collective-permute-start | bytes 700424 | tf_op jit(solution)/shard_map/ppermute | solution.py:81
  29.2 19.4 %copy-start = (bf16[8,24,2432]{2,1,0:T(8,128)(2,1)}, bf16[8,24,2432]{2,1,0:T(8,128)(2,1)S(1)}, u32[]{:S(2)}) copy-start(bf16[8,24,2432]{2,1,0:T(8,128)(2,1)S(1)} %pad_maximum_fusion.p0) | copy-start | bytes 2801668
  29.2 16.8 %collective-permute-start.6 = (bf16[8,24,2432]{2,1,0:T(8,128)(2,1)S(1)}, bf16[8,24,2432]{2,1,0:T(8,128)(2,1)S(1)}, u32[]{:S(2)}, u32[]{:S(2)}) collective-permute-start(bf16[8,24,2432]{2,1,0:T(8,128)(2,1)S(1)} %pad_maximum_fusion.p0), channel_id=1, source_target_pairs={{0,1},{1,0},{2,3},{3,2},{4,5},{5,4},{6,7},{7,6},{8,24},{9,25},{10,... | collective-permute-start | bytes 2801672 | tf_op jit(solution)/shard_map/ppermute | solution.py:81
  31.7 14.3 %collective-permute-start.8 = (bf16[8,24,2432]{2,1,0:T(8,128)(2,1)S(1)}, bf16[8,24,2432]{2,1,0:T(8,128)(2,1)S(1)}, u32[]{:S(2)}, u32[]{:S(2)}) collective-permute-start(bf16[8,24,2432]{2,1,0:T(8,128)(2,1)S(1)} %pad_maximum_fusion.p0), channel_id=1, source_target_pairs={{0,8},{1,9},{2,10},{3,11},{4,12},{5,13},{6,14},{7,15},{8,0},{9,1},... | collective-permute-start | bytes 2801672 | tf_op jit(solution)/shard_map/ppermute | solution.py:85
  31.7 14.3 %collective-permute-start.7 = (bf16[2,24,4864]{2,1,0:T(8,128)(2,1)S(1)}, bf16[2,24,4864]{2,1,0:T(8,128)(2,1)S(1)}, u32[]{:S(2)}, u32[]{:S(2)}) collective-permute-start(bf16[2,24,4864]{2,1,0:T(8,128)(2,1)S(1)} %pad_maximum_fusion.3), channel_id=1, source_target_pairs={{0,4},{1,5},{2,6},{3,7},{4,0},{5,1},{6,2},{7,3},{8,10},{9,11},{10,... | collective-permute-start | bytes 1400840 | tf_op jit(solution)/shard_map/ppermute | solution.py:81
  46.0 4.2 %copy-start.10 = (bf16[8,24,2432]{2,1,0:T(8,128)(2,1)}, bf16[8,24,2432]{2,1,0:T(8,128)(2,1)S(1)}, u32[]{:S(2)}) copy-start(bf16[8,24,2432]{2,1,0:T(8,128)(2,1)S(1)} %collective-permute-done.6.p1) | copy-start | bytes 2801668
  46.0 1.0 copy-start.11
  47.0 3.2 %collective-permute-start.11 = (bf16[8,24,2432]{2,1,0:T(8,128)(2,1)S(1)}, bf16[8,24,2432]{2,1,0:T(8,128)(2,1)S(1)}, u32[]{:S(2)}, u32[]{:S(2)}) collective-permute-start(bf16[8,24,2432]{2,1,0:T(8,128)(2,1)S(1)} %collective-permute-done.6.p1), channel_id=1, source_target_pairs={{0,8},{1,9},{2,10},{3,11},{4,12},{5,13},{6,14},{7,15},{8,0},{9,1},... | collective-permute-start | bytes 2801672 | tf_op jit(solution)/shard_map/ppermute | solution.py:85
  47.1 15.1 %collective-permute-start.9 = (bf16[4,24,4864]{2,1,0:T(8,128)(2,1)S(1)}, bf16[4,24,4864]{2,1,0:T(8,128)(2,1)S(1)}, u32[]{:S(2)}, u32[]{:S(2)}) collective-permute-start(bf16[4,24,4864]{2,1,0:T(8,128)(2,1)S(1)} %pad_maximum_fusion.1), channel_id=1, source_target_pairs={{0,16},{1,17},{2,18},{3,19},{4,20},{5,21},{6,22},{7,23},{8,9},{9,8... | collective-permute-start | bytes 2801672 | tf_op jit(solution)/shard_map/ppermute | solution.py:81
  48.6 13.6 %collective-permute-start.10 = (bf16[4,64,768]{2,1,0:T(8,128)(2,1)S(1)}, bf16[4,64,768]{2,1,0:T(8,128)(2,1)S(1)}, u32[]{:S(2)}, u32[]{:S(2)}) collective-permute-start(bf16[4,64,768]{2,1,0:T(8,128)(2,1)S(1)} %pad_maximum_fusion.4), channel_id=1, source_target_pairs={{0,2},{1,3},{2,0},{3,1},{4,6},{5,7},{6,4},{7,5},{8,12},{9,13},{10,... | collective-permute-start | bytes 1179656 | tf_op jit(solution)/shard_map/ppermute | solution.py:81
  48.9 1.2 copy-start.4
  50.2 1.0 copy-start.12
  63.2 23.9 %collective-permute-start.12 = (bf16[8,24,4864]{2,1,0:T(8,128)(2,1)}, bf16[8,24,4864]{2,1,0:T(8,128)(2,1)}, u32[]{:S(2)}, u32[]{:S(2)}) collective-permute-start(bf16[8,24,4864]{2,1,0:T(8,128)(2,1)} %constant_dynamic-update-slice_fusion.b0), channel_id=1, source_target_pairs={{0,1},{1,0},{2,3},{3,2},{4,5},{5,4},{6,7},{7,6},{8,24},{9,25},{10,... | collective-permute-start | bytes 5603336 | tf_op jit(solution)/shard_map/ppermute | solution.py:81
  63.4 23.8 %copy-start.2 = (bf16[8,64,768]{2,1,0:T(8,128)(2,1)}, bf16[8,64,768]{2,1,0:T(8,128)(2,1)S(1)}, u32[]{:S(2)}) copy-start(bf16[8,64,768]{2,1,0:T(8,128)(2,1)S(1)} %constant_dynamic-update-slice_fusion.4.d0) | copy-start | bytes 2359300
  63.4 10.4 %copy-start.5 = (bf16[8,24,4864]{2,1,0:T(8,128)(2,1)S(1)}, bf16[8,24,4864]{2,1,0:T(8,128)(2,1)}, u32[]{:S(2)}) copy-start(bf16[8,24,4864]{2,1,0:T(8,128)(2,1)} %constant_dynamic-update-slice_fusion.b0) | copy-start | bytes 5603332
  63.4 20.2 %collective-permute-start.13 = (bf16[8,64,768]{2,1,0:T(8,128)(2,1)S(1)}, bf16[8,64,768]{2,1,0:T(8,128)(2,1)S(1)}, u32[]{:S(2)}, u32[]{:S(2)}) collective-permute-start(bf16[8,64,768]{2,1,0:T(8,128)(2,1)S(1)} %constant_dynamic-update-slice_fusion.4.d0), channel_id=1, source_target_pairs={{0,4},{1,5},{2,6},{3,7},{4,0},{5,1},{6,2},{7,3},{8,10},{9,11},{10,... | collective-permute-start | bytes 2359304 | tf_op jit(solution)/shard_map/ppermute | solution.py:81
  73.8 18.0 %collective-permute-start.14 = (bf16[8,24,4864]{2,1,0:T(8,128)(2,1)S(1)}, bf16[8,24,4864]{2,1,0:T(8,128)(2,1)}, u32[]{:S(2)}, u32[]{:S(2)}) collective-permute-start(bf16[8,24,4864]{2,1,0:T(8,128)(2,1)S(1)} %copy-done.5), channel_id=1, source_target_pairs={{0,8},{1,9},{2,10},{3,11},{4,12},{5,13},{6,14},{7,15},{8,0},{9,1},... | collective-permute-start | bytes 5603336 | tf_op jit(solution)/shard_map/ppermute | solution.py:85
  83.6 9.9 %copy-start.13 = (bf16[8,64,768]{2,1,0:T(8,128)(2,1)}, bf16[8,64,768]{2,1,0:T(8,128)(2,1)S(1)}, u32[]{:S(2)}) copy-start(bf16[8,64,768]{2,1,0:T(8,128)(2,1)S(1)} %collective-permute-done.13.d1) | copy-start | bytes 2359300
  87.1 6.4 %collective-permute-start.15 = (bf16[8,24,4864]{2,1,0:T(8,128)(2,1)}, bf16[8,24,4864]{2,1,0:T(8,128)(2,1)}, u32[]{:S(2)}, u32[]{:S(2)}) collective-permute-start(bf16[8,24,4864]{2,1,0:T(8,128)(2,1)} %collective-permute-done.12.b1), channel_id=1, source_target_pairs={{0,8},{1,9},{2,10},{3,11},{4,12},{5,13},{6,14},{7,15},{8,0},{9,1},... | collective-permute-start | bytes 5603336 | tf_op jit(solution)/shard_map/ppermute | solution.py:85
  87.1 4.7 %collective-permute-start.16 = (bf16[8,64,768]{2,1,0:T(8,128)(2,1)S(1)}, bf16[8,64,768]{2,1,0:T(8,128)(2,1)}, u32[]{:S(2)}, u32[]{:S(2)}) collective-permute-start(bf16[8,64,768]{2,1,0:T(8,128)(2,1)S(1)} %constant_dynamic-update-slice_fusion.4.d0), channel_id=1, source_target_pairs={{0,8},{1,9},{2,10},{3,11},{4,12},{5,13},{6,14},{7,15},{8,0},{9,1},... | collective-permute-start | bytes 2359304 | tf_op jit(solution)/shard_map/ppermute | solution.py:85
  87.6 5.3 %collective-permute-start.17 = (bf16[8,64,768]{2,1,0:T(8,128)(2,1)S(1)}, bf16[8,64,768]{2,1,0:T(8,128)(2,1)}, u32[]{:S(2)}, u32[]{:S(2)}) collective-permute-start(bf16[8,64,768]{2,1,0:T(8,128)(2,1)S(1)} %collective-permute-done.13.d1), channel_id=1, source_target_pairs={{0,8},{1,9},{2,10},{3,11},{4,12},{5,13},{6,14},{7,15},{8,0},{9,1},... | collective-permute-start | bytes 2359304 | tf_op jit(solution)/shard_map/ppermute | solution.py:85
  154.8 1.5 collective-permute-start.18
  157.2 4.2 %collective-permute-start.19 = (f32[40,384]{1,0:T(8,128)S(1)}, f32[40,384]{1,0:T(8,128)S(1)}, u32[]{:S(2)}, u32[]{:S(2)}) collective-permute-start(f32[40,384]{1,0:T(8,128)S(1)} %add.31), channel_id=1, source_target_pairs={{0,16},{1,17},{2,18},{3,19},{4,20},{5,21},{6,22},{7,23},{8,24},{9,... | collective-permute-start | bytes 184328 | tf_op jit(solution)/shard_map/ppermute | solution.py:105
  158.3 5.4 %collective-permute-start.20 = (f32[40,384]{1,0:T(8,128)S(1)}, f32[40,384]{1,0:T(8,128)S(1)}, u32[]{:S(2)}, u32[]{:S(2)}) collective-permute-start(f32[40,384]{1,0:T(8,128)S(1)} %add.31), channel_id=1, source_target_pairs={{0,1},{1,0},{2,3},{3,2},{4,5},{5,4},{6,7},{7,6},{8,9},{9,8},{10,11... | collective-permute-start | bytes 184328 | tf_op jit(solution)/shard_map/ppermute | solution.py:105
  158.3 5.4 %collective-permute-start.21 = (f32[40,384]{1,0:T(8,128)S(1)}, f32[40,384]{1,0:T(8,128)S(1)}, u32[]{:S(2)}, u32[]{:S(2)}) collective-permute-start(f32[40,384]{1,0:T(8,128)S(1)} %add.31), channel_id=1, source_target_pairs={{0,17},{1,16},{2,19},{3,18},{4,21},{5,20},{6,23},{7,22},{8,25},{9,... | collective-permute-start | bytes 184328 | tf_op jit(solution)/shard_map/ppermute | solution.py:105
  163.8 5.8 %collective-permute-start.22 = (f32[40,384]{1,0:T(8,128)S(1)}, f32[40,384]{1,0:T(8,128)S(1)}, u32[]{:S(2)}, u32[]{:S(2)}) collective-permute-start(f32[40,384]{1,0:T(8,128)S(1)} %add_add_fusion.1), channel_id=1, source_target_pairs={{0,2},{1,3},{2,0},{3,1},{4,6},{5,7},{6,4},{7,5},{8,10},{9,11},{10,... | collective-permute-start | bytes 184328 | tf_op jit(solution)/shard_map/ppermute | solution.py:105
  165.8 5.9 %collective-permute-start.23 = (f32[40,384]{1,0:T(8,128)S(1)}, f32[40,384]{1,0:T(8,128)S(1)}, u32[]{:S(2)}, u32[]{:S(2)}) collective-permute-start(f32[40,384]{1,0:T(8,128)S(1)} %add_add_fusion.1), channel_id=1, source_target_pairs={{0,4},{1,5},{2,6},{3,7},{4,0},{5,1},{6,2},{7,3},{8,12},{9,13},{10,... | collective-permute-start | bytes 184328 | tf_op jit(solution)/shard_map/ppermute | solution.py:105
  166.5 6.1 %collective-permute-start.24 = (f32[40,384]{1,0:T(8,128)S(1)}, f32[40,384]{1,0:T(8,128)S(1)}, u32[]{:S(2)}, u32[]{:S(2)}) collective-permute-start(f32[40,384]{1,0:T(8,128)S(1)} %add_add_fusion.1), channel_id=1, source_target_pairs={{0,6},{1,7},{2,4},{3,5},{4,2},{5,3},{6,0},{7,1},{8,14},{9,15},{10,... | collective-permute-start | bytes 184328 | tf_op jit(solution)/shard_map/ppermute | solution.py:105
  172.6 1.3 copy-start.1
  172.7 1.3 collective-permute-start.25
  174.0 0.6 copy-start.3

commit v4 on v3

--- a/solution.py
+++ b/solution.py
@@ -233,7 +233,7 @@
             pltpu.SemaphoreType.DMA((shards,)),
             pltpu.SemaphoreType.DMA(()),
         ],
-        compiler_params=pltpu.CompilerParams(vmem_limit_bytes=VMEM_LIMIT),
+        compiler_params=pltpu.CompilerParams(vmem_limit_bytes=58 * MIB),
         cost_estimate=pl.CostEstimate(
             flops=2 * rows * width * width * 3, bytes_accessed=14 * MIB, transcendentals=0
         ),
@@ -345,10 +345,10 @@
 
 ROW_TILE = 256
 ROW_TILES = 2
-ROW_LAG = 12
+ROW_LAG = 8
 PIECE = 64
 SIDE = 256
-FF_CHUNK = 512
+FF_CHUNK = 1024
 
 
 def fold(value):
@@ -697,6 +697,7 @@
         functools.partial(adamw_kernel, count),
         in_specs=[smem, smem] + [vmem] * 8,
         out_shape=[like, like, pair, pair] + [like] * 6,
+        compiler_params=pltpu.CompilerParams(vmem_limit_bytes=16 * MIB),
     )(scalars, core, mine, other, down, up, dm, dv, um, uv)
 
 
@@ -817,7 +818,11 @@
         b4 = stage(b, layout, zf, 3)
         d = join(d, d3)
         d4 = stage(d, layout, zl, 3)
+    step_counter = step[0].astype(f32)
+    scalars = jnp.stack([1.0 - beta_one**step_counter, 1.0 - beta_two**step_counter, rate[0]])
+    core = jnp.reshape((lax.axis_index(AXES) & layout.core) != 0, (1,)).astype(jnp.int32)
     half = attend(0, document_numbers, qkv)
+    ids_d, scalars, core, *half = together(ids_d, scalars, core, *half)
     if fast:
         b5 = swap_cores(after(b, *half), layout)
         d5 = swap_cores(after(d, *half), layout)
@@ -831,7 +836,6 @@
     activations, grad_mid, grad_context, sums = row_local(
         ids, ids_d, tokens, cotangent, context, small_rows, inner_rows, parts_b, parts_d
     )
-    core = jnp.reshape((lax.axis_index(AXES) & layout.core) != 0, (1,)).astype(jnp.int32)
     input_grad, keep, send = attend_back(
         core, tokens, qkv, context, grad_context, inverse, attention, up, red, sums, grad_mid, down, weight
     )
@@ -839,8 +843,6 @@
     total = exchange(total, layout, layout.x_bits + layout.y_bits)
     total = exchange(total, layout, layout.z_bits)
     other = swap_cores(total, layout)
-    step_counter = step[0].astype(f32)
-    scalars = jnp.stack([1.0 - beta_one**step_counter, 1.0 - beta_two**step_counter, rate[0]])
     gd, gu, gain_grad, shift_grad, pd, pu, dm, dv, um, uv = adamw(
         layout.n,
         scalars,

time: 177 us -> 176 us (level)
    ppermute x12, waiting for transfers between devices: 31.7 us -> 29 us  [stage(): return lax.ppermute(held, AXES, layout.stage_pairs(orders, t))]
    ppermute x6, waiting for transfers between devices: 6.07 us -> 8.11 us  [exchange(): lax.ppermute(total, AXES, layout.pairs(c))]
    unnamed x32 -> x40, local copies, waits for them, and re-layouts: 3.92 us -> 3.44 us
  transfers between devices with their start and end apart: 26 -> 26, of which waited for: 16 -> 18; matrix products, arithmetic and copies ran while one was open for 3% -> 4% of each run, Pallas kernels for 15% -> 15%
where the time goes in v4:
time: 176 us
  Pallas kernels  89.6 us (51%)
  waiting for transfers between devices  45.4 us (26%)
  starting transfers between devices  26.3 us (15%)
  local copies, waits for them, and re-layouts  6.84 us (4%)
  other arithmetic  5.02 us (3%)
  between operations  2.44 us (1%)
    pallas_call x1, Pallas kernels, row_local(): pl.pallas_call(rows_kernel, grid=(rows // tile,), in_specs=[pl.BlockSpec(...  34.8 us
    ppermute x12, waiting for transfers between devices, stage(): return lax.ppermute(held, AXES, layout.stage_pairs(orders, t))  29 us
    pallas_call x1, Pallas kernels, attend_back(): pl.pallas_call(attend_back_kernel, grid=(rows // length, steps), in_specs...  26.5 us
    ppermute x12, starting transfers between devices, stage(): return lax.ppermute(held, AXES, layout.stage_pairs(orders, t))  17.3 us
    pallas_call x2, Pallas kernels, attend(): pl.pallas_call(functools.partial(attend_kernel, pack), grid=(steps,), in_...  16 us
    pallas_call x1, Pallas kernels, project(): pl.pallas_call(project_kernel, grid=(rows // tile,), in_specs=[pl.BlockSp...  11.1 us
    ppermute x8, waiting for transfers between devices, swap_cores(): return lax.ppermute(value, AXES, layout.core_pairs())  8.25 us
    ppermute x6, waiting for transfers between devices, exchange(): lax.ppermute(total, AXES, layout.pairs(c))  8.11 us
  transfers between devices with their start and end apart: 26, of which 18 were waited for; matrix products, arithmetic and copies ran while one was open for 4% of the time, Pallas kernels for 15%

profile of v4, /device:TPU:0, one launch (start us, length us, event | category | flops | bytes accessed | tf_op | source)
XLA Modules:
  0.0 175.6 jit_solution(9275047722648020399)
XLA Ops:
  0.7 0.7 fusion.10
  1.4 0.8 fusion.5
  2.3 3.1 %collective-permute-start = (bf16[1,24,2432]{2,1,0:T(8,128)(2,1)S(1)}, bf16[1,24,2432]{2,1,0:T(8,128)(2,1)S(1)}, u32[]{:S(2)}, u32[]{:S(2)}) collective-permute-start(bf16[1,24,2432]{2,1,0:T(8,128)(2,1)S(1)} %fusion.5), channel_id=1, source_target_pairs={{0,2},{1,3},{2,0},{3,1},{4,6},{5,7},{6,4},{7,5},{8,12},{9,13},{10,... | collective-permute-start | bytes 350216 | tf_op jit(solution)/shard_map/ppermute | solution.py:81
  5.4 0.9 slice_bitcast_fusion
  6.3 1.5 collective-permute-start.1
  7.7 0.8 slice.13
  8.5 0.7 slice.14
  9.2 1.6 collective-permute-done.1
  10.9 2.7 %collective-permute-start.2 = (bf16[2,24,2432]{2,1,0:T(8,128)(2,1)S(1)}, bf16[2,24,2432]{2,1,0:T(8,128)(2,1)S(1)}, u32[]{:S(2)}, u32[]{:S(2)}) collective-permute-start(bf16[2,24,2432]{2,1,0:T(8,128)(2,1)S(1)} %pad_maximum_fusion.5), channel_id=1, source_target_pairs={{0,4},{1,5},{2,6},{3,7},{4,0},{5,1},{6,2},{7,3},{8,10},{9,11},{10,... | collective-permute-start | bytes 700424 | tf_op jit(solution)/shard_map/ppermute | solution.py:81
  13.6 1.6 collective-permute-start.3
  15.2 0.9 maximum_bitcast_fusion
  16.1 3.2 %collective-permute-done.3 = bf16[2,64,768]{2,1,0:T(8,128)(2,1)S(1)} collective-permute-done((bf16[2,64,768]{2,1,0:T(8,128)(2,1)S(1)}, bf16[2,64,768]{2,1,0:T(8,128)(2,1)S(1)}, u32[]{:S(2)}, u32[]{:S(2)}) %collective-permute-start.3) | collective-permute-done | bytes 196640 | tf_op jit(solution)/shard_map/ppermute | solution.py:81
  19.3 1.1 collective-permute-done.2
  20.4 1.6 collective-permute-start.4
  22.8 6.3 %collective-permute-done.5 = bf16[1,24,4864]{2,1,0:T(8,128)(2,1)S(1)} collective-permute-done((bf16[1,24,4864]{2,1,0:T(8,128)(2,1)S(1)}, bf16[1,24,4864]{2,1,0:T(8,128)(2,1)S(1)}, u32[]{:S(2)}, u32[]{:S(2)}) %collective-permute-start.5) | collective-permute-done | bytes 233504 | tf_op jit(solution)/shard_map/ppermute | solution.py:81
  29.2 2.5 %collective-permute-start.6 = (bf16[8,24,2432]{2,1,0:T(8,128)(2,1)S(1)}, bf16[8,24,2432]{2,1,0:T(8,128)(2,1)S(1)}, u32[]{:S(2)}, u32[]{:S(2)}) collective-permute-start(bf16[8,24,2432]{2,1,0:T(8,128)(2,1)S(1)} %pad_maximum_fusion.p0), channel_id=1, source_target_pairs={{0,1},{1,0},{2,3},{3,2},{4,5},{5,4},{6,7},{7,6},{8,24},{9,25},{10,... | collective-permute-start | bytes 2801672 | tf_op jit(solution)/shard_map/ppermute | solution.py:81
  31.8 0.7 constant_dynamic-update-slice_fusion.3
  32.5 13.5 %collective-permute-done.7 = bf16[2,24,4864]{2,1,0:T(8,128)(2,1)S(1)} collective-permute-done((bf16[2,24,4864]{2,1,0:T(8,128)(2,1)S(1)}, bf16[2,24,4864]{2,1,0:T(8,128)(2,1)S(1)}, u32[]{:S(2)}, u32[]{:S(2)}) %collective-permute-start.7) | collective-permute-done | bytes 466976 | tf_op jit(solution)/shard_map/ppermute | solution.py:81
  46.2 1.5 collective-permute-start.9
  47.7 0.7 constant_dynamic-update-slice_fusion.2
  48.7 0.8 constant_dynamic-update-slice_fusion.1
  49.5 0.9 copy-done.14
  50.4 11.1 %shard_map.328 = (bf16[1024,2304]{1,0:T(8,128)(2,1)}, bf16[768,2304]{1,0:T(8,128)(2,1)}, bf16[16,1024]{1,0:T(8,128)(2,1)}, f32[8,768]{1,0:T(8,128)}, f32[8,3072]{1,0:T(8,128)}) custom-call(s32[32]{0:T(128)} %pad_add_fusion.ids_ref, bf16[1024,768]{1,0:T(8,128)(2,1)} %x_ref.5, f32[2,8,768]{2,1,0:T(8,128)} %bitcast.20, f32[2,8,768]{2,1,0:T(8,128)} %up_ref.5, ...), custom_call_target="tpu_custom_call" | custom-call | flops 3623878656 | bytes 14680064 | tf_op jit(solution)/shard_map/pallas_call | solution.py:206
  61.5 1.0 constant_dynamic-update-slice_fusion.b0
  64.0 2.5 %collective-permute-start.13 = (bf16[8,64,768]{2,1,0:T(8,128)(2,1)S(1)}, bf16[8,64,768]{2,1,0:T(8,128)(2,1)S(1)}, u32[]{:S(2)}, u32[]{:S(2)}) collective-permute-start(bf16[8,64,768]{2,1,0:T(8,128)(2,1)S(1)} %constant_dynamic-update-slice_fusion.4.d0), channel_id=1, source_target_pairs={{0,4},{1,5},{2,6},{3,7},{4,0},{5,1},{6,2},{7,3},{8,10},{9,11},{10,... | collective-permute-start | bytes 2359304 | tf_op jit(solution)/shard_map/ppermute | solution.py:81
  67.2 8.0 %shard_map.329 = (bf16[1024,768]{1,0:T(8,128)(2,1)}, bf16[24,512,512]{2,1,0:T(8,128)(2,1)}, f32[1024,768]{1,0:T(8,128)}) custom-call(s32[2,512]{1,0:T(2,128)} %seg_ref.3, bf16[1024,2304]{1,0:T(8,128)(2,1)} %get-tuple-element.77.q_ref.k_ref.v_ref, bf16[1024,2304]{1,0:T(8,128)(2,1)} %get-tuple-element.77.q_ref.k_ref.v_ref, ...), custom_call_target="tpu_custom_call" | custom-call | flops 3221225472 | bytes 10485760 | tf_op jit(solution)/shard_map/pallas_call | solution.py:301
  75.2 8.0 %shard_map.330 = (bf16[1024,768]{1,0:T(8,128)(2,1)}, bf16[24,512,512]{2,1,0:T(8,128)(2,1)}, f32[1024,768]{1,0:T(8,128)}) custom-call(s32[2,512]{1,0:T(2,128)} %seg_ref.3, bf16[1024,2304]{1,0:T(8,128)(2,1)} %get-tuple-element.77.q_ref.k_ref.v_ref, ...), custom_call_target="tpu_custom_call", output_to_operand_aliasing={{0}: (4, {}), {1}: (5, {}), {2}: (6, {})} | custom-call | flops 3221225472 | bytes 10485760 | tf_op jit(solution)/shard_map/pallas_call | solution.py:301
  83.2 1.1 collective-permute-done.13.d1
  84.3 2.1 %collective-permute-done.12.b1 = bf16[8,24,4864]{2,1,0:T(8,128)(2,1)} collective-permute-done((bf16[8,24,4864]{2,1,0:T(8,128)(2,1)}, bf16[8,24,4864]{2,1,0:T(8,128)(2,1)}, u32[]{:S(2)}, u32[]{:S(2)}) %collective-permute-start.12) | collective-permute-done | bytes 1867808 | tf_op jit(solution)/shard_map/ppermute | solution.py:81
  86.9 4.1 %collective-permute-done.16.d2 = bf16[8,64,768]{2,1,0:T(8,128)(2,1)S(1)} collective-permute-done((bf16[8,64,768]{2,1,0:T(8,128)(2,1)S(1)}, bf16[8,64,768]{2,1,0:T(8,128)(2,1)S(1)}, u32[]{:S(2)}, u32[]{:S(2)}) %collective-permute-start.16) | collective-permute-done | bytes 786464 | tf_op jit(solution)/shard_map/ppermute | solution.py:85
  91.0 1.1 collective-permute-done.17.d3
  93.0 34.8 %shard_map.331 = (bf16[1024,768]{1,0:T(8,128)(2,1)}, f32[1024,768]{1,0:T(8,128)}, bf16[1024,768]{1,0:T(8,128)(2,1)}, f32[8,768]{1,0:T(8,128)}) custom-call(s32[32]{0:T(128)} %pad_add_fusion.ids_ref, s32[32]{0:T(128)} %pad_add_fusion.1.ids_d_ref, bf16[1024,768]{1,0:T(8,128)(2,1)} %x_ref.5, bf16[1024,768]{1,0:T(8,128)(2,1)} %cot_ref.1, ...), custom_call_target="tpu_custom_call" | custom-call | flops 21743271936 | bytes 20971520 | tf_op jit(solution)/shard_map/pallas_call | solution.py:480
  127.9 26.5 %shard_map.332 = (f32[1024,768]{1,0:T(8,128)}, f32[40,384]{1,0:T(8,128)}, f32[40,384]{1,0:T(8,128)}) custom-call(s32[1]{0:T(128)} %bitcast.core_ref, bf16[1024,768]{1,0:T(8,128)(2,1)} %x_ref.5, bf16[1024,2304]{1,0:T(8,128)(2,1)} %get-tuple-element.77.q_ref.k_ref.v_ref, bf16[1024,2304]{1,0:T(8,128)(2,1)} %get-tuple-element.77.q_ref.k_ref.v_ref, ...), custom_call_target="tpu_custom_call" | custom-call | flops 12884901888 | bytes 29360128 | tf_op jit(solution)/shard_map/pallas_call | solution.py:620
  154.8 1.1 collective-permute-done.18
  155.9 0.8 add.31
  156.7 1.0 collective-permute-start.19
  157.8 1.2 collective-permute-start.20
  159.0 1.2 collective-permute-start.21
  160.2 0.8 collective-permute-done.19
  161.0 1.0 collective-permute-done.20
  162.0 2.1 %collective-permute-done.21 = f32[40,384]{1,0:T(8,128)S(1)} collective-permute-done((f32[40,384]{1,0:T(8,128)S(1)}, f32[40,384]{1,0:T(8,128)S(1)}, u32[]{:S(2)}, u32[]{:S(2)}) %collective-permute-start.21) | collective-permute-done | bytes 61472 | tf_op jit(solution)/shard_map/ppermute | solution.py:105
  164.1 1.2 collective-permute-start.22
  165.3 1.5 collective-permute-start.23
  166.8 1.8 %collective-permute-start.24 = (f32[40,384]{1,0:T(8,128)S(1)}, f32[40,384]{1,0:T(8,128)S(1)}, u32[]{:S(2)}, u32[]{:S(2)}) collective-permute-start(f32[40,384]{1,0:T(8,128)S(1)} %add_add_fusion.1), channel_id=1, source_target_pairs={{0,6},{1,7},{2,4},{3,5},{4,2},{5,3},{6,0},{7,1},{8,14},{9,15},{10,... | collective-permute-start | bytes 184328 | tf_op jit(solution)/shard_map/ppermute | solution.py:105
  168.8 2.6 %collective-permute-done.23 = f32[40,384]{1,0:T(8,128)S(1)} collective-permute-done((f32[40,384]{1,0:T(8,128)S(1)}, f32[40,384]{1,0:T(8,128)S(1)}, u32[]{:S(2)}, u32[]{:S(2)}) %collective-permute-start.23) | collective-permute-done | bytes 61472 | tf_op jit(solution)/shard_map/ppermute | solution.py:105
  171.4 1.4 collective-permute-done.24
  172.9 1.2 collective-permute-done.25.other_ref
  174.2 1.3 shard_map.333
  (72 shorter events, 4.5 us)
Async XLA Ops:
  0.6 21.4 %copy-start.8 = (s32[16]{0:T(128)S(1)}, s32[16]{0:T(128)}, u32[]{:S(2)}) copy-start(s32[16]{0:T(128)} %constant.32.clone) | copy-start | bytes 196
  0.7 21.4 %copy-start.9 = (s32[16]{0:T(128)S(1)}, s32[16]{0:T(128)}, u32[]{:S(2)}) copy-start(s32[16]{0:T(128)} %constant.33.clone) | copy-start | bytes 196
  0.7 21.4 %copy-start.10 = (s32[16]{0:T(128)S(1)}, s32[16]{0:T(128)}, u32[]{:S(2)}) copy-start(s32[16]{0:T(128)} %constant.34.clone) | copy-start | bytes 196
  0.7 21.3 %copy-start.11 = (s32[16]{0:T(128)S(1)}, s32[16]{0:T(128)}, u32[]{:S(2)}) copy-start(s32[16]{0:T(128)} %constant.35.clone) | copy-start | bytes 196
  2.3 8.6 %collective-permute-start = (bf16[1,24,2432]{2,1,0:T(8,128)(2,1)S(1)}, bf16[1,24,2432]{2,1,0:T(8,128)(2,1)S(1)}, u32[]{:S(2)}, u32[]{:S(2)}) collective-permute-start(bf16[1,24,2432]{2,1,0:T(8,128)(2,1)S(1)} %fusion.5), channel_id=1, source_target_pairs={{0,2},{1,3},{2,0},{3,1},{4,6},{5,7},{6,4},{7,5},{8,12},{9,13},{10,... | collective-permute-start | bytes 350216 | tf_op jit(solution)/shard_map/ppermute | solution.py:81
  6.3 4.6 %collective-permute-start.1 = (bf16[1,64,768]{2,1,0:T(8,128)(2,1)S(1)}, bf16[1,64,768]{2,1,0:T(8,128)(2,1)S(1)}, u32[]{:S(2)}, u32[]{:S(2)}) collective-permute-start(bf16[1,64,768]{2,1,0:T(8,128)(2,1)S(1)} %slice_bitcast_fusion), channel_id=1, source_target_pairs={{0,16},{1,17},{2,18},{3,19},{4,20},{5,21},{6,22},{7,23},{8,9},{9,8... | collective-permute-start | bytes 294920 | tf_op jit(solution)/shard_map/ppermute | solution.py:81
  10.9 9.5 %collective-permute-start.2 = (bf16[2,24,2432]{2,1,0:T(8,128)(2,1)S(1)}, bf16[2,24,2432]{2,1,0:T(8,128)(2,1)S(1)}, u32[]{:S(2)}, u32[]{:S(2)}) collective-permute-start(bf16[2,24,2432]{2,1,0:T(8,128)(2,1)S(1)} %pad_maximum_fusion.5), channel_id=1, source_target_pairs={{0,4},{1,5},{2,6},{3,7},{4,0},{5,1},{6,2},{7,3},{8,10},{9,11},{10,... | collective-permute-start | bytes 700424 | tf_op jit(solution)/shard_map/ppermute | solution.py:81
  13.6 5.7 %collective-permute-start.3 = (bf16[2,64,768]{2,1,0:T(8,128)(2,1)S(1)}, bf16[2,64,768]{2,1,0:T(8,128)(2,1)S(1)}, u32[]{:S(2)}, u32[]{:S(2)}) collective-permute-start(bf16[2,64,768]{2,1,0:T(8,128)(2,1)S(1)} %pad_maximum_fusion.6), channel_id=1, source_target_pairs={{0,1},{1,0},{2,3},{3,2},{4,5},{5,4},{6,7},{7,6},{8,24},{9,25},{10,... | collective-permute-start | bytes 589832 | tf_op jit(solution)/shard_map/ppermute | solution.py:81
  20.4 8.6 %collective-permute-start.4 = (bf16[4,24,2432]{2,1,0:T(8,128)(2,1)S(1)}, bf16[4,24,2432]{2,1,0:T(8,128)(2,1)S(1)}, u32[]{:S(2)}, u32[]{:S(2)}) collective-permute-start(bf16[4,24,2432]{2,1,0:T(8,128)(2,1)S(1)} %pad_maximum_fusion.2), channel_id=1, source_target_pairs={{0,16},{1,17},{2,18},{3,19},{4,20},{5,21},{6,22},{7,23},{8,9},{9,8... | collective-permute-start | bytes 1400840 | tf_op jit(solution)/shard_map/ppermute | solution.py:81
  22.0 7.0 %collective-permute-start.5 = (bf16[1,24,4864]{2,1,0:T(8,128)(2,1)S(1)}, bf16[1,24,4864]{2,1,0:T(8,128)(2,1)S(1)}, u32[]{:S(2)}, u32[]{:S(2)}) collective-permute-start(bf16[1,24,4864]{2,1,0:T(8,128)(2,1)S(1)} %maximum_bitcast_fusion), channel_id=1, source_target_pairs={{0,2},{1,3},{2,0},{3,1},{4,6},{5,7},{6,4},{7,5},{8,12},{9,13},{10,... | collective-permute-start | bytes 700424 | tf_op jit(solution)/shard_map/ppermute | solution.py:81
  29.2 19.2 %copy-start.6 = (bf16[8,24,2432]{2,1,0:T(8,128)(2,1)}, bf16[8,24,2432]{2,1,0:T(8,128)(2,1)S(1)}, u32[]{:S(2)}) copy-start(bf16[8,24,2432]{2,1,0:T(8,128)(2,1)S(1)} %pad_maximum_fusion.p0) | copy-start | bytes 2801668
  29.2 16.8 %collective-permute-start.6 = (bf16[8,24,2432]{2,1,0:T(8,128)(2,1)S(1)}, bf16[8,24,2432]{2,1,0:T(8,128)(2,1)S(1)}, u32[]{:S(2)}, u32[]{:S(2)}) collective-permute-start(bf16[8,24,2432]{2,1,0:T(8,128)(2,1)S(1)} %pad_maximum_fusion.p0), channel_id=1, source_target_pairs={{0,1},{1,0},{2,3},{3,2},{4,5},{5,4},{6,7},{7,6},{8,24},{9,25},{10,... | collective-permute-start | bytes 2801672 | tf_op jit(solution)/shard_map/ppermute | solution.py:81
  31.7 14.3 %collective-permute-start.8 = (bf16[8,24,2432]{2,1,0:T(8,128)(2,1)S(1)}, bf16[8,24,2432]{2,1,0:T(8,128)(2,1)S(1)}, u32[]{:S(2)}, u32[]{:S(2)}) collective-permute-start(bf16[8,24,2432]{2,1,0:T(8,128)(2,1)S(1)} %pad_maximum_fusion.p0), channel_id=1, source_target_pairs={{0,8},{1,9},{2,10},{3,11},{4,12},{5,13},{6,14},{7,15},{8,0},{9,1},... | collective-permute-start | bytes 2801672 | tf_op jit(solution)/shard_map/ppermute | solution.py:85
  31.7 14.3 %collective-permute-start.7 = (bf16[2,24,4864]{2,1,0:T(8,128)(2,1)S(1)}, bf16[2,24,4864]{2,1,0:T(8,128)(2,1)S(1)}, u32[]{:S(2)}, u32[]{:S(2)}) collective-permute-start(bf16[2,24,4864]{2,1,0:T(8,128)(2,1)S(1)} %pad_maximum_fusion.3), channel_id=1, source_target_pairs={{0,4},{1,5},{2,6},{3,7},{4,0},{5,1},{6,2},{7,3},{8,10},{9,11},{10,... | collective-permute-start | bytes 1400840 | tf_op jit(solution)/shard_map/ppermute | solution.py:81
  46.0 4.4 %copy-start.12 = (bf16[8,24,2432]{2,1,0:T(8,128)(2,1)}, bf16[8,24,2432]{2,1,0:T(8,128)(2,1)S(1)}, u32[]{:S(2)}) copy-start(bf16[8,24,2432]{2,1,0:T(8,128)(2,1)S(1)} %collective-permute-done.6.p1) | copy-start | bytes 2801668
  46.0 4.4 %copy-start.13 = (bf16[8,24,2432]{2,1,0:T(8,128)(2,1)}, bf16[8,24,2432]{2,1,0:T(8,128)(2,1)S(1)}, u32[]{:S(2)}) copy-start(bf16[8,24,2432]{2,1,0:T(8,128)(2,1)S(1)} %collective-permute-done.8.p2) | copy-start | bytes 2801668
  46.0 3.4 %collective-permute-start.11 = (bf16[8,24,2432]{2,1,0:T(8,128)(2,1)S(1)}, bf16[8,24,2432]{2,1,0:T(8,128)(2,1)S(1)}, u32[]{:S(2)}, u32[]{:S(2)}) collective-permute-start(bf16[8,24,2432]{2,1,0:T(8,128)(2,1)S(1)} %collective-permute-done.6.p1), channel_id=1, source_target_pairs={{0,8},{1,9},{2,10},{3,11},{4,12},{5,13},{6,14},{7,15},{8,0},{9,1},... | collective-permute-start | bytes 2801672 | tf_op jit(solution)/shard_map/ppermute | solution.py:85
  46.2 15.3 %collective-permute-start.9 = (bf16[4,24,4864]{2,1,0:T(8,128)(2,1)S(1)}, bf16[4,24,4864]{2,1,0:T(8,128)(2,1)S(1)}, u32[]{:S(2)}, u32[]{:S(2)}) collective-permute-start(bf16[4,24,4864]{2,1,0:T(8,128)(2,1)S(1)} %pad_maximum_fusion.1), channel_id=1, source_target_pairs={{0,16},{1,17},{2,18},{3,19},{4,20},{5,21},{6,22},{7,23},{8,9},{9,8... | collective-permute-start | bytes 2801672 | tf_op jit(solution)/shard_map/ppermute | solution.py:81
  48.4 13.1 %collective-permute-start.10 = (bf16[4,64,768]{2,1,0:T(8,128)(2,1)S(1)}, bf16[4,64,768]{2,1,0:T(8,128)(2,1)S(1)}, u32[]{:S(2)}, u32[]{:S(2)}) collective-permute-start(bf16[4,64,768]{2,1,0:T(8,128)(2,1)S(1)} %pad_maximum_fusion.4), channel_id=1, source_target_pairs={{0,2},{1,3},{2,0},{3,1},{4,6},{5,7},{6,4},{7,5},{8,12},{9,13},{10,... | collective-permute-start | bytes 1179656 | tf_op jit(solution)/shard_map/ppermute | solution.py:81
  49.5 1.0 copy-start.14
  62.5 23.9 %collective-permute-start.12 = (bf16[8,24,4864]{2,1,0:T(8,128)(2,1)}, bf16[8,24,4864]{2,1,0:T(8,128)(2,1)}, u32[]{:S(2)}, u32[]{:S(2)}) collective-permute-start(bf16[8,24,4864]{2,1,0:T(8,128)(2,1)} %constant_dynamic-update-slice_fusion.b0), channel_id=1, source_target_pairs={{0,1},{1,0},{2,3},{3,2},{4,5},{5,4},{6,7},{7,6},{8,24},{9,25},{10,... | collective-permute-start | bytes 5603336 | tf_op jit(solution)/shard_map/ppermute | solution.py:81
  64.0 22.4 %copy-start.7 = (bf16[8,64,768]{2,1,0:T(8,128)(2,1)}, bf16[8,64,768]{2,1,0:T(8,128)(2,1)S(1)}, u32[]{:S(2)}) copy-start(bf16[8,64,768]{2,1,0:T(8,128)(2,1)S(1)} %constant_dynamic-update-slice_fusion.4.d0) | copy-start | bytes 2359300
  64.0 20.2 %collective-permute-start.13 = (bf16[8,64,768]{2,1,0:T(8,128)(2,1)S(1)}, bf16[8,64,768]{2,1,0:T(8,128)(2,1)S(1)}, u32[]{:S(2)}, u32[]{:S(2)}) collective-permute-start(bf16[8,64,768]{2,1,0:T(8,128)(2,1)S(1)} %constant_dynamic-update-slice_fusion.4.d0), channel_id=1, source_target_pairs={{0,4},{1,5},{2,6},{3,7},{4,0},{5,1},{6,2},{7,3},{8,10},{9,11},{10,... | collective-permute-start | bytes 2359304 | tf_op jit(solution)/shard_map/ppermute | solution.py:81
  75.2 15.8 %collective-permute-start.14 = (bf16[8,24,4864]{2,1,0:T(8,128)(2,1)}, bf16[8,24,4864]{2,1,0:T(8,128)(2,1)}, u32[]{:S(2)}, u32[]{:S(2)}) collective-permute-start(bf16[8,24,4864]{2,1,0:T(8,128)(2,1)} %constant_dynamic-update-slice_fusion.b0), channel_id=1, source_target_pairs={{0,8},{1,9},{2,10},{3,11},{4,12},{5,13},{6,14},{7,15},{8,0},{9,1},... | collective-permute-start | bytes 5603336 | tf_op jit(solution)/shard_map/ppermute | solution.py:85
  84.3 8.5 %copy-start.15 = (bf16[8,64,768]{2,1,0:T(8,128)(2,1)}, bf16[8,64,768]{2,1,0:T(8,128)(2,1)S(1)}, u32[]{:S(2)}) copy-start(bf16[8,64,768]{2,1,0:T(8,128)(2,1)S(1)} %collective-permute-done.13.d1) | copy-start | bytes 2359300
  86.4 6.4 %collective-permute-start.15 = (bf16[8,24,4864]{2,1,0:T(8,128)(2,1)}, bf16[8,24,4864]{2,1,0:T(8,128)(2,1)}, u32[]{:S(2)}, u32[]{:S(2)}) collective-permute-start(bf16[8,24,4864]{2,1,0:T(8,128)(2,1)} %collective-permute-done.12.b1), channel_id=1, source_target_pairs={{0,8},{1,9},{2,10},{3,11},{4,12},{5,13},{6,14},{7,15},{8,0},{9,1},... | collective-permute-start | bytes 5603336 | tf_op jit(solution)/shard_map/ppermute | solution.py:85
  86.4 4.6 %collective-permute-start.16 = (bf16[8,64,768]{2,1,0:T(8,128)(2,1)S(1)}, bf16[8,64,768]{2,1,0:T(8,128)(2,1)S(1)}, u32[]{:S(2)}, u32[]{:S(2)}) collective-permute-start(bf16[8,64,768]{2,1,0:T(8,128)(2,1)S(1)} %constant_dynamic-update-slice_fusion.4.d0), channel_id=1, source_target_pairs={{0,8},{1,9},{2,10},{3,11},{4,12},{5,13},{6,14},{7,15},{8,0},{9,1},... | collective-permute-start | bytes 2359304 | tf_op jit(solution)/shard_map/ppermute | solution.py:85
  86.9 5.2 %collective-permute-start.17 = (bf16[8,64,768]{2,1,0:T(8,128)(2,1)S(1)}, bf16[8,64,768]{2,1,0:T(8,128)(2,1)S(1)}, u32[]{:S(2)}, u32[]{:S(2)}) collective-permute-start(bf16[8,64,768]{2,1,0:T(8,128)(2,1)S(1)} %collective-permute-done.13.d1), channel_id=1, source_target_pairs={{0,8},{1,9},{2,10},{3,11},{4,12},{5,13},{6,14},{7,15},{8,0},{9,1},... | collective-permute-start | bytes 2359304 | tf_op jit(solution)/shard_map/ppermute | solution.py:85
  91.0 1.8 %copy-start.16 = (bf16[8,64,768]{2,1,0:T(8,128)(2,1)}, bf16[8,64,768]{2,1,0:T(8,128)(2,1)S(1)}, u32[]{:S(2)}) copy-start(bf16[8,64,768]{2,1,0:T(8,128)(2,1)S(1)} %collective-permute-done.16.d2) | copy-start | bytes 2359300
  92.1 0.9 copy-start.17
  127.8 46.4 %copy-start = (f32[2,768,8]{1,2,0:T(8,128)S(1)}, f32[2,768,8]{1,2,0:T(8,128)}, u32[]{:S(2)}) copy-start(f32[2,768,8]{1,2,0:T(8,128)} %param.37) | copy-start | bytes 147460
  127.8 46.3 %copy-start.1 = (f32[2,8,768]{2,1,0:T(8,128)S(1)}, f32[2,8,768]{2,1,0:T(8,128)}, u32[]{:S(2)}) copy-start(f32[2,8,768]{2,1,0:T(8,128)} %up_ref.5) | copy-start | bytes 147460
  127.8 46.3 %copy-start.2 = (f32[2,768,8]{1,2,0:T(8,128)S(1)}, f32[2,768,8]{1,2,0:T(8,128)}, u32[]{:S(2)}) copy-start(f32[2,768,8]{1,2,0:T(8,128)} %param.39) | copy-start | bytes 147460
  127.8 46.3 %copy-start.3 = (f32[2,768,8]{1,2,0:T(8,128)S(1)}, f32[2,768,8]{1,2,0:T(8,128)}, u32[]{:S(2)}) copy-start(f32[2,768,8]{1,2,0:T(8,128)} %param.40) | copy-start | bytes 147460
  127.8 46.3 %copy-start.4 = (f32[2,8,768]{2,1,0:T(8,128)S(1)}, f32[2,8,768]{2,1,0:T(8,128)}, u32[]{:S(2)}) copy-start(f32[2,8,768]{2,1,0:T(8,128)} %um_ref.1) | copy-start | bytes 147460
  127.9 46.3 %copy-start.5 = (f32[2,8,768]{2,1,0:T(8,128)S(1)}, f32[2,8,768]{2,1,0:T(8,128)}, u32[]{:S(2)}) copy-start(f32[2,8,768]{2,1,0:T(8,128)} %uv_ref.1) | copy-start | bytes 147460
  154.3 1.6 collective-permute-start.18
  156.7 4.3 %collective-permute-start.19 = (f32[40,384]{1,0:T(8,128)S(1)}, f32[40,384]{1,0:T(8,128)S(1)}, u32[]{:S(2)}, u32[]{:S(2)}) collective-permute-start(f32[40,384]{1,0:T(8,128)S(1)} %add.31), channel_id=1, source_target_pairs={{0,16},{1,17},{2,18},{3,19},{4,20},{5,21},{6,22},{7,23},{8,24},{9,... | collective-permute-start | bytes 184328 | tf_op jit(solution)/shard_map/ppermute | solution.py:105
  157.8 4.2 %collective-permute-start.20 = (f32[40,384]{1,0:T(8,128)S(1)}, f32[40,384]{1,0:T(8,128)S(1)}, u32[]{:S(2)}, u32[]{:S(2)}) collective-permute-start(f32[40,384]{1,0:T(8,128)S(1)} %add.31), channel_id=1, source_target_pairs={{0,1},{1,0},{2,3},{3,2},{4,5},{5,4},{6,7},{7,6},{8,9},{9,8},{10,11... | collective-permute-start | bytes 184328 | tf_op jit(solution)/shard_map/ppermute | solution.py:105
  159.0 5.1 %collective-permute-start.21 = (f32[40,384]{1,0:T(8,128)S(1)}, f32[40,384]{1,0:T(8,128)S(1)}, u32[]{:S(2)}, u32[]{:S(2)}) collective-permute-start(f32[40,384]{1,0:T(8,128)S(1)} %add.31), channel_id=1, source_target_pairs={{0,17},{1,16},{2,19},{3,18},{4,21},{5,20},{6,23},{7,22},{8,25},{9,... | collective-permute-start | bytes 184328 | tf_op jit(solution)/shard_map/ppermute | solution.py:105
  164.1 4.7 %collective-permute-start.22 = (f32[40,384]{1,0:T(8,128)S(1)}, f32[40,384]{1,0:T(8,128)S(1)}, u32[]{:S(2)}, u32[]{:S(2)}) collective-permute-start(f32[40,384]{1,0:T(8,128)S(1)} %add_add_fusion.1), channel_id=1, source_target_pairs={{0,2},{1,3},{2,0},{3,1},{4,6},{5,7},{6,4},{7,5},{8,10},{9,11},{10,... | collective-permute-start | bytes 184328 | tf_op jit(solution)/shard_map/ppermute | solution.py:105
  165.3 6.1 %collective-permute-start.23 = (f32[40,384]{1,0:T(8,128)S(1)}, f32[40,384]{1,0:T(8,128)S(1)}, u32[]{:S(2)}, u32[]{:S(2)}) collective-permute-start(f32[40,384]{1,0:T(8,128)S(1)} %add_add_fusion.1), channel_id=1, source_target_pairs={{0,4},{1,5},{2,6},{3,7},{4,0},{5,1},{6,2},{7,3},{8,12},{9,13},{10,... | collective-permute-start | bytes 184328 | tf_op jit(solution)/shard_map/ppermute | solution.py:105
  166.8 6.0 %collective-permute-start.24 = (f32[40,384]{1,0:T(8,128)S(1)}, f32[40,384]{1,0:T(8,128)S(1)}, u32[]{:S(2)}, u32[]{:S(2)}) collective-permute-start(f32[40,384]{1,0:T(8,128)S(1)} %add_add_fusion.1), channel_id=1, source_target_pairs={{0,6},{1,7},{2,4},{3,5},{4,2},{5,3},{6,0},{7,1},{8,14},{9,15},{10,... | collective-permute-start | bytes 184328 | tf_op jit(solution)/shard_map/ppermute | solution.py:105
  172.8 1.3 collective-permute-start.25

commit v5 on v4

--- a/solution.py
+++ b/solution.py
@@ -521,7 +521,7 @@
     )(ids, ids_d, tokens, cotangent, context, small, inner_bias, *parts_b, *parts_d)
 
 
-BACK_LAG = 3
+BACK_LAG = 1
 
 
 def attend_back_kernel(core_ref, x_ref, q_ref, k_ref, v_ref, ctx_ref, dctx_ref, inverse_ref, w_ref, up_ref, red_ref,
@@ -756,9 +756,10 @@
         a, b, d = block_a[None], block_b[None], outer_weight[None, :OUTER_ROWS]
         a1 = stage(a, layout, zf, 0)
         d1 = stage(d, layout, zl, 0)
-        a1, d1 = together(a1, d1)
-        a, d = join(a, a1), join(d, d1)
+        a1, b, d = together(a1, b, d)
+        a = join(a, a1)
         a2 = stage(a, layout, zf, 1)
+        d = join(d, after(d1, a1))
         d2 = stage(d, layout, zl, 1)
         a2, d2, b = together(a2, d2, b)
         a, d = join(a, a2), join(d, d2)

time: 176 us -> 175 us (level)
  transfers between devices with their start and end apart: 26 -> 26, of which waited for: 18 -> 19; matrix products, arithmetic and copies ran while one was open for 4% -> 4% of each run, Pallas kernels for 15% -> 15%
where the time goes in v5:
time: 175 us
  Pallas kernels  89 us (51%)
  waiting for transfers between devices  45.3 us (26%)
  starting transfers between devices  26.1 us (15%)
  local copies, waits for them, and re-layouts  6.84 us (4%)
  other arithmetic  5.02 us (3%)
  between operations  2.45 us (1%)
    pallas_call x1, Pallas kernels, row_local(): pl.pallas_call(rows_kernel, grid=(rows // tile,), in_specs=[pl.BlockSpec(...  34.8 us
    ppermute x12, waiting for transfers between devices, stage(): return lax.ppermute(held, AXES, layout.stage_pairs(orders, t))  29 us
    pallas_call x1, Pallas kernels, attend_back(): pl.pallas_call(attend_back_kernel, grid=(rows // length, steps), in_specs...  25.8 us
    ppermute x12, starting transfers between devices, stage(): return lax.ppermute(held, AXES, layout.stage_pairs(orders, t))  17.1 us
    pallas_call x2, Pallas kernels, attend(): pl.pallas_call(functools.partial(attend_kernel, pack), grid=(steps,), in_...  16 us
    pallas_call x1, Pallas kernels, project(): pl.pallas_call(project_kernel, grid=(rows // tile,), in_specs=[pl.BlockSp...  11.1 us
    ppermute x8, waiting for transfers between devices, swap_cores(): return lax.ppermute(value, AXES, layout.core_pairs())  8.25 us
    ppermute x6, waiting for transfers between devices, exchange(): lax.ppermute(total, AXES, layout.pairs(c))  7.99 us
  transfers between devices with their start and end apart: 26, of which 19 were waited for; matrix products, arithmetic and copies ran while one was open for 4% of the time, Pallas kernels for 15%

profile of v5, /device:TPU:0, one launch (start us, length us, event | category | flops | bytes accessed | tf_op | source)
XLA Modules:
  0.0 174.7 jit_solution(3607731278856667960)
XLA Ops:
  0.7 0.7 fusion.10
  1.4 0.8 fusion.5
  2.3 3.1 %collective-permute-start = (bf16[1,24,2432]{2,1,0:T(8,128)(2,1)S(1)}, bf16[1,24,2432]{2,1,0:T(8,128)(2,1)S(1)}, u32[]{:S(2)}, u32[]{:S(2)}) collective-permute-start(bf16[1,24,2432]{2,1,0:T(8,128)(2,1)S(1)} %fusion.5), channel_id=1, source_target_pairs={{0,2},{1,3},{2,0},{3,1},{4,6},{5,7},{6,4},{7,5},{8,12},{9,13},{10,... | collective-permute-start | bytes 350216 | tf_op jit(solution)/shard_map/ppermute | solution.py:81
  5.4 0.9 slice_bitcast_fusion
  6.3 1.5 collective-permute-start.2
  7.7 0.8 slice.12
  8.5 0.7 slice.13
  9.2 0.9 maximum_bitcast_fusion
  10.9 2.6 %collective-permute-start.1 = (bf16[2,24,2432]{2,1,0:T(8,128)(2,1)S(1)}, bf16[2,24,2432]{2,1,0:T(8,128)(2,1)S(1)}, u32[]{:S(2)}, u32[]{:S(2)}) collective-permute-start(bf16[2,24,2432]{2,1,0:T(8,128)(2,1)S(1)} %pad_maximum_fusion.5), channel_id=1, source_target_pairs={{0,4},{1,5},{2,6},{3,7},{4,0},{5,1},{6,2},{7,3},{8,10},{9,11},{10,... | collective-permute-start | bytes 700424 | tf_op jit(solution)/shard_map/ppermute | solution.py:81
  13.5 1.6 collective-permute-start.3
  15.1 4.2 %collective-permute-done.3 = bf16[2,64,768]{2,1,0:T(8,128)(2,1)S(1)} collective-permute-done((bf16[2,64,768]{2,1,0:T(8,128)(2,1)S(1)}, bf16[2,64,768]{2,1,0:T(8,128)(2,1)S(1)}, u32[]{:S(2)}, u32[]{:S(2)}) %collective-permute-start.3) | collective-permute-done | bytes 196640 | tf_op jit(solution)/shard_map/ppermute | solution.py:81
  19.2 1.1 collective-permute-done.1
  20.4 1.6 collective-permute-start.4
  22.7 6.3 %collective-permute-done.5 = bf16[1,24,4864]{2,1,0:T(8,128)(2,1)S(1)} collective-permute-done((bf16[1,24,4864]{2,1,0:T(8,128)(2,1)S(1)}, bf16[1,24,4864]{2,1,0:T(8,128)(2,1)S(1)}, u32[]{:S(2)}, u32[]{:S(2)}) %collective-permute-start.5) | collective-permute-done | bytes 233504 | tf_op jit(solution)/shard_map/ppermute | solution.py:81
  29.2 2.2 %collective-permute-start.6 = (bf16[8,24,2432]{2,1,0:T(8,128)(2,1)S(1)}, bf16[8,24,2432]{2,1,0:T(8,128)(2,1)S(1)}, u32[]{:S(2)}, u32[]{:S(2)}) collective-permute-start(bf16[8,24,2432]{2,1,0:T(8,128)(2,1)S(1)} %pad_maximum_fusion.p0), channel_id=1, source_target_pairs={{0,1},{1,0},{2,3},{3,2},{4,5},{5,4},{6,7},{7,6},{8,24},{9,25},{10,... | collective-permute-start | bytes 2801672 | tf_op jit(solution)/shard_map/ppermute | solution.py:81
  31.5 0.7 constant_dynamic-update-slice_fusion.3
  32.2 13.6 %collective-permute-done.7 = bf16[2,24,4864]{2,1,0:T(8,128)(2,1)S(1)} collective-permute-done((bf16[2,24,4864]{2,1,0:T(8,128)(2,1)S(1)}, bf16[2,24,4864]{2,1,0:T(8,128)(2,1)S(1)}, u32[]{:S(2)}, u32[]{:S(2)}) %collective-permute-start.7) | collective-permute-done | bytes 466976 | tf_op jit(solution)/shard_map/ppermute | solution.py:81
  46.0 1.5 collective-permute-start.9
  47.5 0.7 constant_dynamic-update-slice_fusion.2
  48.5 0.8 constant_dynamic-update-slice_fusion.1
  49.3 0.9 copy-done.14
  50.3 11.1 %shard_map.328 = (bf16[1024,2304]{1,0:T(8,128)(2,1)}, bf16[768,2304]{1,0:T(8,128)(2,1)}, bf16[16,1024]{1,0:T(8,128)(2,1)}, f32[8,768]{1,0:T(8,128)}, f32[8,3072]{1,0:T(8,128)}) custom-call(s32[32]{0:T(128)} %pad_add_fusion.ids_ref, bf16[1024,768]{1,0:T(8,128)(2,1)} %x_ref.5, f32[2,8,768]{2,1,0:T(8,128)} %bitcast.20, f32[2,8,768]{2,1,0:T(8,128)} %up_ref.5, ...), custom_call_target="tpu_custom_call" | custom-call | flops 3623878656 | bytes 14680064 | tf_op jit(solution)/shard_map/pallas_call | solution.py:206
  61.4 1.0 constant_dynamic-update-slice_fusion.b0
  63.9 2.6 %collective-permute-start.13 = (bf16[8,64,768]{2,1,0:T(8,128)(2,1)S(1)}, bf16[8,64,768]{2,1,0:T(8,128)(2,1)S(1)}, u32[]{:S(2)}, u32[]{:S(2)}) collective-permute-start(bf16[8,64,768]{2,1,0:T(8,128)(2,1)S(1)} %constant_dynamic-update-slice_fusion.4.d0), channel_id=1, source_target_pairs={{0,4},{1,5},{2,6},{3,7},{4,0},{5,1},{6,2},{7,3},{8,10},{9,11},{10,... | collective-permute-start | bytes 2359304 | tf_op jit(solution)/shard_map/ppermute | solution.py:81
  67.2 8.0 %shard_map.329 = (bf16[1024,768]{1,0:T(8,128)(2,1)}, bf16[24,512,512]{2,1,0:T(8,128)(2,1)}, f32[1024,768]{1,0:T(8,128)}) custom-call(s32[2,512]{1,0:T(2,128)} %seg_ref.3, bf16[1024,2304]{1,0:T(8,128)(2,1)} %get-tuple-element.81.q_ref.k_ref.v_ref, bf16[1024,2304]{1,0:T(8,128)(2,1)} %get-tuple-element.81.q_ref.k_ref.v_ref, ...), custom_call_target="tpu_custom_call" | custom-call | flops 3221225472 | bytes 10485760 | tf_op jit(solution)/shard_map/pallas_call | solution.py:301
  75.2 8.0 %shard_map.330 = (bf16[1024,768]{1,0:T(8,128)(2,1)}, bf16[24,512,512]{2,1,0:T(8,128)(2,1)}, f32[1024,768]{1,0:T(8,128)}) custom-call(s32[2,512]{1,0:T(2,128)} %seg_ref.3, bf16[1024,2304]{1,0:T(8,128)(2,1)} %get-tuple-element.81.q_ref.k_ref.v_ref, ...), custom_call_target="tpu_custom_call", output_to_operand_aliasing={{0}: (4, {}), {1}: (5, {}), {2}: (6, {})} | custom-call | flops 3221225472 | bytes 10485760 | tf_op jit(solution)/shard_map/pallas_call | solution.py:301
  83.1 1.1 collective-permute-done.13.d1
  84.3 2.0 %collective-permute-done.12.b1 = bf16[8,24,4864]{2,1,0:T(8,128)(2,1)} collective-permute-done((bf16[8,24,4864]{2,1,0:T(8,128)(2,1)}, bf16[8,24,4864]{2,1,0:T(8,128)(2,1)}, u32[]{:S(2)}, u32[]{:S(2)}) %collective-permute-start.12) | collective-permute-done | bytes 1867808 | tf_op jit(solution)/shard_map/ppermute | solution.py:81
  86.8 4.1 %collective-permute-done.16.d2 = bf16[8,64,768]{2,1,0:T(8,128)(2,1)S(1)} collective-permute-done((bf16[8,64,768]{2,1,0:T(8,128)(2,1)S(1)}, bf16[8,64,768]{2,1,0:T(8,128)(2,1)S(1)}, u32[]{:S(2)}, u32[]{:S(2)}) %collective-permute-start.16) | collective-permute-done | bytes 786464 | tf_op jit(solution)/shard_map/ppermute | solution.py:85
  90.8 1.1 collective-permute-done.17.d3
  92.0 0.7 collective-permute-done.15.b3
  92.8 34.8 %shard_map.331 = (bf16[1024,768]{1,0:T(8,128)(2,1)}, f32[1024,768]{1,0:T(8,128)}, bf16[1024,768]{1,0:T(8,128)(2,1)}, f32[8,768]{1,0:T(8,128)}) custom-call(s32[32]{0:T(128)} %pad_add_fusion.ids_ref, s32[32]{0:T(128)} %pad_add_fusion.1.ids_d_ref, bf16[1024,768]{1,0:T(8,128)(2,1)} %x_ref.5, bf16[1024,768]{1,0:T(8,128)(2,1)} %cot_ref.1, ...), custom_call_target="tpu_custom_call" | custom-call | flops 21743271936 | bytes 20971520 | tf_op jit(solution)/shard_map/pallas_call | solution.py:480
  127.7 25.8 %shard_map.332 = (f32[1024,768]{1,0:T(8,128)}, f32[40,384]{1,0:T(8,128)}, f32[40,384]{1,0:T(8,128)}) custom-call(s32[1]{0:T(128)} %bitcast.core_ref, bf16[1024,768]{1,0:T(8,128)(2,1)} %x_ref.5, bf16[1024,2304]{1,0:T(8,128)(2,1)} %get-tuple-element.81.q_ref.k_ref.v_ref, bf16[1024,2304]{1,0:T(8,128)(2,1)} %get-tuple-element.81.q_ref.k_ref.v_ref, ...), custom_call_target="tpu_custom_call" | custom-call | flops 12884901888 | bytes 29360128 | tf_op jit(solution)/shard_map/pallas_call | solution.py:620
  154.0 1.1 collective-permute-done.18
  155.1 0.8 add.31
  156.0 1.0 collective-permute-start.19
  157.0 1.3 collective-permute-start.20
  158.3 1.2 collective-permute-start.21
  159.5 0.8 collective-permute-done.19
  160.2 1.0 collective-permute-done.20
  161.2 2.1 %collective-permute-done.21 = f32[40,384]{1,0:T(8,128)S(1)} collective-permute-done((f32[40,384]{1,0:T(8,128)S(1)}, f32[40,384]{1,0:T(8,128)S(1)}, u32[]{:S(2)}, u32[]{:S(2)}) %collective-permute-start.21) | collective-permute-done | bytes 61472 | tf_op jit(solution)/shard_map/ppermute | solution.py:105
  163.4 1.0 collective-permute-start.22
  164.4 1.5 collective-permute-start.23
  165.9 2.0 %collective-permute-start.24 = (f32[40,384]{1,0:T(8,128)S(1)}, f32[40,384]{1,0:T(8,128)S(1)}, u32[]{:S(2)}, u32[]{:S(2)}) collective-permute-start(f32[40,384]{1,0:T(8,128)S(1)} %add_add_fusion.1), channel_id=1, source_target_pairs={{0,6},{1,7},{2,4},{3,5},{4,2},{5,3},{6,0},{7,1},{8,14},{9,15},{10,... | collective-permute-start | bytes 184328 | tf_op jit(solution)/shard_map/ppermute | solution.py:105
  167.9 2.6 %collective-permute-done.23 = f32[40,384]{1,0:T(8,128)S(1)} collective-permute-done((f32[40,384]{1,0:T(8,128)S(1)}, f32[40,384]{1,0:T(8,128)S(1)}, u32[]{:S(2)}, u32[]{:S(2)}) %collective-permute-start.23) | collective-permute-done | bytes 61472 | tf_op jit(solution)/shard_map/ppermute | solution.py:105
  170.6 1.4 collective-permute-done.24
  172.0 1.2 collective-permute-done.25.other_ref
  173.3 1.3 shard_map.333
  (72 shorter events, 4.5 us)
Async XLA Ops:
  0.6 21.3 %copy-start.8 = (s32[16]{0:T(128)S(1)}, s32[16]{0:T(128)}, u32[]{:S(2)}) copy-start(s32[16]{0:T(128)} %constant.32.clone) | copy-start | bytes 196
  0.7 21.3 %copy-start.9 = (s32[16]{0:T(128)S(1)}, s32[16]{0:T(128)}, u32[]{:S(2)}) copy-start(s32[16]{0:T(128)} %constant.33.clone) | copy-start | bytes 196
  0.7 21.3 %copy-start.10 = (s32[16]{0:T(128)S(1)}, s32[16]{0:T(128)}, u32[]{:S(2)}) copy-start(s32[16]{0:T(128)} %constant.34.clone) | copy-start | bytes 196
  0.7 21.3 %copy-start.11 = (s32[16]{0:T(128)S(1)}, s32[16]{0:T(128)}, u32[]{:S(2)}) copy-start(s32[16]{0:T(128)} %constant.35.clone) | copy-start | bytes 196
  2.3 7.9 %collective-permute-start = (bf16[1,24,2432]{2,1,0:T(8,128)(2,1)S(1)}, bf16[1,24,2432]{2,1,0:T(8,128)(2,1)S(1)}, u32[]{:S(2)}, u32[]{:S(2)}) collective-permute-start(bf16[1,24,2432]{2,1,0:T(8,128)(2,1)S(1)} %fusion.5), channel_id=1, source_target_pairs={{0,2},{1,3},{2,0},{3,1},{4,6},{5,7},{6,4},{7,5},{8,12},{9,13},{10,... | collective-permute-start | bytes 350216 | tf_op jit(solution)/shard_map/ppermute | solution.py:81
  6.3 4.6 %collective-permute-start.2 = (bf16[1,64,768]{2,1,0:T(8,128)(2,1)S(1)}, bf16[1,64,768]{2,1,0:T(8,128)(2,1)S(1)}, u32[]{:S(2)}, u32[]{:S(2)}) collective-permute-start(bf16[1,64,768]{2,1,0:T(8,128)(2,1)S(1)} %slice_bitcast_fusion), channel_id=1, source_target_pairs={{0,16},{1,17},{2,18},{3,19},{4,20},{5,21},{6,22},{7,23},{8,9},{9,8... | collective-permute-start | bytes 294920 | tf_op jit(solution)/shard_map/ppermute | solution.py:81
  10.9 9.5 %collective-permute-start.1 = (bf16[2,24,2432]{2,1,0:T(8,128)(2,1)S(1)}, bf16[2,24,2432]{2,1,0:T(8,128)(2,1)S(1)}, u32[]{:S(2)}, u32[]{:S(2)}) collective-permute-start(bf16[2,24,2432]{2,1,0:T(8,128)(2,1)S(1)} %pad_maximum_fusion.5), channel_id=1, source_target_pairs={{0,4},{1,5},{2,6},{3,7},{4,0},{5,1},{6,2},{7,3},{8,10},{9,11},{10,... | collective-permute-start | bytes 700424 | tf_op jit(solution)/shard_map/ppermute | solution.py:81
  13.5 5.7 %collective-permute-start.3 = (bf16[2,64,768]{2,1,0:T(8,128)(2,1)S(1)}, bf16[2,64,768]{2,1,0:T(8,128)(2,1)S(1)}, u32[]{:S(2)}, u32[]{:S(2)}) collective-permute-start(bf16[2,64,768]{2,1,0:T(8,128)(2,1)S(1)} %pad_maximum_fusion.6), channel_id=1, source_target_pairs={{0,1},{1,0},{2,3},{3,2},{4,5},{5,4},{6,7},{7,6},{8,24},{9,25},{10,... | collective-permute-start | bytes 589832 | tf_op jit(solution)/shard_map/ppermute | solution.py:81
  20.4 8.6 %collective-permute-start.4 = (bf16[4,24,2432]{2,1,0:T(8,128)(2,1)S(1)}, bf16[4,24,2432]{2,1,0:T(8,128)(2,1)S(1)}, u32[]{:S(2)}, u32[]{:S(2)}) collective-permute-start(bf16[4,24,2432]{2,1,0:T(8,128)(2,1)S(1)} %pad_maximum_fusion.2), channel_id=1, source_target_pairs={{0,16},{1,17},{2,18},{3,19},{4,20},{5,21},{6,22},{7,23},{8,9},{9,8... | collective-permute-start | bytes 1400840 | tf_op jit(solution)/shard_map/ppermute | solution.py:81
  22.0 7.0 %collective-permute-start.5 = (bf16[1,24,4864]{2,1,0:T(8,128)(2,1)S(1)}, bf16[1,24,4864]{2,1,0:T(8,128)(2,1)S(1)}, u32[]{:S(2)}, u32[]{:S(2)}) collective-permute-start(bf16[1,24,4864]{2,1,0:T(8,128)(2,1)S(1)} %maximum_bitcast_fusion), channel_id=1, source_target_pairs={{0,2},{1,3},{2,0},{3,1},{4,6},{5,7},{6,4},{7,5},{8,12},{9,13},{10,... | collective-permute-start | bytes 700424 | tf_op jit(solution)/shard_map/ppermute | solution.py:81
  29.2 19.0 %copy-start.6 = (bf16[8,24,2432]{2,1,0:T(8,128)(2,1)}, bf16[8,24,2432]{2,1,0:T(8,128)(2,1)S(1)}, u32[]{:S(2)}) copy-start(bf16[8,24,2432]{2,1,0:T(8,128)(2,1)S(1)} %pad_maximum_fusion.p0) | copy-start | bytes 2801668
  29.2 16.6 %collective-permute-start.6 = (bf16[8,24,2432]{2,1,0:T(8,128)(2,1)S(1)}, bf16[8,24,2432]{2,1,0:T(8,128)(2,1)S(1)}, u32[]{:S(2)}, u32[]{:S(2)}) collective-permute-start(bf16[8,24,2432]{2,1,0:T(8,128)(2,1)S(1)} %pad_maximum_fusion.p0), channel_id=1, source_target_pairs={{0,1},{1,0},{2,3},{3,2},{4,5},{5,4},{6,7},{7,6},{8,24},{9,25},{10,... | collective-permute-start | bytes 2801672 | tf_op jit(solution)/shard_map/ppermute | solution.py:81
  31.3 14.5 %collective-permute-start.8 = (bf16[8,24,2432]{2,1,0:T(8,128)(2,1)S(1)}, bf16[8,24,2432]{2,1,0:T(8,128)(2,1)S(1)}, u32[]{:S(2)}, u32[]{:S(2)}) collective-permute-start(bf16[8,24,2432]{2,1,0:T(8,128)(2,1)S(1)} %pad_maximum_fusion.p0), channel_id=1, source_target_pairs={{0,8},{1,9},{2,10},{3,11},{4,12},{5,13},{6,14},{7,15},{8,0},{9,1},... | collective-permute-start | bytes 2801672 | tf_op jit(solution)/shard_map/ppermute | solution.py:85
  31.4 14.4 %collective-permute-start.7 = (bf16[2,24,4864]{2,1,0:T(8,128)(2,1)S(1)}, bf16[2,24,4864]{2,1,0:T(8,128)(2,1)S(1)}, u32[]{:S(2)}, u32[]{:S(2)}) collective-permute-start(bf16[2,24,4864]{2,1,0:T(8,128)(2,1)S(1)} %pad_maximum_fusion.3), channel_id=1, source_target_pairs={{0,4},{1,5},{2,6},{3,7},{4,0},{5,1},{6,2},{7,3},{8,10},{9,11},{10,... | collective-permute-start | bytes 1400840 | tf_op jit(solution)/shard_map/ppermute | solution.py:81
  45.8 4.5 %copy-start.12 = (bf16[8,24,2432]{2,1,0:T(8,128)(2,1)}, bf16[8,24,2432]{2,1,0:T(8,128)(2,1)S(1)}, u32[]{:S(2)}) copy-start(bf16[8,24,2432]{2,1,0:T(8,128)(2,1)S(1)} %collective-permute-done.6.p1) | copy-start | bytes 2801668
  45.8 4.5 %copy-start.13 = (bf16[8,24,2432]{2,1,0:T(8,128)(2,1)}, bf16[8,24,2432]{2,1,0:T(8,128)(2,1)S(1)}, u32[]{:S(2)}) copy-start(bf16[8,24,2432]{2,1,0:T(8,128)(2,1)S(1)} %collective-permute-done.8.p2) | copy-start | bytes 2801668
  45.8 3.5 %collective-permute-start.11 = (bf16[8,24,2432]{2,1,0:T(8,128)(2,1)S(1)}, bf16[8,24,2432]{2,1,0:T(8,128)(2,1)S(1)}, u32[]{:S(2)}, u32[]{:S(2)}) collective-permute-start(bf16[8,24,2432]{2,1,0:T(8,128)(2,1)S(1)} %collective-permute-done.6.p1), channel_id=1, source_target_pairs={{0,8},{1,9},{2,10},{3,11},{4,12},{5,13},{6,14},{7,15},{8,0},{9,1},... | collective-permute-start | bytes 2801672 | tf_op jit(solution)/shard_map/ppermute | solution.py:85
  46.0 15.4 %collective-permute-start.9 = (bf16[4,24,4864]{2,1,0:T(8,128)(2,1)S(1)}, bf16[4,24,4864]{2,1,0:T(8,128)(2,1)S(1)}, u32[]{:S(2)}, u32[]{:S(2)}) collective-permute-start(bf16[4,24,4864]{2,1,0:T(8,128)(2,1)S(1)} %pad_maximum_fusion.1), channel_id=1, source_target_pairs={{0,16},{1,17},{2,18},{3,19},{4,20},{5,21},{6,22},{7,23},{8,9},{9,8... | collective-permute-start | bytes 2801672 | tf_op jit(solution)/shard_map/ppermute | solution.py:81
  48.2 13.2 %collective-permute-start.10 = (bf16[4,64,768]{2,1,0:T(8,128)(2,1)S(1)}, bf16[4,64,768]{2,1,0:T(8,128)(2,1)S(1)}, u32[]{:S(2)}, u32[]{:S(2)}) collective-permute-start(bf16[4,64,768]{2,1,0:T(8,128)(2,1)S(1)} %pad_maximum_fusion.4), channel_id=1, source_target_pairs={{0,2},{1,3},{2,0},{3,1},{4,6},{5,7},{6,4},{7,5},{8,12},{9,13},{10,... | collective-permute-start | bytes 1179656 | tf_op jit(solution)/shard_map/ppermute | solution.py:81
  49.3 1.0 copy-start.14
  62.4 23.9 %collective-permute-start.12 = (bf16[8,24,4864]{2,1,0:T(8,128)(2,1)}, bf16[8,24,4864]{2,1,0:T(8,128)(2,1)}, u32[]{:S(2)}, u32[]{:S(2)}) collective-permute-start(bf16[8,24,4864]{2,1,0:T(8,128)(2,1)} %constant_dynamic-update-slice_fusion.b0), channel_id=1, source_target_pairs={{0,1},{1,0},{2,3},{3,2},{4,5},{5,4},{6,7},{7,6},{8,24},{9,25},{10,... | collective-permute-start | bytes 5603336 | tf_op jit(solution)/shard_map/ppermute | solution.py:81
  63.9 22.4 %copy-start.7 = (bf16[8,64,768]{2,1,0:T(8,128)(2,1)}, bf16[8,64,768]{2,1,0:T(8,128)(2,1)S(1)}, u32[]{:S(2)}) copy-start(bf16[8,64,768]{2,1,0:T(8,128)(2,1)S(1)} %constant_dynamic-update-slice_fusion.4.d0) | copy-start | bytes 2359300
  63.9 20.3 %collective-permute-start.13 = (bf16[8,64,768]{2,1,0:T(8,128)(2,1)S(1)}, bf16[8,64,768]{2,1,0:T(8,128)(2,1)S(1)}, u32[]{:S(2)}, u32[]{:S(2)}) collective-permute-start(bf16[8,64,768]{2,1,0:T(8,128)(2,1)S(1)} %constant_dynamic-update-slice_fusion.4.d0), channel_id=1, source_target_pairs={{0,4},{1,5},{2,6},{3,7},{4,0},{5,1},{6,2},{7,3},{8,10},{9,11},{10,... | collective-permute-start | bytes 2359304 | tf_op jit(solution)/shard_map/ppermute | solution.py:81
  75.1 15.7 %collective-permute-start.14 = (bf16[8,24,4864]{2,1,0:T(8,128)(2,1)}, bf16[8,24,4864]{2,1,0:T(8,128)(2,1)}, u32[]{:S(2)}, u32[]{:S(2)}) collective-permute-start(bf16[8,24,4864]{2,1,0:T(8,128)(2,1)} %constant_dynamic-update-slice_fusion.b0), channel_id=1, source_target_pairs={{0,8},{1,9},{2,10},{3,11},{4,12},{5,13},{6,14},{7,15},{8,0},{9,1},... | collective-permute-start | bytes 5603336 | tf_op jit(solution)/shard_map/ppermute | solution.py:85
  84.3 8.4 %copy-start.15 = (bf16[8,64,768]{2,1,0:T(8,128)(2,1)}, bf16[8,64,768]{2,1,0:T(8,128)(2,1)S(1)}, u32[]{:S(2)}) copy-start(bf16[8,64,768]{2,1,0:T(8,128)(2,1)S(1)} %collective-permute-done.13.d1) | copy-start | bytes 2359300
  86.3 6.4 %collective-permute-start.15 = (bf16[8,24,4864]{2,1,0:T(8,128)(2,1)}, bf16[8,24,4864]{2,1,0:T(8,128)(2,1)}, u32[]{:S(2)}, u32[]{:S(2)}) collective-permute-start(bf16[8,24,4864]{2,1,0:T(8,128)(2,1)} %collective-permute-done.12.b1), channel_id=1, source_target_pairs={{0,8},{1,9},{2,10},{3,11},{4,12},{5,13},{6,14},{7,15},{8,0},{9,1},... | collective-permute-start | bytes 5603336 | tf_op jit(solution)/shard_map/ppermute | solution.py:85
  86.3 4.6 %collective-permute-start.16 = (bf16[8,64,768]{2,1,0:T(8,128)(2,1)S(1)}, bf16[8,64,768]{2,1,0:T(8,128)(2,1)S(1)}, u32[]{:S(2)}, u32[]{:S(2)}) collective-permute-start(bf16[8,64,768]{2,1,0:T(8,128)(2,1)S(1)} %constant_dynamic-update-slice_fusion.4.d0), channel_id=1, source_target_pairs={{0,8},{1,9},{2,10},{3,11},{4,12},{5,13},{6,14},{7,15},{8,0},{9,1},... | collective-permute-start | bytes 2359304 | tf_op jit(solution)/shard_map/ppermute | solution.py:85
  86.8 5.2 %collective-permute-start.17 = (bf16[8,64,768]{2,1,0:T(8,128)(2,1)S(1)}, bf16[8,64,768]{2,1,0:T(8,128)(2,1)S(1)}, u32[]{:S(2)}, u32[]{:S(2)}) collective-permute-start(bf16[8,64,768]{2,1,0:T(8,128)(2,1)S(1)} %collective-permute-done.13.d1), channel_id=1, source_target_pairs={{0,8},{1,9},{2,10},{3,11},{4,12},{5,13},{6,14},{7,15},{8,0},{9,1},... | collective-permute-start | bytes 2359304 | tf_op jit(solution)/shard_map/ppermute | solution.py:85
  90.8 1.8 %copy-start.16 = (bf16[8,64,768]{2,1,0:T(8,128)(2,1)}, bf16[8,64,768]{2,1,0:T(8,128)(2,1)S(1)}, u32[]{:S(2)}) copy-start(bf16[8,64,768]{2,1,0:T(8,128)(2,1)S(1)} %collective-permute-done.16.d2) | copy-start | bytes 2359300
  92.0 0.9 copy-start.17
  127.7 45.6 %copy-start = (f32[2,768,8]{1,2,0:T(8,128)S(1)}, f32[2,768,8]{1,2,0:T(8,128)}, u32[]{:S(2)}) copy-start(f32[2,768,8]{1,2,0:T(8,128)} %param.37) | copy-start | bytes 147460
  127.7 45.6 %copy-start.1 = (f32[2,8,768]{2,1,0:T(8,128)S(1)}, f32[2,8,768]{2,1,0:T(8,128)}, u32[]{:S(2)}) copy-start(f32[2,8,768]{2,1,0:T(8,128)} %up_ref.5) | copy-start | bytes 147460
  127.7 45.6 %copy-start.2 = (f32[2,768,8]{1,2,0:T(8,128)S(1)}, f32[2,768,8]{1,2,0:T(8,128)}, u32[]{:S(2)}) copy-start(f32[2,768,8]{1,2,0:T(8,128)} %param.39) | copy-start | bytes 147460
  127.7 45.6 %copy-start.3 = (f32[2,768,8]{1,2,0:T(8,128)S(1)}, f32[2,768,8]{1,2,0:T(8,128)}, u32[]{:S(2)}) copy-start(f32[2,768,8]{1,2,0:T(8,128)} %param.40) | copy-start | bytes 147460
  127.7 45.6 %copy-start.4 = (f32[2,8,768]{2,1,0:T(8,128)S(1)}, f32[2,8,768]{2,1,0:T(8,128)}, u32[]{:S(2)}) copy-start(f32[2,8,768]{2,1,0:T(8,128)} %um_ref.1) | copy-start | bytes 147460
  127.7 45.6 %copy-start.5 = (f32[2,8,768]{2,1,0:T(8,128)S(1)}, f32[2,8,768]{2,1,0:T(8,128)}, u32[]{:S(2)}) copy-start(f32[2,8,768]{2,1,0:T(8,128)} %uv_ref.1) | copy-start | bytes 147460
  153.6 1.5 collective-permute-start.18
  156.0 4.3 %collective-permute-start.19 = (f32[40,384]{1,0:T(8,128)S(1)}, f32[40,384]{1,0:T(8,128)S(1)}, u32[]{:S(2)}, u32[]{:S(2)}) collective-permute-start(f32[40,384]{1,0:T(8,128)S(1)} %add.31), channel_id=1, source_target_pairs={{0,16},{1,17},{2,18},{3,19},{4,20},{5,21},{6,22},{7,23},{8,24},{9,... | collective-permute-start | bytes 184328 | tf_op jit(solution)/shard_map/ppermute | solution.py:105
  157.0 4.2 %collective-permute-start.20 = (f32[40,384]{1,0:T(8,128)S(1)}, f32[40,384]{1,0:T(8,128)S(1)}, u32[]{:S(2)}, u32[]{:S(2)}) collective-permute-start(f32[40,384]{1,0:T(8,128)S(1)} %add.31), channel_id=1, source_target_pairs={{0,1},{1,0},{2,3},{3,2},{4,5},{5,4},{6,7},{7,6},{8,9},{9,8},{10,11... | collective-permute-start | bytes 184328 | tf_op jit(solution)/shard_map/ppermute | solution.py:105
  158.3 5.1 %collective-permute-start.21 = (f32[40,384]{1,0:T(8,128)S(1)}, f32[40,384]{1,0:T(8,128)S(1)}, u32[]{:S(2)}, u32[]{:S(2)}) collective-permute-start(f32[40,384]{1,0:T(8,128)S(1)} %add.31), channel_id=1, source_target_pairs={{0,17},{1,16},{2,19},{3,18},{4,21},{5,20},{6,23},{7,22},{8,25},{9,... | collective-permute-start | bytes 184328 | tf_op jit(solution)/shard_map/ppermute | solution.py:105
  163.4 4.5 %collective-permute-start.22 = (f32[40,384]{1,0:T(8,128)S(1)}, f32[40,384]{1,0:T(8,128)S(1)}, u32[]{:S(2)}, u32[]{:S(2)}) collective-permute-start(f32[40,384]{1,0:T(8,128)S(1)} %add_add_fusion.1), channel_id=1, source_target_pairs={{0,2},{1,3},{2,0},{3,1},{4,6},{5,7},{6,4},{7,5},{8,10},{9,11},{10,... | collective-permute-start | bytes 184328 | tf_op jit(solution)/shard_map/ppermute | solution.py:105
  164.4 6.2 %collective-permute-start.23 = (f32[40,384]{1,0:T(8,128)S(1)}, f32[40,384]{1,0:T(8,128)S(1)}, u32[]{:S(2)}, u32[]{:S(2)}) collective-permute-start(f32[40,384]{1,0:T(8,128)S(1)} %add_add_fusion.1), channel_id=1, source_target_pairs={{0,4},{1,5},{2,6},{3,7},{4,0},{5,1},{6,2},{7,3},{8,12},{9,13},{10,... | collective-permute-start | bytes 184328 | tf_op jit(solution)/shard_map/ppermute | solution.py:105
  165.9 6.0 %collective-permute-start.24 = (f32[40,384]{1,0:T(8,128)S(1)}, f32[40,384]{1,0:T(8,128)S(1)}, u32[]{:S(2)}, u32[]{:S(2)}) collective-permute-start(f32[40,384]{1,0:T(8,128)S(1)} %add_add_fusion.1), channel_id=1, source_target_pairs={{0,6},{1,7},{2,4},{3,5},{4,2},{5,3},{6,0},{7,1},{8,14},{9,15},{10,... | collective-permute-start | bytes 184328 | tf_op jit(solution)/shard_map/ppermute | solution.py:105
  171.9 1.3 collective-permute-start.25

commit v6 on v5

--- a/solution.py
+++ b/solution.py
@@ -177,8 +177,9 @@
     down = down_ref[...].reshape(2 * rank, width).astype(bf16)
     up = (2.0 * up_ref[...].astype(bf16).astype(f32)).astype(bf16)
     zero = jnp.zeros((rank, width), bf16)
-    reduced = nt(x, down).astype(bf16)
-    red_ref[...] = nt(down, x).astype(bf16)
+    wide = nt(x, down)
+    reduced = wide.astype(bf16)
+    red_ref[...] = wide.T.astype(bf16)
     up_query = jnp.concatenate([up[0], zero], axis=0)
     up_value = jnp.concatenate([zero, up[1]], axis=0)
     chunk = 256

time: 175 us -> 175 us (level)
  transfers between devices with their start and end apart: 26 -> 26, of which waited for: 19 -> 18; matrix products, arithmetic and copies ran while one was open for 4% -> 4% of each run, Pallas kernels for 15% -> 15%
where the time goes in v6:
time: 175 us
  Pallas kernels  89 us (51%)
  waiting for transfers between devices  45.3 us (26%)
  starting transfers between devices  26.1 us (15%)
  local copies, waits for them, and re-layouts  6.84 us (4%)
  other arithmetic  5.02 us (3%)
  between operations  2.45 us (1%)
    pallas_call x1, Pallas kernels, row_local(): pl.pallas_call(rows_kernel, grid=(rows // tile,), in_specs=[pl.BlockSpec(...  34.8 us
    ppermute x12, waiting for transfers between devices, stage(): return lax.ppermute(held, AXES, layout.stage_pairs(orders, t))  29 us
    pallas_call x1, Pallas kernels, attend_back(): pl.pallas_call(attend_back_kernel, grid=(rows // length, steps), in_specs...  25.8 us
    ppermute x12, starting transfers between devices, stage(): return lax.ppermute(held, AXES, layout.stage_pairs(orders, t))  17.1 us
    pallas_call x2, Pallas kernels, attend(): pl.pallas_call(functools.partial(attend_kernel, pack), grid=(steps,), in_...  16 us
    pallas_call x1, Pallas kernels, project(): pl.pallas_call(project_kernel, grid=(rows // tile,), in_specs=[pl.BlockSp...  11.1 us
    ppermute x8, waiting for transfers between devices, swap_cores(): return lax.ppermute(value, AXES, layout.core_pairs())  8.25 us
    ppermute x6, waiting for transfers between devices, exchange(): lax.ppermute(total, AXES, layout.pairs(c))  8.01 us
  transfers between devices with their start and end apart: 26, of which 18 were waited for; matrix products, arithmetic and copies ran while one was open for 4% of the time, Pallas kernels for 15%

profile of v6, /device:TPU:0, one launch (start us, length us, event | category | flops | bytes accessed | tf_op | source)
XLA Modules:
  0.0 174.8 jit_solution(13423673611513684621)
XLA Ops:
  0.7 0.7 fusion.10
  1.4 0.8 fusion.5
  2.3 3.1 %collective-permute-start = (bf16[1,24,2432]{2,1,0:T(8,128)(2,1)S(1)}, bf16[1,24,2432]{2,1,0:T(8,128)(2,1)S(1)}, u32[]{:S(2)}, u32[]{:S(2)}) collective-permute-start(bf16[1,24,2432]{2,1,0:T(8,128)(2,1)S(1)} %fusion.5), channel_id=1, source_target_pairs={{0,2},{1,3},{2,0},{3,1},{4,6},{5,7},{6,4},{7,5},{8,12},{9,13},{10,... | collective-permute-start | bytes 350216 | tf_op jit(solution)/shard_map/ppermute | solution.py:81
  5.4 0.9 slice_bitcast_fusion
  6.3 1.5 collective-permute-start.2
  7.7 0.8 slice.12
  8.5 0.7 slice.13
  9.2 0.9 maximum_bitcast_fusion
  10.9 2.6 %collective-permute-start.1 = (bf16[2,24,2432]{2,1,0:T(8,128)(2,1)S(1)}, bf16[2,24,2432]{2,1,0:T(8,128)(2,1)S(1)}, u32[]{:S(2)}, u32[]{:S(2)}) collective-permute-start(bf16[2,24,2432]{2,1,0:T(8,128)(2,1)S(1)} %pad_maximum_fusion.5), channel_id=1, source_target_pairs={{0,4},{1,5},{2,6},{3,7},{4,0},{5,1},{6,2},{7,3},{8,10},{9,11},{10,... | collective-permute-start | bytes 700424 | tf_op jit(solution)/shard_map/ppermute | solution.py:81
  13.5 1.6 collective-permute-start.3
  15.1 4.2 %collective-permute-done.3 = bf16[2,64,768]{2,1,0:T(8,128)(2,1)S(1)} collective-permute-done((bf16[2,64,768]{2,1,0:T(8,128)(2,1)S(1)}, bf16[2,64,768]{2,1,0:T(8,128)(2,1)S(1)}, u32[]{:S(2)}, u32[]{:S(2)}) %collective-permute-start.3) | collective-permute-done | bytes 196640 | tf_op jit(solution)/shard_map/ppermute | solution.py:81
  19.2 1.1 collective-permute-done.1
  20.4 1.6 collective-permute-start.4
  22.7 6.3 %collective-permute-done.5 = bf16[1,24,4864]{2,1,0:T(8,128)(2,1)S(1)} collective-permute-done((bf16[1,24,4864]{2,1,0:T(8,128)(2,1)S(1)}, bf16[1,24,4864]{2,1,0:T(8,128)(2,1)S(1)}, u32[]{:S(2)}, u32[]{:S(2)}) %collective-permute-start.5) | collective-permute-done | bytes 233504 | tf_op jit(solution)/shard_map/ppermute | solution.py:81
  29.2 2.2 %collective-permute-start.6 = (bf16[8,24,2432]{2,1,0:T(8,128)(2,1)S(1)}, bf16[8,24,2432]{2,1,0:T(8,128)(2,1)S(1)}, u32[]{:S(2)}, u32[]{:S(2)}) collective-permute-start(bf16[8,24,2432]{2,1,0:T(8,128)(2,1)S(1)} %pad_maximum_fusion.p0), channel_id=1, source_target_pairs={{0,1},{1,0},{2,3},{3,2},{4,5},{5,4},{6,7},{7,6},{8,24},{9,25},{10,... | collective-permute-start | bytes 2801672 | tf_op jit(solution)/shard_map/ppermute | solution.py:81
  31.5 0.7 constant_dynamic-update-slice_fusion.3
  32.2 13.6 %collective-permute-done.7 = bf16[2,24,4864]{2,1,0:T(8,128)(2,1)S(1)} collective-permute-done((bf16[2,24,4864]{2,1,0:T(8,128)(2,1)S(1)}, bf16[2,24,4864]{2,1,0:T(8,128)(2,1)S(1)}, u32[]{:S(2)}, u32[]{:S(2)}) %collective-permute-start.7) | collective-permute-done | bytes 466976 | tf_op jit(solution)/shard_map/ppermute | solution.py:81
  46.0 1.5 collective-permute-start.9
  47.5 0.7 constant_dynamic-update-slice_fusion.2
  48.5 0.8 constant_dynamic-update-slice_fusion.1
  49.3 0.9 copy-done.14
  50.3 11.1 %shard_map.328 = (bf16[1024,2304]{1,0:T(8,128)(2,1)}, bf16[768,2304]{1,0:T(8,128)(2,1)}, bf16[16,1024]{1,0:T(8,128)(2,1)}, f32[8,768]{1,0:T(8,128)}, f32[8,3072]{1,0:T(8,128)}) custom-call(s32[32]{0:T(128)} %pad_add_fusion.ids_ref, bf16[1024,768]{1,0:T(8,128)(2,1)} %x_ref.5, f32[2,8,768]{2,1,0:T(8,128)} %bitcast.20, f32[2,8,768]{2,1,0:T(8,128)} %up_ref.5, ...), custom_call_target="tpu_custom_call" | custom-call | flops 3623878656 | bytes 14680064 | tf_op jit(solution)/shard_map/pallas_call | solution.py:207
  61.4 1.0 constant_dynamic-update-slice_fusion.b0
  63.9 2.6 %collective-permute-start.13 = (bf16[8,64,768]{2,1,0:T(8,128)(2,1)S(1)}, bf16[8,64,768]{2,1,0:T(8,128)(2,1)S(1)}, u32[]{:S(2)}, u32[]{:S(2)}) collective-permute-start(bf16[8,64,768]{2,1,0:T(8,128)(2,1)S(1)} %constant_dynamic-update-slice_fusion.4.d0), channel_id=1, source_target_pairs={{0,4},{1,5},{2,6},{3,7},{4,0},{5,1},{6,2},{7,3},{8,10},{9,11},{10,... | collective-permute-start | bytes 2359304 | tf_op jit(solution)/shard_map/ppermute | solution.py:81
  67.2 8.0 %shard_map.329 = (bf16[1024,768]{1,0:T(8,128)(2,1)}, bf16[24,512,512]{2,1,0:T(8,128)(2,1)}, f32[1024,768]{1,0:T(8,128)}) custom-call(s32[2,512]{1,0:T(2,128)} %seg_ref.3, bf16[1024,2304]{1,0:T(8,128)(2,1)} %get-tuple-element.81.q_ref.k_ref.v_ref, bf16[1024,2304]{1,0:T(8,128)(2,1)} %get-tuple-element.81.q_ref.k_ref.v_ref, ...), custom_call_target="tpu_custom_call" | custom-call | flops 3221225472 | bytes 10485760 | tf_op jit(solution)/shard_map/pallas_call | solution.py:302
  75.2 8.0 %shard_map.330 = (bf16[1024,768]{1,0:T(8,128)(2,1)}, bf16[24,512,512]{2,1,0:T(8,128)(2,1)}, f32[1024,768]{1,0:T(8,128)}) custom-call(s32[2,512]{1,0:T(2,128)} %seg_ref.3, bf16[1024,2304]{1,0:T(8,128)(2,1)} %get-tuple-element.81.q_ref.k_ref.v_ref, ...), custom_call_target="tpu_custom_call", output_to_operand_aliasing={{0}: (4, {}), {1}: (5, {}), {2}: (6, {})} | custom-call | flops 3221225472 | bytes 10485760 | tf_op jit(solution)/shard_map/pallas_call | solution.py:302
  83.2 1.1 collective-permute-done.13.d1
  84.3 2.0 %collective-permute-done.12.b1 = bf16[8,24,4864]{2,1,0:T(8,128)(2,1)} collective-permute-done((bf16[8,24,4864]{2,1,0:T(8,128)(2,1)}, bf16[8,24,4864]{2,1,0:T(8,128)(2,1)}, u32[]{:S(2)}, u32[]{:S(2)}) %collective-permute-start.12) | collective-permute-done | bytes 1867808 | tf_op jit(solution)/shard_map/ppermute | solution.py:81
  86.8 4.1 %collective-permute-done.16.d2 = bf16[8,64,768]{2,1,0:T(8,128)(2,1)S(1)} collective-permute-done((bf16[8,64,768]{2,1,0:T(8,128)(2,1)S(1)}, bf16[8,64,768]{2,1,0:T(8,128)(2,1)S(1)}, u32[]{:S(2)}, u32[]{:S(2)}) %collective-permute-start.16) | collective-permute-done | bytes 786464 | tf_op jit(solution)/shard_map/ppermute | solution.py:85
  90.9 1.1 collective-permute-done.17.d3
  92.0 0.7 collective-permute-done.15.b3
  92.9 34.8 %shard_map.331 = (bf16[1024,768]{1,0:T(8,128)(2,1)}, f32[1024,768]{1,0:T(8,128)}, bf16[1024,768]{1,0:T(8,128)(2,1)}, f32[8,768]{1,0:T(8,128)}) custom-call(s32[32]{0:T(128)} %pad_add_fusion.ids_ref, s32[32]{0:T(128)} %pad_add_fusion.1.ids_d_ref, bf16[1024,768]{1,0:T(8,128)(2,1)} %x_ref.5, bf16[1024,768]{1,0:T(8,128)(2,1)} %cot_ref.1, ...), custom_call_target="tpu_custom_call" | custom-call | flops 21743271936 | bytes 20971520 | tf_op jit(solution)/shard_map/pallas_call | solution.py:481
  127.8 25.8 %shard_map.332 = (f32[1024,768]{1,0:T(8,128)}, f32[40,384]{1,0:T(8,128)}, f32[40,384]{1,0:T(8,128)}) custom-call(s32[1]{0:T(128)} %bitcast.core_ref, bf16[1024,768]{1,0:T(8,128)(2,1)} %x_ref.5, bf16[1024,2304]{1,0:T(8,128)(2,1)} %get-tuple-element.81.q_ref.k_ref.v_ref, bf16[1024,2304]{1,0:T(8,128)(2,1)} %get-tuple-element.81.q_ref.k_ref.v_ref, ...), custom_call_target="tpu_custom_call" | custom-call | flops 12884901888 | bytes 29360128 | tf_op jit(solution)/shard_map/pallas_call | solution.py:621
  154.0 1.1 collective-permute-done.18
  155.1 0.8 add.31
  156.0 1.1 collective-permute-start.19
  157.0 1.3 collective-permute-start.20
  158.3 1.2 collective-permute-start.21
  159.5 0.8 collective-permute-done.19
  160.2 1.0 collective-permute-done.20
  161.3 2.1 %collective-permute-done.21 = f32[40,384]{1,0:T(8,128)S(1)} collective-permute-done((f32[40,384]{1,0:T(8,128)S(1)}, f32[40,384]{1,0:T(8,128)S(1)}, u32[]{:S(2)}, u32[]{:S(2)}) %collective-permute-start.21) | collective-permute-done | bytes 61472 | tf_op jit(solution)/shard_map/ppermute | solution.py:105
  163.4 1.0 collective-permute-start.22
  164.4 1.5 collective-permute-start.23
  165.9 1.9 %collective-permute-start.24 = (f32[40,384]{1,0:T(8,128)S(1)}, f32[40,384]{1,0:T(8,128)S(1)}, u32[]{:S(2)}, u32[]{:S(2)}) collective-permute-start(f32[40,384]{1,0:T(8,128)S(1)} %add_add_fusion.1), channel_id=1, source_target_pairs={{0,6},{1,7},{2,4},{3,5},{4,2},{5,3},{6,0},{7,1},{8,14},{9,15},{10,... | collective-permute-start | bytes 184328 | tf_op jit(solution)/shard_map/ppermute | solution.py:105
  167.9 2.6 %collective-permute-done.23 = f32[40,384]{1,0:T(8,128)S(1)} collective-permute-done((f32[40,384]{1,0:T(8,128)S(1)}, f32[40,384]{1,0:T(8,128)S(1)}, u32[]{:S(2)}, u32[]{:S(2)}) %collective-permute-start.23) | collective-permute-done | bytes 61472 | tf_op jit(solution)/shard_map/ppermute | solution.py:105
  170.6 1.4 collective-permute-done.24
  172.1 1.2 collective-permute-done.25.other_ref
  173.3 1.3 shard_map.333
  (72 shorter events, 4.5 us)
Async XLA Ops:
  0.6 21.3 %copy-start.8 = (s32[16]{0:T(128)S(1)}, s32[16]{0:T(128)}, u32[]{:S(2)}) copy-start(s32[16]{0:T(128)} %constant.32.clone) | copy-start | bytes 196
  0.7 21.3 %copy-start.9 = (s32[16]{0:T(128)S(1)}, s32[16]{0:T(128)}, u32[]{:S(2)}) copy-start(s32[16]{0:T(128)} %constant.33.clone) | copy-start | bytes 196
  0.7 21.3 %copy-start.10 = (s32[16]{0:T(128)S(1)}, s32[16]{0:T(128)}, u32[]{:S(2)}) copy-start(s32[16]{0:T(128)} %constant.34.clone) | copy-start | bytes 196
  0.7 21.3 %copy-start.11 = (s32[16]{0:T(128)S(1)}, s32[16]{0:T(128)}, u32[]{:S(2)}) copy-start(s32[16]{0:T(128)} %constant.35.clone) | copy-start | bytes 196
  2.3 7.9 %collective-permute-start = (bf16[1,24,2432]{2,1,0:T(8,128)(2,1)S(1)}, bf16[1,24,2432]{2,1,0:T(8,128)(2,1)S(1)}, u32[]{:S(2)}, u32[]{:S(2)}) collective-permute-start(bf16[1,24,2432]{2,1,0:T(8,128)(2,1)S(1)} %fusion.5), channel_id=1, source_target_pairs={{0,2},{1,3},{2,0},{3,1},{4,6},{5,7},{6,4},{7,5},{8,12},{9,13},{10,... | collective-permute-start | bytes 350216 | tf_op jit(solution)/shard_map/ppermute | solution.py:81
  6.3 4.6 %collective-permute-start.2 = (bf16[1,64,768]{2,1,0:T(8,128)(2,1)S(1)}, bf16[1,64,768]{2,1,0:T(8,128)(2,1)S(1)}, u32[]{:S(2)}, u32[]{:S(2)}) collective-permute-start(bf16[1,64,768]{2,1,0:T(8,128)(2,1)S(1)} %slice_bitcast_fusion), channel_id=1, source_target_pairs={{0,16},{1,17},{2,18},{3,19},{4,20},{5,21},{6,22},{7,23},{8,9},{9,8... | collective-permute-start | bytes 294920 | tf_op jit(solution)/shard_map/ppermute | solution.py:81
  10.9 9.5 %collective-permute-start.1 = (bf16[2,24,2432]{2,1,0:T(8,128)(2,1)S(1)}, bf16[2,24,2432]{2,1,0:T(8,128)(2,1)S(1)}, u32[]{:S(2)}, u32[]{:S(2)}) collective-permute-start(bf16[2,24,2432]{2,1,0:T(8,128)(2,1)S(1)} %pad_maximum_fusion.5), channel_id=1, source_target_pairs={{0,4},{1,5},{2,6},{3,7},{4,0},{5,1},{6,2},{7,3},{8,10},{9,11},{10,... | collective-permute-start | bytes 700424 | tf_op jit(solution)/shard_map/ppermute | solution.py:81
  13.5 5.7 %collective-permute-start.3 = (bf16[2,64,768]{2,1,0:T(8,128)(2,1)S(1)}, bf16[2,64,768]{2,1,0:T(8,128)(2,1)S(1)}, u32[]{:S(2)}, u32[]{:S(2)}) collective-permute-start(bf16[2,64,768]{2,1,0:T(8,128)(2,1)S(1)} %pad_maximum_fusion.6), channel_id=1, source_target_pairs={{0,1},{1,0},{2,3},{3,2},{4,5},{5,4},{6,7},{7,6},{8,24},{9,25},{10,... | collective-permute-start | bytes 589832 | tf_op jit(solution)/shard_map/ppermute | solution.py:81
  20.4 8.6 %collective-permute-start.4 = (bf16[4,24,2432]{2,1,0:T(8,128)(2,1)S(1)}, bf16[4,24,2432]{2,1,0:T(8,128)(2,1)S(1)}, u32[]{:S(2)}, u32[]{:S(2)}) collective-permute-start(bf16[4,24,2432]{2,1,0:T(8,128)(2,1)S(1)} %pad_maximum_fusion.2), channel_id=1, source_target_pairs={{0,16},{1,17},{2,18},{3,19},{4,20},{5,21},{6,22},{7,23},{8,9},{9,8... | collective-permute-start | bytes 1400840 | tf_op jit(solution)/shard_map/ppermute | solution.py:81
  22.0 7.0 %collective-permute-start.5 = (bf16[1,24,4864]{2,1,0:T(8,128)(2,1)S(1)}, bf16[1,24,4864]{2,1,0:T(8,128)(2,1)S(1)}, u32[]{:S(2)}, u32[]{:S(2)}) collective-permute-start(bf16[1,24,4864]{2,1,0:T(8,128)(2,1)S(1)} %maximum_bitcast_fusion), channel_id=1, source_target_pairs={{0,2},{1,3},{2,0},{3,1},{4,6},{5,7},{6,4},{7,5},{8,12},{9,13},{10,... | collective-permute-start | bytes 700424 | tf_op jit(solution)/shard_map/ppermute | solution.py:81
  29.2 19.0 %copy-start.6 = (bf16[8,24,2432]{2,1,0:T(8,128)(2,1)}, bf16[8,24,2432]{2,1,0:T(8,128)(2,1)S(1)}, u32[]{:S(2)}) copy-start(bf16[8,24,2432]{2,1,0:T(8,128)(2,1)S(1)} %pad_maximum_fusion.p0) | copy-start | bytes 2801668
  29.2 16.6 %collective-permute-start.6 = (bf16[8,24,2432]{2,1,0:T(8,128)(2,1)S(1)}, bf16[8,24,2432]{2,1,0:T(8,128)(2,1)S(1)}, u32[]{:S(2)}, u32[]{:S(2)}) collective-permute-start(bf16[8,24,2432]{2,1,0:T(8,128)(2,1)S(1)} %pad_maximum_fusion.p0), channel_id=1, source_target_pairs={{0,1},{1,0},{2,3},{3,2},{4,5},{5,4},{6,7},{7,6},{8,24},{9,25},{10,... | collective-permute-start | bytes 2801672 | tf_op jit(solution)/shard_map/ppermute | solution.py:81
  31.3 14.5 %collective-permute-start.8 = (bf16[8,24,2432]{2,1,0:T(8,128)(2,1)S(1)}, bf16[8,24,2432]{2,1,0:T(8,128)(2,1)S(1)}, u32[]{:S(2)}, u32[]{:S(2)}) collective-permute-start(bf16[8,24,2432]{2,1,0:T(8,128)(2,1)S(1)} %pad_maximum_fusion.p0), channel_id=1, source_target_pairs={{0,8},{1,9},{2,10},{3,11},{4,12},{5,13},{6,14},{7,15},{8,0},{9,1},... | collective-permute-start | bytes 2801672 | tf_op jit(solution)/shard_map/ppermute | solution.py:85
  31.4 14.4 %collective-permute-start.7 = (bf16[2,24,4864]{2,1,0:T(8,128)(2,1)S(1)}, bf16[2,24,4864]{2,1,0:T(8,128)(2,1)S(1)}, u32[]{:S(2)}, u32[]{:S(2)}) collective-permute-start(bf16[2,24,4864]{2,1,0:T(8,128)(2,1)S(1)} %pad_maximum_fusion.3), channel_id=1, source_target_pairs={{0,4},{1,5},{2,6},{3,7},{4,0},{5,1},{6,2},{7,3},{8,10},{9,11},{10,... | collective-permute-start | bytes 1400840 | tf_op jit(solution)/shard_map/ppermute | solution.py:81
  45.8 4.5 %copy-start.12 = (bf16[8,24,2432]{2,1,0:T(8,128)(2,1)}, bf16[8,24,2432]{2,1,0:T(8,128)(2,1)S(1)}, u32[]{:S(2)}) copy-start(bf16[8,24,2432]{2,1,0:T(8,128)(2,1)S(1)} %collective-permute-done.6.p1) | copy-start | bytes 2801668
  45.8 4.5 %copy-start.13 = (bf16[8,24,2432]{2,1,0:T(8,128)(2,1)}, bf16[8,24,2432]{2,1,0:T(8,128)(2,1)S(1)}, u32[]{:S(2)}) copy-start(bf16[8,24,2432]{2,1,0:T(8,128)(2,1)S(1)} %collective-permute-done.8.p2) | copy-start | bytes 2801668
  45.8 3.5 %collective-permute-start.11 = (bf16[8,24,2432]{2,1,0:T(8,128)(2,1)S(1)}, bf16[8,24,2432]{2,1,0:T(8,128)(2,1)S(1)}, u32[]{:S(2)}, u32[]{:S(2)}) collective-permute-start(bf16[8,24,2432]{2,1,0:T(8,128)(2,1)S(1)} %collective-permute-done.6.p1), channel_id=1, source_target_pairs={{0,8},{1,9},{2,10},{3,11},{4,12},{5,13},{6,14},{7,15},{8,0},{9,1},... | collective-permute-start | bytes 2801672 | tf_op jit(solution)/shard_map/ppermute | solution.py:85
  46.0 15.4 %collective-permute-start.9 = (bf16[4,24,4864]{2,1,0:T(8,128)(2,1)S(1)}, bf16[4,24,4864]{2,1,0:T(8,128)(2,1)S(1)}, u32[]{:S(2)}, u32[]{:S(2)}) collective-permute-start(bf16[4,24,4864]{2,1,0:T(8,128)(2,1)S(1)} %pad_maximum_fusion.1), channel_id=1, source_target_pairs={{0,16},{1,17},{2,18},{3,19},{4,20},{5,21},{6,22},{7,23},{8,9},{9,8... | collective-permute-start | bytes 2801672 | tf_op jit(solution)/shard_map/ppermute | solution.py:81
  48.2 13.2 %collective-permute-start.10 = (bf16[4,64,768]{2,1,0:T(8,128)(2,1)S(1)}, bf16[4,64,768]{2,1,0:T(8,128)(2,1)S(1)}, u32[]{:S(2)}, u32[]{:S(2)}) collective-permute-start(bf16[4,64,768]{2,1,0:T(8,128)(2,1)S(1)} %pad_maximum_fusion.4), channel_id=1, source_target_pairs={{0,2},{1,3},{2,0},{3,1},{4,6},{5,7},{6,4},{7,5},{8,12},{9,13},{10,... | collective-permute-start | bytes 1179656 | tf_op jit(solution)/shard_map/ppermute | solution.py:81
  49.3 1.0 copy-start.14
  62.4 23.9 %collective-permute-start.12 = (bf16[8,24,4864]{2,1,0:T(8,128)(2,1)}, bf16[8,24,4864]{2,1,0:T(8,128)(2,1)}, u32[]{:S(2)}, u32[]{:S(2)}) collective-permute-start(bf16[8,24,4864]{2,1,0:T(8,128)(2,1)} %constant_dynamic-update-slice_fusion.b0), channel_id=1, source_target_pairs={{0,1},{1,0},{2,3},{3,2},{4,5},{5,4},{6,7},{7,6},{8,24},{9,25},{10,... | collective-permute-start | bytes 5603336 | tf_op jit(solution)/shard_map/ppermute | solution.py:81
  63.9 22.4 %copy-start.7 = (bf16[8,64,768]{2,1,0:T(8,128)(2,1)}, bf16[8,64,768]{2,1,0:T(8,128)(2,1)S(1)}, u32[]{:S(2)}) copy-start(bf16[8,64,768]{2,1,0:T(8,128)(2,1)S(1)} %constant_dynamic-update-slice_fusion.4.d0) | copy-start | bytes 2359300
  63.9 20.3 %collective-permute-start.13 = (bf16[8,64,768]{2,1,0:T(8,128)(2,1)S(1)}, bf16[8,64,768]{2,1,0:T(8,128)(2,1)S(1)}, u32[]{:S(2)}, u32[]{:S(2)}) collective-permute-start(bf16[8,64,768]{2,1,0:T(8,128)(2,1)S(1)} %constant_dynamic-update-slice_fusion.4.d0), channel_id=1, source_target_pairs={{0,4},{1,5},{2,6},{3,7},{4,0},{5,1},{6,2},{7,3},{8,10},{9,11},{10,... | collective-permute-start | bytes 2359304 | tf_op jit(solution)/shard_map/ppermute | solution.py:81
  75.2 15.7 %collective-permute-start.14 = (bf16[8,24,4864]{2,1,0:T(8,128)(2,1)}, bf16[8,24,4864]{2,1,0:T(8,128)(2,1)}, u32[]{:S(2)}, u32[]{:S(2)}) collective-permute-start(bf16[8,24,4864]{2,1,0:T(8,128)(2,1)} %constant_dynamic-update-slice_fusion.b0), channel_id=1, source_target_pairs={{0,8},{1,9},{2,10},{3,11},{4,12},{5,13},{6,14},{7,15},{8,0},{9,1},... | collective-permute-start | bytes 5603336 | tf_op jit(solution)/shard_map/ppermute | solution.py:85
  84.3 8.4 %copy-start.15 = (bf16[8,64,768]{2,1,0:T(8,128)(2,1)}, bf16[8,64,768]{2,1,0:T(8,128)(2,1)S(1)}, u32[]{:S(2)}) copy-start(bf16[8,64,768]{2,1,0:T(8,128)(2,1)S(1)} %collective-permute-done.13.d1) | copy-start | bytes 2359300
  86.3 6.4 %collective-permute-start.15 = (bf16[8,24,4864]{2,1,0:T(8,128)(2,1)}, bf16[8,24,4864]{2,1,0:T(8,128)(2,1)}, u32[]{:S(2)}, u32[]{:S(2)}) collective-permute-start(bf16[8,24,4864]{2,1,0:T(8,128)(2,1)} %collective-permute-done.12.b1), channel_id=1, source_target_pairs={{0,8},{1,9},{2,10},{3,11},{4,12},{5,13},{6,14},{7,15},{8,0},{9,1},... | collective-permute-start | bytes 5603336 | tf_op jit(solution)/shard_map/ppermute | solution.py:85
  86.3 4.6 %collective-permute-start.16 = (bf16[8,64,768]{2,1,0:T(8,128)(2,1)S(1)}, bf16[8,64,768]{2,1,0:T(8,128)(2,1)S(1)}, u32[]{:S(2)}, u32[]{:S(2)}) collective-permute-start(bf16[8,64,768]{2,1,0:T(8,128)(2,1)S(1)} %constant_dynamic-update-slice_fusion.4.d0), channel_id=1, source_target_pairs={{0,8},{1,9},{2,10},{3,11},{4,12},{5,13},{6,14},{7,15},{8,0},{9,1},... | collective-permute-start | bytes 2359304 | tf_op jit(solution)/shard_map/ppermute | solution.py:85
  86.8 5.2 %collective-permute-start.17 = (bf16[8,64,768]{2,1,0:T(8,128)(2,1)S(1)}, bf16[8,64,768]{2,1,0:T(8,128)(2,1)S(1)}, u32[]{:S(2)}, u32[]{:S(2)}) collective-permute-start(bf16[8,64,768]{2,1,0:T(8,128)(2,1)S(1)} %collective-permute-done.13.d1), channel_id=1, source_target_pairs={{0,8},{1,9},{2,10},{3,11},{4,12},{5,13},{6,14},{7,15},{8,0},{9,1},... | collective-permute-start | bytes 2359304 | tf_op jit(solution)/shard_map/ppermute | solution.py:85
  90.9 1.8 %copy-start.16 = (bf16[8,64,768]{2,1,0:T(8,128)(2,1)}, bf16[8,64,768]{2,1,0:T(8,128)(2,1)S(1)}, u32[]{:S(2)}) copy-start(bf16[8,64,768]{2,1,0:T(8,128)(2,1)S(1)} %collective-permute-done.16.d2) | copy-start | bytes 2359300
  92.0 0.9 copy-start.17
  127.7 45.6 %copy-start = (f32[2,768,8]{1,2,0:T(8,128)S(1)}, f32[2,768,8]{1,2,0:T(8,128)}, u32[]{:S(2)}) copy-start(f32[2,768,8]{1,2,0:T(8,128)} %param.37) | copy-start | bytes 147460
  127.7 45.6 %copy-start.1 = (f32[2,8,768]{2,1,0:T(8,128)S(1)}, f32[2,8,768]{2,1,0:T(8,128)}, u32[]{:S(2)}) copy-start(f32[2,8,768]{2,1,0:T(8,128)} %up_ref.5) | copy-start | bytes 147460
  127.7 45.6 %copy-start.2 = (f32[2,768,8]{1,2,0:T(8,128)S(1)}, f32[2,768,8]{1,2,0:T(8,128)}, u32[]{:S(2)}) copy-start(f32[2,768,8]{1,2,0:T(8,128)} %param.39) | copy-start | bytes 147460
  127.7 45.6 %copy-start.3 = (f32[2,768,8]{1,2,0:T(8,128)S(1)}, f32[2,768,8]{1,2,0:T(8,128)}, u32[]{:S(2)}) copy-start(f32[2,768,8]{1,2,0:T(8,128)} %param.40) | copy-start | bytes 147460
  127.7 45.6 %copy-start.4 = (f32[2,8,768]{2,1,0:T(8,128)S(1)}, f32[2,8,768]{2,1,0:T(8,128)}, u32[]{:S(2)}) copy-start(f32[2,8,768]{2,1,0:T(8,128)} %um_ref.1) | copy-start | bytes 147460
  127.8 45.6 %copy-start.5 = (f32[2,8,768]{2,1,0:T(8,128)S(1)}, f32[2,8,768]{2,1,0:T(8,128)}, u32[]{:S(2)}) copy-start(f32[2,8,768]{2,1,0:T(8,128)} %uv_ref.1) | copy-start | bytes 147460
  153.6 1.5 collective-permute-start.18
  156.0 4.3 %collective-permute-start.19 = (f32[40,384]{1,0:T(8,128)S(1)}, f32[40,384]{1,0:T(8,128)S(1)}, u32[]{:S(2)}, u32[]{:S(2)}) collective-permute-start(f32[40,384]{1,0:T(8,128)S(1)} %add.31), channel_id=1, source_target_pairs={{0,16},{1,17},{2,18},{3,19},{4,20},{5,21},{6,22},{7,23},{8,24},{9,... | collective-permute-start | bytes 184328 | tf_op jit(solution)/shard_map/ppermute | solution.py:105
  157.0 4.2 %collective-permute-start.20 = (f32[40,384]{1,0:T(8,128)S(1)}, f32[40,384]{1,0:T(8,128)S(1)}, u32[]{:S(2)}, u32[]{:S(2)}) collective-permute-start(f32[40,384]{1,0:T(8,128)S(1)} %add.31), channel_id=1, source_target_pairs={{0,1},{1,0},{2,3},{3,2},{4,5},{5,4},{6,7},{7,6},{8,9},{9,8},{10,11... | collective-permute-start | bytes 184328 | tf_op jit(solution)/shard_map/ppermute | solution.py:105
  158.3 5.1 %collective-permute-start.21 = (f32[40,384]{1,0:T(8,128)S(1)}, f32[40,384]{1,0:T(8,128)S(1)}, u32[]{:S(2)}, u32[]{:S(2)}) collective-permute-start(f32[40,384]{1,0:T(8,128)S(1)} %add.31), channel_id=1, source_target_pairs={{0,17},{1,16},{2,19},{3,18},{4,21},{5,20},{6,23},{7,22},{8,25},{9,... | collective-permute-start | bytes 184328 | tf_op jit(solution)/shard_map/ppermute | solution.py:105
  163.4 4.5 %collective-permute-start.22 = (f32[40,384]{1,0:T(8,128)S(1)}, f32[40,384]{1,0:T(8,128)S(1)}, u32[]{:S(2)}, u32[]{:S(2)}) collective-permute-start(f32[40,384]{1,0:T(8,128)S(1)} %add_add_fusion.1), channel_id=1, source_target_pairs={{0,2},{1,3},{2,0},{3,1},{4,6},{5,7},{6,4},{7,5},{8,10},{9,11},{10,... | collective-permute-start | bytes 184328 | tf_op jit(solution)/shard_map/ppermute | solution.py:105
  164.4 6.2 %collective-permute-start.23 = (f32[40,384]{1,0:T(8,128)S(1)}, f32[40,384]{1,0:T(8,128)S(1)}, u32[]{:S(2)}, u32[]{:S(2)}) collective-permute-start(f32[40,384]{1,0:T(8,128)S(1)} %add_add_fusion.1), channel_id=1, source_target_pairs={{0,4},{1,5},{2,6},{3,7},{4,0},{5,1},{6,2},{7,3},{8,12},{9,13},{10,... | collective-permute-start | bytes 184328 | tf_op jit(solution)/shard_map/ppermute | solution.py:105
  165.9 6.0 %collective-permute-start.24 = (f32[40,384]{1,0:T(8,128)S(1)}, f32[40,384]{1,0:T(8,128)S(1)}, u32[]{:S(2)}, u32[]{:S(2)}) collective-permute-start(f32[40,384]{1,0:T(8,128)S(1)} %add_add_fusion.1), channel_id=1, source_target_pairs={{0,6},{1,7},{2,4},{3,5},{4,2},{5,3},{6,0},{7,1},{8,14},{9,15},{10,... | collective-permute-start | bytes 184328 | tf_op jit(solution)/shard_map/ppermute | solution.py:105
  172.0 1.3 collective-permute-start.25
